TPU v7x, 32 devices: a whole 2x2x4 slice. The times are simulated.
32 devices in a mesh: shard: 8 (over y, x, core), seq: 4 (over z).
Axes of the slice: x: 2, y: 2, z: 4, core: 2. Of those that a mesh axis runs over, the one named last changes fastest.
Arguments:
- tokens: bfloat16 [4, 8192, 512], P(None, ('shard', 'seq')), may hold values from -7.1 to 7.1
- ln1_gain: bfloat16 [512], P('shard'), may hold values from 0.25 to 1.75
- ln1_bias: bfloat16 [512], P('shard'), may hold values from -2.5 to 2.5
- qkv_weight: bfloat16 [512, 1536], P('shard'), may hold values from -0.25 to 0.25
- out_weight: bfloat16 [512, 512], P('shard'), may hold values from -0.5 to 0.5
- out_bias: bfloat16 [512], P('shard'), may hold values from -2.5 to 2.5
- ln2_gain: bfloat16 [512], P('shard'), may hold values from 0.25 to 1.75
- ln2_bias: bfloat16 [512], P('shard'), may hold values from -2.5 to 2.5
- up_weight: bfloat16 [512, 2048], P('shard'), may hold values from -0.25 to 0.25
- up_bias: bfloat16 [2048], P('shard'), may hold values from -2.5 to 2.5
- down_weight: bfloat16 [2048, 512], P('shard'), may hold values from -0.125 to 0.125
- down_bias: bfloat16 [512], P('shard'), may hold values from -2.5 to 2.5
- cotangent: bfloat16 [4, 8192, 512], P(None, ('shard', 'seq')), may hold values from -15.4 to 15.4
Outputs:
- block_out: bfloat16 [4, 8192, 512], P(None, ('shard', 'seq'))
- grad_tokens: float32 [4, 8192, 512], P(None, ('shard', 'seq'))
- grad_ln1_gain: float32 [512], P('shard')
- grad_ln1_bias: float32 [512], P('shard')
- grad_qkv_weight: float32 [512, 1536], P('shard')
- grad_out_weight: float32 [512, 512], P('shard')
- grad_out_bias: float32 [512], P('shard')
- grad_ln2_gain: float32 [512], P('shard')
- grad_ln2_bias: float32 [512], P('shard')
- grad_up_weight: float32 [512, 2048], P('shard')
- grad_up_bias: float32 [2048], P('shard')
- grad_down_weight: float32 [2048, 512], P('shard')
- grad_down_bias: float32 [512], P('shard')
All inputs are finite; a program needn't handle non-finite values.
Results may differ from a plain program's by a relative error of at most 0.02.
Values may be sent and summed in bfloat16 or wider, within the bound.
A program may use at most 128 MiB of HBM per device.

v0:
```python
import math

import jax
import jax.numpy as jnp
from jax import lax
from jax.sharding import PartitionSpec as P

H = 8
HD = 64
SPAN = 128


epsilon = 1e-05


def layer_norm(values, norm_gain, norm_shift):
    center = values - jnp.mean(values, axis=-1, keepdims=True)
    spread = jnp.mean(center * center, axis=-1, keepdims=True)
    return center * lax.rsqrt(spread + epsilon) * norm_gain + norm_shift


def gelu_exact(values):
    return jax.nn.gelu(values, approximate=False)


def contract_rows(left_matrix, right_matrix):
    return lax.dot_general(
        left_matrix, right_matrix, (((0,), (0,)), ((), ())), preferred_element_type=jnp.float32
    )


def times_transpose(left_matrix, right_matrix):
    return lax.dot_general(
        left_matrix, right_matrix, (((1,), (1,)), ((), ())), preferred_element_type=jnp.float32
    )


def joint_scores(query_rows, key_rows, key_all, causal, earlier):
    factor = HD ** (-0.5)
    local_part = factor * jnp.einsum(
        "bjihd,bjkhd->bjhik", query_rows, key_rows, preferred_element_type=jnp.float32
    )
    summary = factor * jnp.einsum(
        "bjihd,bfhd->bjhif", query_rows, key_all, preferred_element_type=jnp.float32
    ) + math.log(SPAN)
    local_part = jnp.where(causal[None, None, None], local_part, -jnp.inf)
    summary = jnp.where(earlier[None, :, None, None, :], summary, -jnp.inf)
    return (local_part, summary)


def attend(query_rows, key_rows, value_rows, key_all, value_all, causal, earlier):
    local_part, summary = joint_scores(query_rows, key_rows, key_all, causal, earlier)
    row_max = jnp.maximum(jnp.max(local_part, axis=-1), jnp.max(summary, axis=-1))
    local_exp = jnp.exp(local_part - row_max[..., None])
    summary_exp = jnp.exp(summary - row_max[..., None])
    row_total = jnp.sum(local_exp, axis=-1) + jnp.sum(summary_exp, axis=-1)
    log_total = row_max + jnp.log(row_total)
    local_weights = (local_exp / row_total[..., None]).astype(jnp.bfloat16)
    summary_weights = (summary_exp / row_total[..., None]).astype(jnp.bfloat16)
    mixed_heads = jnp.einsum(
        "bjhik,bjkhd->bjihd", local_weights, value_rows, preferred_element_type=jnp.float32
    )
    mixed_heads = mixed_heads + jnp.einsum(
        "bjhif,bfhd->bjihd", summary_weights, value_all, preferred_element_type=jnp.float32
    )
    return (mixed_heads, log_total, local_weights, summary_weights)


def attend_back(
    grad_mixed,
    query_rows,
    key_rows,
    value_rows,
    key_all,
    value_all,
    causal,
    earlier,
    log_total,
    local_weights,
    summary_weights,
):
    factor = HD ** (-0.5)
    local_part, summary = joint_scores(query_rows, key_rows, key_all, causal, earlier)
    local_prob = jnp.exp(local_part - log_total[..., None])
    summary_prob = jnp.exp(summary - log_total[..., None])
    grad_local_w = jnp.einsum(
        "bjihd,bjkhd->bjhik", grad_mixed, value_rows, preferred_element_type=jnp.float32
    )
    grad_summary_w = jnp.einsum(
        "bjihd,bfhd->bjhif", grad_mixed, value_all, preferred_element_type=jnp.float32
    )
    row_inner = jnp.sum(local_prob * grad_local_w, axis=-1) + jnp.sum(
        summary_prob * grad_summary_w, axis=-1
    )
    grad_local = (local_prob * (grad_local_w - row_inner[..., None])).astype(jnp.bfloat16)
    grad_summary = (summary_prob * (grad_summary_w - row_inner[..., None])).astype(jnp.bfloat16)
    grad_query = jnp.einsum(
        "bjhik,bjkhd->bjihd", grad_local, key_rows, preferred_element_type=jnp.float32
    )
    grad_query = factor * (
        grad_query
        + jnp.einsum("bjhif,bfhd->bjihd", grad_summary, key_all, preferred_element_type=jnp.float32)
    )
    grad_key = factor * jnp.einsum(
        "bjhik,bjihd->bjkhd", grad_local, query_rows, preferred_element_type=jnp.float32
    )
    grad_key_all = factor * jnp.einsum(
        "bjhif,bjihd->bfhd", grad_summary, query_rows, preferred_element_type=jnp.float32
    )
    grad_value = jnp.einsum(
        "bjhik,bjihd->bjkhd", local_weights, grad_mixed, preferred_element_type=jnp.float32
    )
    grad_value_all = jnp.einsum(
        "bjhif,bjihd->bfhd", summary_weights, grad_mixed, preferred_element_type=jnp.float32
    )
    return (grad_query, grad_key, grad_value, grad_key_all, grad_value_all)


def local(
    tokens,
    ln1_gain,
    ln1_bias,
    qkv_weight,
    out_weight,
    out_bias,
    ln2_gain,
    ln2_bias,
    up_weight,
    up_bias,
    down_weight,
    down_bias,
    cotangent,
):
    seq_count = lax.axis_size("seq")
    shard_count = lax.axis_size("shard")
    shard_place = lax.axis_index("shard")
    batch_size, local_len, model_width = tokens.shape
    heads_here = H // seq_count
    head_width = heads_here * HD
    group_len = local_len * seq_count
    spans_here = group_len // SPAN
    spans_all = spans_here * shard_count
    row_count = batch_size * local_len
    shards = (
        ln1_gain,
        ln1_bias,
        qkv_weight,
        out_weight,
        out_bias,
        ln2_gain,
        ln2_bias,
        up_weight,
        up_bias,
        down_weight,
        down_bias,
    )
    gathered = (
        lax.all_gather(shards[0], "shard", axis=0, tiled=True),
        lax.all_gather(shards[1], "shard", axis=0, tiled=True),
        lax.all_gather(shards[2], "shard", axis=0, tiled=True),
        lax.all_gather(shards[3], "shard", axis=0, tiled=True),
        lax.all_gather(shards[4], "shard", axis=0, tiled=True),
        lax.all_gather(shards[5], "shard", axis=0, tiled=True),
        lax.all_gather(shards[6], "shard", axis=0, tiled=True),
        lax.all_gather(shards[7], "shard", axis=0, tiled=True),
        lax.all_gather(shards[8], "shard", axis=0, tiled=True),
        lax.all_gather(shards[9], "shard", axis=0, tiled=True),
        lax.all_gather(shards[10], "shard", axis=0, tiled=True),
    )
    (
        gain_one,
        bias_one,
        qkv_full,
        out_full,
        out_shift,
        gain_two,
        bias_two,
        up_full,
        up_shift,
        down_full,
        down_shift,
    ) = gathered
    flat_tokens = tokens.reshape(row_count, model_width).astype(jnp.float32)
    normed = layer_norm(
        flat_tokens, gain_one.astype(jnp.float32), bias_one.astype(jnp.float32)
    ).astype(jnp.bfloat16)
    packed = jnp.dot(normed, qkv_full, preferred_element_type=jnp.float32).astype(jnp.bfloat16)
    span_place = jnp.arange(SPAN)
    packed_heads = packed.reshape(batch_size, local_len, 3, seq_count, head_width)
    headed = lax.all_to_all(packed_heads, "seq", split_axis=3, concat_axis=1, tiled=True)
    headed = headed.reshape(batch_size, spans_here, SPAN, 3, heads_here, HD)
    query_rows = headed[:, :, :, 0]
    key_rows = headed[:, :, :, 1]
    value_rows = headed[:, :, :, 2]
    key_means = jnp.mean(key_rows, axis=2, dtype=jnp.float32).astype(jnp.bfloat16)
    value_means = jnp.mean(value_rows, axis=2, dtype=jnp.float32).astype(jnp.bfloat16)
    key_all, value_all = (
        lax.all_gather(key_means, "shard", axis=1, tiled=True),
        lax.all_gather(value_means, "shard", axis=1, tiled=True),
    )
    causal = span_place[:, None] >= span_place[None, :]
    global_span = shard_place * spans_here + jnp.arange(spans_here)
    earlier = global_span[:, None] > jnp.arange(spans_all)[None, :]
    mixed_heads, log_total, local_weights, summary_weights = attend(
        query_rows, key_rows, value_rows, key_all, value_all, causal, earlier
    )
    attended = mixed_heads.astype(jnp.bfloat16).reshape(batch_size, group_len, head_width)
    attended = lax.all_to_all(attended, "seq", split_axis=1, concat_axis=2, tiled=True)
    attended_rows = attended.reshape(row_count, model_width)
    middle = (
        flat_tokens
        + jnp.dot(attended_rows, out_full, preferred_element_type=jnp.float32)
        + out_shift.astype(jnp.float32)
    )
    second = layer_norm(middle, gain_two.astype(jnp.float32), bias_two.astype(jnp.float32)).astype(
        jnp.bfloat16
    )
    before = jnp.dot(second, up_full, preferred_element_type=jnp.float32) + up_shift.astype(
        jnp.float32
    )
    hidden = gelu_exact(before).astype(jnp.bfloat16)
    block_out = (
        middle
        + jnp.dot(hidden, down_full, preferred_element_type=jnp.float32)
        + down_shift.astype(jnp.float32)
    )
    block_out = block_out.astype(jnp.bfloat16).reshape(batch_size, local_len, model_width)
    incoming = cotangent.reshape(row_count, model_width)
    grad_down = contract_rows(hidden, incoming)
    grad_down_shift = jnp.sum(incoming, axis=0, dtype=jnp.float32)
    grad_hidden = times_transpose(incoming, down_full)
    gelu_value, gelu_pull = jax.vjp(gelu_exact, before)
    grad_before = gelu_pull(grad_hidden)[0].astype(jnp.bfloat16)
    grad_up = contract_rows(second, grad_before)
    grad_up_shift = jnp.sum(grad_before, axis=0, dtype=jnp.float32)
    grad_second = times_transpose(grad_before, up_full)
    norm_value, norm_pull = jax.vjp(
        layer_norm, middle, gain_two.astype(jnp.float32), bias_two.astype(jnp.float32)
    )
    grad_middle_norm, grad_gain_two, grad_bias_two = norm_pull(grad_second)
    grad_middle = incoming.astype(jnp.float32) + grad_middle_norm
    grad_branch = grad_middle.astype(jnp.bfloat16)
    grad_out = contract_rows(attended_rows, grad_branch)
    grad_out_shift = jnp.sum(grad_branch, axis=0, dtype=jnp.float32)
    grad_attended = times_transpose(grad_branch, out_full).astype(jnp.bfloat16)
    grad_attended = grad_attended.reshape(batch_size, local_len, seq_count, head_width)
    grad_headed = lax.all_to_all(grad_attended, "seq", split_axis=2, concat_axis=1, tiled=True)
    grad_mixed = grad_headed.reshape(batch_size, spans_here, SPAN, heads_here, HD)
    grad_query, grad_key, grad_value, grad_key_all, grad_value_all = attend_back(
        grad_mixed,
        query_rows,
        key_rows,
        value_rows,
        key_all,
        value_all,
        causal,
        earlier,
        log_total,
        local_weights,
        summary_weights,
    )
    grad_key_means, grad_value_means = (
        lax.psum_scatter(
            grad_key_all.astype(jnp.bfloat16), "shard", scatter_dimension=1, tiled=True
        ).astype(jnp.float32),
        lax.psum_scatter(
            grad_value_all.astype(jnp.bfloat16), "shard", scatter_dimension=1, tiled=True
        ).astype(jnp.float32),
    )
    grad_key = grad_key + grad_key_means[:, :, None] / SPAN
    grad_value = grad_value + grad_value_means[:, :, None] / SPAN
    grad_packed = jnp.stack([grad_query, grad_key, grad_value], axis=3).astype(jnp.bfloat16)
    grad_packed = grad_packed.reshape(batch_size, group_len, 3, 1, head_width)
    grad_packed = lax.all_to_all(grad_packed, "seq", split_axis=1, concat_axis=3, tiled=True)
    grad_packed = grad_packed.reshape(row_count, 3 * model_width)
    grad_qkv = contract_rows(normed, grad_packed)
    grad_normed = times_transpose(grad_packed, qkv_full)
    first_value, first_pull = jax.vjp(
        layer_norm, flat_tokens, gain_one.astype(jnp.float32), bias_one.astype(jnp.float32)
    )
    grad_flat_norm, grad_gain_one, grad_bias_one = first_pull(grad_normed)
    grad_tokens = (grad_middle + grad_flat_norm).reshape(batch_size, local_len, model_width)
    all_grads = (
        grad_gain_one,
        grad_bias_one,
        grad_qkv,
        grad_out,
        grad_out_shift,
        grad_gain_two,
        grad_bias_two,
        grad_up,
        grad_up_shift,
        grad_down,
        grad_down_shift,
    )
    owned_grads = (
        lax.psum_scatter(
            all_grads[0].astype(jnp.bfloat16), "shard", scatter_dimension=0, tiled=True
        ).astype(jnp.float32),
        lax.psum_scatter(
            all_grads[1].astype(jnp.bfloat16), "shard", scatter_dimension=0, tiled=True
        ).astype(jnp.float32),
        lax.psum_scatter(
            all_grads[2].astype(jnp.bfloat16), "shard", scatter_dimension=0, tiled=True
        ).astype(jnp.float32),
        lax.psum_scatter(
            all_grads[3].astype(jnp.bfloat16), "shard", scatter_dimension=0, tiled=True
        ).astype(jnp.float32),
        lax.psum_scatter(
            all_grads[4].astype(jnp.bfloat16), "shard", scatter_dimension=0, tiled=True
        ).astype(jnp.float32),
        lax.psum_scatter(
            all_grads[5].astype(jnp.bfloat16), "shard", scatter_dimension=0, tiled=True
        ).astype(jnp.float32),
        lax.psum_scatter(
            all_grads[6].astype(jnp.bfloat16), "shard", scatter_dimension=0, tiled=True
        ).astype(jnp.float32),
        lax.psum_scatter(
            all_grads[7].astype(jnp.bfloat16), "shard", scatter_dimension=0, tiled=True
        ).astype(jnp.float32),
        lax.psum_scatter(
            all_grads[8].astype(jnp.bfloat16), "shard", scatter_dimension=0, tiled=True
        ).astype(jnp.float32),
        lax.psum_scatter(
            all_grads[9].astype(jnp.bfloat16), "shard", scatter_dimension=0, tiled=True
        ).astype(jnp.float32),
        lax.psum_scatter(
            all_grads[10].astype(jnp.bfloat16), "shard", scatter_dimension=0, tiled=True
        ).astype(jnp.float32),
    )
    owned_grads = (
        lax.psum(owned_grads[0].astype(jnp.bfloat16), "seq").astype(jnp.float32),
        lax.psum(owned_grads[1].astype(jnp.bfloat16), "seq").astype(jnp.float32),
        lax.psum(owned_grads[2].astype(jnp.bfloat16), "seq").astype(jnp.float32),
        lax.psum(owned_grads[3].astype(jnp.bfloat16), "seq").astype(jnp.float32),
        lax.psum(owned_grads[4].astype(jnp.bfloat16), "seq").astype(jnp.float32),
        lax.psum(owned_grads[5].astype(jnp.bfloat16), "seq").astype(jnp.float32),
        lax.psum(owned_grads[6].astype(jnp.bfloat16), "seq").astype(jnp.float32),
        lax.psum(owned_grads[7].astype(jnp.bfloat16), "seq").astype(jnp.float32),
        lax.psum(owned_grads[8].astype(jnp.bfloat16), "seq").astype(jnp.float32),
        lax.psum(owned_grads[9].astype(jnp.bfloat16), "seq").astype(jnp.float32),
        lax.psum(owned_grads[10].astype(jnp.bfloat16), "seq").astype(jnp.float32),
    )
    return (
        block_out,
        grad_tokens,
        owned_grads[0],
        owned_grads[1],
        owned_grads[2],
        owned_grads[3],
        owned_grads[4],
        owned_grads[5],
        owned_grads[6],
        owned_grads[7],
        owned_grads[8],
        owned_grads[9],
        owned_grads[10],
    )


def solution(mesh):
    return jax.shard_map(
        local,
        mesh=mesh,
        in_specs=(
            P(None, ("shard", "seq"), None),
            P("shard"),
            P("shard"),
            P("shard", None),
            P("shard", None),
            P("shard"),
            P("shard"),
            P("shard"),
            P("shard", None),
            P("shard"),
            P("shard", None),
            P("shard"),
            P(None, ("shard", "seq"), None),
        ),
        out_specs=(
            P(None, ("shard", "seq"), None),
            P(None, ("shard", "seq"), None),
            P("shard"),
            P("shard"),
            P("shard", None),
            P("shard", None),
            P("shard"),
            P("shard"),
            P("shard"),
            P("shard", None),
            P("shard"),
            P("shard", None),
            P("shard"),
        ),
        check_vma=False,
    )
```

profile of v0, /device:TPU:0, one launch (start us, length us, event | category | flops | bytes accessed | tf_op | source)
XLA Modules:
  0.0 617.8 jit_solution(7081787107406855617)
XLA Ops:
  14.2 16.0 %all-reduce.14 = (bf16[512]{0:T(512)(128)(2,1)S(1)}, bf16[512]{0:T(512)(128)(2,1)S(1)}, bf16[512]{0:T(512)(128)(2,1)S(1)}, bf16[512]{0:T(512)(128)(2,1)S(1)}, bf16[512]{0:T(512)(128)(2,1)}) all-reduce(bf16[512]{0:T(512)(128)(2,1)S(1)} %dynamic-update-slice.2, ...), channel_id=1, replica_groups=mesh['shard'=8,'seq'=4] {'shard'}, use_global_device_ids=true, to_apply=%add.2 | all-reduce | flops 2560 | bytes 10240
  43.4 6.2 %reshape.280 = bf16[4,256,3,4,128]{4,3,2,1,0:T(4,128)(2,1)} reshape(bf16[1024,1536]{1,0:T(8,128)(2,1)} %convolution_convert_fusion) | data formatting | bytes 6291456 | tf_op jit(solution)/shard_map/reshape | solution.py:189
  49.6 6.0 copy.155
  61.1 70.6 %all-to-all-done = bf16[4,256,3,4,128]{1,4,2,0,3:T(8,128)(2,1)} async-done(((bf16[4,256,3,4,128]{1,4,2,0,3:T(8,128)(2,1)}), bf16[4,256,3,4,128]{1,4,2,0,3:T(8,128)(2,1)}, u32[]{:S(2)}, u32[]{:S(2)}) %all-to-all-start) | async-done | bytes 3145760 | tf_op jit(solution)/shard_map/all_to_all | solution.py:190
  131.7 6.0 copy.156
  146.8 9.2 %all_gather.42 = bf16[4,64,2,64]{3,1,2,0:T(8,128)(2,1)S(1)} all-gather(bf16[4,8,2,64]{3,1,2,0:T(8,128)(2,1)S(1)} %fusion.61), channel_id=1, replica_groups=mesh['shard'=8,'seq'=4] {'shard'}, dimensions={1}, use_global_device_ids=true | all-gather | bytes 73728 | tf_op jit(solution)/shard_map/all_gather | solution.py:198
  160.2 8.1 %all_gather.43 = bf16[4,64,2,64]{3,1,2,0:T(8,128)(2,1)S(1)} all-gather(bf16[4,8,2,64]{3,1,2,0:T(8,128)(2,1)S(1)} %fusion.60), channel_id=1, replica_groups=mesh['shard'=8,'seq'=4] {'shard'}, dimensions={1}, use_global_device_ids=true | all-gather | bytes 73728 | tf_op jit(solution)/shard_map/all_gather | solution.py:199
  173.7 6.0 copy.206
  190.5 8.8 %all-gather = bf16[8,1,256]{2,1,0:T(2,128)(2,1)S(1)} all-gather(bf16[1,1,256]{2,1,0:T(2,128)(2,1)S(1)} %reshape.309), channel_id=1, replica_groups=mesh['shard'=8,'seq'=4] {'shard'}, dimensions={0}, use_global_device_ids=true | all-gather | bytes 4608 | tf_op jit(solution)/shard_map/all_gather | solution.py:166
  199.9 10.7 %all_gather.44 = bf16[512,512]{1,0:T(8,128)(2,1)} all-gather(bf16[64,512]{1,0:T(8,128)(2,1)S(1)} %copy-done.34), channel_id=1, replica_groups=mesh['shard'=8,'seq'=4] {'shard'}, dimensions={0}, use_global_device_ids=true | all-gather | bytes 589824 | tf_op jit(solution)/shard_map/all_gather | solution.py:161
  220.5 24.8 %multiply_convert_fusion = (bf16[1024,2048]{1,0:T(8,128)(2,1)}, f32[1024,2048]{1,0:T(8,128)}, f32[1024,2048]{1,0:T(8,128)}) fusion(f32[2048]{0:T(1024)S(1)} %bitcast.229, bf16[512,2048]{1,0:T(8,128)(2,1)} %all-gather.7.cloned.1.call-done, f32[1024,512]{1,0:T(8,128)} %copy-done.14, f32[512]{0:T(512)S(1)} %convert_element_type.220, ...), kind=kOutput, calls=%fused_computation.3 | convolution fusion | flops 2288517120 | bytes 25186304 | tf_op jit(solution)/shard_map/dot_general | solution.py:218
  245.3 11.1 %fusion.77 = (bf16[2048]{0:T(1024)(128)(2,1)}, bf16[1024,2048]{1,0:T(8,128)(2,1)S(1)}) fusion(f32[1024,2048]{1,0:T(8,128)} %get-tuple-element.51, bf16[1024,512]{1,0:T(8,128)(2,1)} %bitcast.213, bf16[2048,512]{1,0:T(8,128)(2,1)} %all-gather.9.cloned.1.call-done, f32[1024,2048]{1,0:T(8,128)} %get-tuple-element.68, f32[2048]{0:T(1024)S(1)} %bitcast.230), kind=kOutput, calls=%fused_computation.149 | convolution fusion | flops 2181036032 | bytes 24129536 | tf_op jit(solution)/shard_map/dot_general | solution.py:33
  273.7 25.7 %all-to-all-done.2 = bf16[4,256,4,128]{1,3,0,2:T(8,128)(2,1)} async-done(((bf16[4,256,4,128]{1,3,0,2:T(8,128)(2,1)}), bf16[4,256,4,128]{1,3,0,2:T(8,128)(2,1)}, u32[]{:S(2)}, u32[]{:S(2)}) %all-to-all-start.2) | async-done | bytes 1048608 | tf_op jit(solution)/shard_map/all_to_all | solution.py:247
  321.4 6.1 convolution_convert_fusion.2
  338.3 9.8 %reduce-scatter.19.cloned.1.call-done = bf16[8,512]{1,0:T(8,128)(2,1)} async-done(((bf16[64,512]{1,0:T(8,128)(2,1)}), bf16[8,512]{1,0:T(8,128)(2,1)}) %reduce-scatter.19.cloned.1.call-update) | async-done | bytes 8208
  355.7 29.3 %reduce-scatter.21.cloned.1.call-done = bf16[8,512]{1,0:T(8,128)(2,1)} async-done(((bf16[64,512]{1,0:T(8,128)(2,1)}), bf16[8,512]{1,0:T(8,128)(2,1)}) %reduce-scatter.21.cloned.1.call-update) | async-done | bytes 8208
  394.1 6.0 copy.193
  411.4 64.0 %all-to-all-done.3 = bf16[4,1024,3,1,128]{4,0,3,2,1:T(4,128)(2,1)} async-done(((bf16[4,1024,3,1,128]{4,0,3,2,1:T(4,128)(2,1)}), bf16[4,1024,3,1,128]{4,0,3,2,1:T(4,128)(2,1)}, u32[]{:S(2)}, u32[]{:S(2)}) %all-to-all-start.3) | async-done | bytes 3145760 | tf_op jit(solution)/shard_map/all_to_all | solution.py:274
  482.2 6.3 %reshape.288 = bf16[1024,1536]{1,0:T(8,128)(2,1)} reshape(bf16[4,256,3,4,1,128]{5,3,2,1,0,4:T(4,128)(2,1)} %copy.195) | data formatting | bytes 6291456 | tf_op jit(solution)/shard_map/reshape | solution.py:275
  502.2 9.9 %reduce-scatter.17.cloned.1.call-done = bf16[256,512]{1,0:T(8,128)(2,1)} async-done(((bf16[2048,512]{1,0:T(8,128)(2,1)}), bf16[256,512]{1,0:T(8,128)(2,1)}) %reduce-scatter.17.cloned.1.call-update) | async-done | bytes 262160 | tf_op jit(solution)/shard_map/reduce_scatter | solution.py:324
  512.1 42.2 %reduce-scatter.11.cloned.1.call-done = bf16[64,1536]{1,0:T(8,128)(2,1)} async-done(((bf16[512,1536]{1,0:T(8,128)(2,1)}), bf16[64,1536]{1,0:T(8,128)(2,1)}) %reduce-scatter.11.cloned.1.call-update) | async-done | bytes 196624 | tf_op jit(solution)/shard_map/reduce_scatter | solution.py:303
  557.8 23.8 %all-reduce.13 = (bf16[512]{0:T(512)(128)(2,1)S(1)}, bf16[512]{0:T(512)(128)(2,1)S(1)}, bf16[512]{0:T(512)(128)(2,1)S(1)}, bf16[512]{0:T(512)(128)(2,1)S(1)}, bf...) all-reduce(bf16[512]{0:T(512)(128)(2,1)S(1)} %dynamic-update-slice., ...), channel_id=1, replica_groups=mesh['shard'=8,'seq'=4] {'shard'}, use_global_device_ids=true, to_apply=%add.5 | all-reduce | flops 5632 | bytes 22528
  582.1 12.0 %all-reduce.15 = (bf16[64]{0:T(256)(128)(2,1)S(1)}, bf16[64]{0:T(256)(128)(2,1)S(1)}, bf16[64]{0:T(256)(128)(2,1)S(1)}, bf16[64]{0:T(256)(128)(2,1)S(1)}, bf16[6...) all-reduce(bf16[64]{0:T(256)(128)(2,1)S(1)} %dynamic-slice.7, ...), channel_id=1, replica_groups=mesh['shard'=8,'seq'=4] {'seq'}, use_global_device_ids=true, to_apply=%region_20.21 | all-reduce | flops 640 | bytes 2560 | tf_op jit(solution)/shard_map/psum | solution.py:332
  597.8 6.7 %add_convert_fusion.3 = bf16[1024,512]{1,0:T(8,128)(2,1)} fusion(f32[1024,512]{1,0:T(8,128)} %copy-done.14, bf16[1024,2048]{1,0:T(8,128)(2,1)} %get-tuple-element.50, bf16[2048,512]{1,0:T(8,128)(2,1)} %all-gather.9.cloned.1.call-done, f32[512]{0:T(512)S(1)} %convert_element_type.224), kind=kOutput, calls=%fused_computation.70 | convolution fusion | flops 2149056512 | bytes 9439232 | tf_op jit(solution)/shard_map/dot_general | solution.py:224
  (256 shorter events, 174.9 us)
Async XLA Ops:
  7.2 27.4 %copy-start.2 = (bf16[4,256,512]{2,1,0:T(8,128)(2,1)S(1)}, bf16[4,256,512]{2,1,0:T(8,128)(2,1)}, u32[]{:S(2)}) copy-start(bf16[4,256,512]{2,1,0:T(8,128)(2,1)} %param.13) | copy-start | bytes 3145732
  7.2 31.3 %all-gather.5.cloned.1.call-start = ((), (), s32[]{:S(2)}) async-start(), calls=%async_computation.10 | async-start | bytes 1769472 | tf_op jit(solution)/shard_map/all_gather | solution.py:160
  55.6 76.1 %all-to-all-start = ((bf16[4,256,3,4,128]{1,4,2,0,3:T(8,128)(2,1)}), bf16[4,256,3,4,128]{1,4,2,0,3:T(8,128)(2,1)}, u32[]{:S(2)}, u32[]{:S(2)}) async-start(bf16[4,256,3,4,128]{1,4,2,0,3:T(8,128)(2,1)} %copy.155), calls=%async_computation | async-start | bytes 6291456 | tf_op jit(solution)/shard_map/all_to_all | solution.py:190
  60.3 160.2 %all-gather.7.cloned.1.call-start = ((), (), s32[]{:S(2)}) async-start(), calls=%async_computation.11 | async-start | bytes 2359296 | tf_op jit(solution)/shard_map/all_gather | solution.py:165
  146.1 11.0 %copy-start.24 = (bf16[4,8,128,2,64]{2,1,4,3,0:T(8,128)(2,1)}, bf16[4,8,128,2,64]{2,1,4,3,0:T(8,128)(2,1)S(1)}, u32[]{:S(2)}) copy-start(bf16[4,8,128,2,64]{2,1,4,3,0:T(8,128)(2,1)S(1)} %get-tuple-element.53) | copy-start | bytes 3145732
  146.1 23.3 %copy-start.7 = (bf16[4,8,128,1,2,64]{2,1,5,4,3,0:T(8,128)(2,1)}, bf16[4,8,128,1,2,64]{2,1,5,4,3,0:T(8,128)(2,1)S(1)}, u32[]{:S(2)}) copy-start(bf16[4,8,128,1,2,64]{2,1,5,4,3,0:T(8,128)(2,1)S(1)} %get-tuple-element.52) | copy-start | bytes 3145732
  157.1 11.2 %copy-start = (f32[4,8,2,128,128]{3,4,2,1,0:T(8,128)}, f32[4,8,2,128,128]{3,4,2,1,0:T(8,128)S(1)}, u32[]{:S(2)}) copy-start(f32[4,8,2,128,128]{3,4,2,1,0:T(8,128)S(1)} %get-tuple-element.65) | copy-start | bytes 12582916
  179.6 20.3 %copy-start.34 = (bf16[64,512]{1,0:T(8,128)(2,1)S(1)}, bf16[64,512]{1,0:T(8,128)(2,1)}, u32[]{:S(2)}) copy-start(bf16[64,512]{1,0:T(8,128)(2,1)} %param.17) | copy-start | bytes 196612
  184.8 30.9 %all-to-all-start.1 = ((bf16[4,1024,128]{2,0,1:T(4,128)(2,1)}), bf16[4,1024,128]{2,0,1:T(4,128)(2,1)}, u32[]{:S(2)}, u32[]{:S(2)}) async-start(bf16[4,1024,128]{2,0,1:T(4,128)(2,1)} %reshape.328), calls=%async_computation.1 | async-start | bytes 2097152 | tf_op jit(solution)/shard_map/all_to_all | solution.py:208
  189.0 56.2 %all-gather.9.cloned.1.call-start = ((), (), s32[]{:S(2)}) async-start(), calls=%async_computation.12 | async-start | bytes 2359296 | tf_op jit(solution)/shard_map/all_gather | solution.py:167
  189.8 30.7 %copy-start.41 = (f32[512]{0:T(512)}, f32[512]{0:T(512)S(1)}, u32[]{:S(2)}) copy-start(f32[512]{0:T(512)S(1)} %convert_element_type.220) | copy-start | bytes 6148
  245.3 11.1 %copy-start.15 = (f32[1024,512]{1,0:T(8,128)S(1)}, f32[1024,512]{1,0:T(8,128)}, u32[]{:S(2)}) copy-start(f32[1024,512]{1,0:T(8,128)} %copy-done.14) | copy-start | bytes 6291460
  245.3 11.1 %copy-start.46 = (bf16[512,2048]{1,0:T(8,128)(2,1)S(1)}, bf16[512,2048]{1,0:T(8,128)(2,1)}, u32[]{:S(2)}) copy-start(bf16[512,2048]{1,0:T(8,128)(2,1)} %all-gather.7.cloned.1.call-done) | copy-start | bytes 6291460
  269.3 30.1 %all-to-all-start.2 = ((bf16[4,256,4,128]{1,3,0,2:T(8,128)(2,1)}), bf16[4,256,4,128]{1,3,0,2:T(8,128)(2,1)}, u32[]{:S(2)}, u32[]{:S(2)}) async-start(bf16[4,256,4,128]{1,3,0,2:T(8,128)(2,1)} %copy.173), calls=%async_computation.2 | async-start | bytes 2097152 | tf_op jit(solution)/shard_map/all_to_all | solution.py:247
  273.6 74.5 %reduce-scatter.19.cloned.1.call-start = ((), (), s32[]{:S(2)}) async-start(), calls=%async_computation.17 | async-start | bytes 73728
  316.6 68.4 %reduce-scatter.21.cloned.1.call-start = ((), (), s32[]{:S(2)}) async-start(), calls=%async_computation.18 | async-start | bytes 73728
  318.0 184.2 %reduce-scatter.13.cloned.1.call-start = ((), (), s32[]{:S(2)}) async-start(), calls=%async_computation.14 | async-start | bytes 589824 | tf_op jit(solution)/shard_map/reduce_scatter | solution.py:306
  321.3 180.9 %reduce-scatter.15.cloned.1.call-start = ((), (), s32[]{:S(2)}) async-start(), calls=%async_computation.15 | async-start | bytes 2359296 | tf_op jit(solution)/shard_map/reduce_scatter | solution.py:318
  351.6 34.1 %copy-start.4 = (bf16[4,8,2,128,128]{3,4,2,1,0:T(8,128)(2,1)S(1)}, bf16[4,8,2,128,128]{3,4,2,1,0:T(8,128)(2,1)}, u32[]{:S(2)}) copy-start(bf16[4,8,2,128,128]{3,4,2,1,0:T(8,128)(2,1)} %copy-done.3) | copy-start | bytes 6291460
  400.1 75.3 %all-to-all-start.3 = ((bf16[4,1024,3,1,128]{4,0,3,2,1:T(4,128)(2,1)}), bf16[4,1024,3,1,128]{4,0,3,2,1:T(4,128)(2,1)}, u32[]{:S(2)}, u32[]{:S(2)}) async-start(bf16[4,1024,3,1,128]{4,0,3,2,1:T(4,128)(2,1)} %copy.193), calls=%async_computation.3 | async-start | bytes 6291456 | tf_op jit(solution)/shard_map/all_to_all | solution.py:274
  404.9 107.2 %reduce-scatter.17.cloned.1.call-start = ((), (), s32[]{:S(2)}) async-start(), calls=%async_computation.16 | async-start | bytes 2359296 | tf_op jit(solution)/shard_map/reduce_scatter | solution.py:324
  410.9 143.3 %reduce-scatter.11.cloned.1.call-start = ((), (), s32[]{:S(2)}) async-start(), calls=%async_computation.13 | async-start | bytes 1769472 | tf_op jit(solution)/shard_map/reduce_scatter | solution.py:303
  493.4 111.1 %all-reduce.19.cloned.1.call-start = ((), (), s32[]{:S(2)}) async-start(), calls=%async_computation.19 | async-start | bytes 1572864 | tf_op jit(solution)/shard_map/psum | solution.py:334
  499.6 54.6 %copy-start.6 = (f32[1024,512]{1,0:T(8,128)S(1)}, f32[1024,512]{1,0:T(8,128)}, u32[]{:S(2)}) copy-start(f32[1024,512]{1,0:T(8,128)} %copy-done.5) | copy-start | bytes 6291460
  (39 other events, 118.9 us)
Sparse Core Ops, SparseCore 0:
  9.9 28.5 all-gather.4
  63.0 28.3 all-gather.6
  191.7 29.0 all-gather.8
  316.7 31.3 reduce-scatter.18
  351.8 33.1 reduce-scatter.20
  388.5 34.1 reduce-scatter.12
  426.3 41.2 reduce-scatter.14
  470.8 41.2 reduce-scatter.16
  515.8 38.4 reduce-scatter.10
  556.9 44.6 all-reduce.18
where the time goes:
time: 627 us; the launch traced here: 618 us
  waiting for transfers between devices  262 us (42%)
  local copies, waits for them, and re-layouts  99.5 us (16%)
  matrix products  96.5 us (15%)
  blocking collectives  88.8 us (14%)
  other arithmetic  35 us (6%)
  starting transfers between devices  18.3 us (3%)
  between operations  17.4 us (3%)
    all_to_all x1, waiting for transfers between devices, local(): lax.all_to_all(packed_heads, 'seq', split_axis=3, concat_axis=1, tiled=True)  70.6 us
    all_to_all x1, waiting for transfers between devices, local(): lax.all_to_all(grad_packed, 'seq', split_axis=1, concat_axis=3, tiled=True)  64 us
    reduce_scatter x1, waiting for transfers between devices, local(): lax.psum_scatter(all_grads[2].astype(jnp.bfloat16), 'shard', scatter_dime...  42.2 us
    unnamed x12, waiting for transfers between devices  41.2 us
    unnamed x2, blocking collectives  39.9 us
    all_to_all x1, waiting for transfers between devices, local(): lax.all_to_all(grad_attended, 'seq', split_axis=2, concat_axis=1, tiled=T...  25.7 us
    dot_general x1, matrix products, local(): jnp.dot(second, up_full, preferred_element_type=jnp.float32)  24.8 us
    unnamed x127, local copies, waits for them, and re-layouts  20.6 us
  transfers between devices with their start and end apart: 14, of which 9 were waited for; matrix products, arithmetic and copies ran while one was open for 26% of the time, Pallas kernels for 0%

commit v1 on v0

--- a/solution.py
+++ b/solution.py
@@ -1,8 +1,11 @@
+import functools
 import math
 
 import jax
 import jax.numpy as jnp
 from jax import lax
+from jax.experimental import pallas as pl
+from jax.experimental.pallas import tpu as pltpu
 from jax.sharding import PartitionSpec as P
 
 H = 8
@@ -11,6 +14,1031 @@
 
 
 epsilon = 1e-05
+MESH = pl.DeviceIdType.MESH
+BF = jnp.bfloat16
+F32 = jnp.float32
+
+
+def dot(left, right, left_dim, right_dim):
+    return lax.dot_general(
+        left, right, (((left_dim,), (right_dim,)), ((), ())), preferred_element_type=F32
+    )
+
+
+def rows_of(index, count):
+    return pl.ds(pl.multiple_of(index * count, count), count)
+
+
+def norm_stats(values):
+    center = values - jnp.mean(values, axis=-1, keepdims=True)
+    inverse = lax.rsqrt(jnp.mean(center * center, axis=-1, keepdims=True) + epsilon)
+    return center * inverse, inverse
+
+
+def norm_back(grad, xhat, inverse, gain):
+    scaled = grad * gain
+    first = jnp.mean(scaled, axis=-1, keepdims=True)
+    second = jnp.mean(scaled * xhat, axis=-1, keepdims=True)
+    return inverse * (scaled - first - xhat * second)
+
+
+QKV, OUT, UP, DOWN = range(4)
+GD, GU, GO, GQ, GK, GV = range(6)
+GATHER_STEPS = 9
+REDUCE_STEPS = 8
+
+
+def block_kernel(
+    batch,
+    shard_count,
+    seq_count,
+    tok_hbm,
+    cot_hbm,
+    vecs_ref,
+    wq_hbm,
+    wo_hbm,
+    wu_hbm,
+    wd_hbm,
+    block_out_hbm,
+    grad_tok_hbm,
+    gq_hbm,
+    go_hbm,
+    gu_hbm,
+    gd_hbm,
+    vec_out_ref,
+    tok,
+    cot,
+    wq,
+    wo,
+    wu,
+    wd,
+    vec_all,
+    xhat1,
+    inv1,
+    xb_stage,
+    xb_all,
+    vfull,
+    up_bias,
+    normed,
+    packed,
+    nbar,
+    kv_mean,
+    probs,
+    att,
+    middle,
+    inv2,
+    second,
+    xhat2,
+    hidden,
+    gbefore,
+    bout,
+    gatt,
+    gbranch,
+    gkv,
+    gn_send,
+    gn_recv,
+    gnbar,
+    vsum,
+    upsum,
+    vec_send,
+    vec_recv,
+    g_down,
+    g_up,
+    g_rest,
+    r1_down,
+    r1_up,
+    r1_rest,
+    r2_down,
+    r2_up,
+    r2_rest,
+    r3_down,
+    r3_up,
+    r3_rest,
+    r4_down,
+    r4_up,
+    r4_rest,
+    own_down,
+    own_up,
+    own_rest,
+    w_send,
+    w_recv,
+    w_local,
+    io_sem,
+    vec_s,
+    vec_r,
+    xb_s,
+    xb_r,
+    gn_s,
+    gn_r,
+    vo_s,
+    vo_r,
+    red_s,
+    red_r,
+    out_sem,
+):
+    rows, width = tok.shape
+    ff = up_bias.shape[1]
+    total = shard_count * seq_count
+    groups = rows // SPAN
+    spans_here = groups // batch
+    spans_all = spans_here * total
+    pairs = H // 2
+    lanes = 2 * HD
+    ms = lax.axis_index("shard")
+    mq = lax.axis_index("seq")
+    mt = ms * seq_count + mq
+    core = lax.rem(ms, 2)
+    yx = ms // 2
+
+    def flip(value, bit):
+        return value + bit - 2 * bit * lax.rem(value // bit, 2)
+
+    core_dev = (flip(ms, 1), mq)
+    x_dev = (flip(ms, 2), mq)
+    y_dev = (flip(ms, 4), mq)
+
+    def place(index):
+        return (index // seq_count, lax.rem(index, seq_count))
+
+    tok_in = pltpu.make_async_copy(tok_hbm, tok, io_sem.at[0])
+    cot_in = pltpu.make_async_copy(cot_hbm, cot, io_sem.at[1])
+    tok_in.start()
+    cot_in.start()
+
+    xb_all[...] = jnp.zeros_like(xb_all)
+    barrier = pltpu.get_barrier_semaphore()
+
+    def greet(step, carry):
+        pl.semaphore_signal(
+            barrier, inc=1, device_id=place(lax.rem(mt + step, total)), device_id_type=MESH
+        )
+        return carry
+
+    lax.fori_loop(1, total, greet, 0)
+
+    w_hbm = (wq_hbm, wo_hbm, wu_hbm, wd_hbm)
+    w_full = (wq, wo, wu, wd)
+
+    def gather_copies(which):
+        full = w_full[which]
+        depth = full.shape[0] // shard_count
+        half = depth // 2
+        base = which * GATHER_STEPS
+
+        def block(owner):
+            return full.at[rows_of(owner, depth)]
+
+        def part(owner, side):
+            return full.at[pl.ds(pl.multiple_of(owner * depth + side * half, half), half)]
+
+        x_own, y_own, d_own = flip(ms, 2), flip(ms, 4), flip(flip(ms, 2), 4)
+        plan = (
+            (w_hbm[which], block(ms), x_dev),
+            (w_hbm[which], block(ms), y_dev),
+            (w_hbm[which], block(ms), core_dev),
+            (block(x_own), block(x_own), core_dev),
+            (block(y_own), block(y_own), core_dev),
+            (part(x_own, 0), part(x_own, 0), y_dev),
+            (part(y_own, 1), part(y_own, 1), x_dev),
+            (part(d_own, 0), part(d_own, 0), core_dev),
+            (part(d_own, 1), part(d_own, 1), core_dev),
+        )
+        return [
+            pltpu.make_async_remote_copy(
+                src_ref=src,
+                dst_ref=dst,
+                send_sem=w_send.at[base + step],
+                recv_sem=w_recv.at[base + step],
+                device_id=dev,
+                device_id_type=MESH,
+            )
+            for step, (src, dst, dev) in enumerate(plan)
+        ]
+
+    w_copies = [gather_copies(which) for which in range(4)]
+
+    def own_copy(which):
+        depth = w_full[which].shape[0] // shard_count
+        return pltpu.make_async_copy(
+            w_hbm[which], w_full[which].at[rows_of(ms, depth)], w_local.at[which]
+        )
+
+    def gather_own(which):
+        for step in (0, 1, 2):
+            w_copies[which][step].start()
+        own_copy(which).start()
+
+    def gather_forward(which):
+        c = w_copies[which]
+        c[0].wait_recv()
+        c[5].start()
+        c[3].start()
+        c[1].wait_recv()
+        c[6].start()
+        c[4].start()
+
+    def gather_last(which):
+        c = w_copies[which]
+        c[5].wait_recv()
+        c[7].start()
+        c[6].wait_recv()
+        c[8].start()
+
+    def gather_done(which):
+        c = w_copies[which]
+        for step in (2, 3, 4, 7, 8):
+            c[step].wait_recv()
+        own_copy(which).wait()
+
+    tok_in.wait()
+
+    def first_norm(g, carry):
+        at = rows_of(g, SPAN)
+        xhat, inverse = norm_stats(tok[at, :].astype(F32))
+        xhat1[at, :] = xhat
+        inv1[at, :] = inverse
+        xb_stage[pl.ds(g, 1), :] = jnp.mean(xhat, axis=0, keepdims=True)
+        return carry
+
+    lax.fori_loop(0, groups, first_norm, 0)
+    half_width = width // 2
+    xb_all[mt] = jnp.concatenate(
+        [xb_stage[:, :half_width], xb_stage[:, half_width:]], axis=0
+    ).astype(BF)
+
+    pl.semaphore_wait(barrier, total - 1)
+
+    vec_copies = []
+    for step in range(1, shard_count):
+        target = lax.rem(ms + step, shard_count)
+        vec_copies.append(
+            pltpu.make_async_remote_copy(
+                src_ref=vecs_ref,
+                dst_ref=vec_all.at[ms],
+                send_sem=vec_s.at[step],
+                recv_sem=vec_r.at[step],
+                device_id=(target, mq),
+                device_id_type=MESH,
+            )
+        )
+    gather_own(QKV)
+    for c in vec_copies:
+        c.start()
+    vec_all[ms] = vecs_ref[...]
+
+    def xb_copy(source, target, send_at):
+        return pltpu.make_async_remote_copy(
+            src_ref=xb_all.at[source],
+            dst_ref=xb_all.at[source],
+            send_sem=xb_s.at[send_at],
+            recv_sem=xb_r.at[source],
+            device_id=place(target),
+            device_id_type=MESH,
+        )
+
+    def xb_start(target, carry):
+        xb_copy(mt, target, target).start()
+        return carry
+
+    lax.fori_loop(mt + 1, total, xb_start, 0)
+
+    gather_own(OUT)
+    gather_forward(QKV)
+    for c in vec_copies:
+        c.wait_recv()
+    low_lane = lax.broadcasted_iota(jnp.int32, (8, lanes), 1) < HD
+    for at in range(shard_count // 2):
+        even = vec_all[2 * at]
+        odd = vec_all[2 * at + 1]
+        vfull[:, at * lanes : (at + 1) * lanes] = jnp.where(
+            low_lane, even[0:8, :], pltpu.roll(odd[0:8, :], HD, axis=1)
+        )
+    up_here = ff // shard_count
+    for owner in range(shard_count):
+        piece = vec_all[owner]
+        for r in range(up_here // lanes):
+            start = owner * up_here + r * lanes
+            up_bias[0:1, start : start + lanes] = piece[8 + r : 9 + r, :]
+    gather_last(QKV)
+    gather_own(UP)
+    gather_done(QKV)
+    gain1, bias1 = vfull[0:1, :], vfull[1:2, :]
+    out_shift = vfull[2:3, :]
+    gain2, bias2 = vfull[3:4, :], vfull[4:5, :]
+    down_shift = vfull[5:6, :]
+
+    big = 512
+
+    def project(i, carry):
+        at = rows_of(i, big)
+        tile = (xhat1[at, :] * gain1 + bias1).astype(BF)
+        normed[at, :] = tile
+        for n in range(3):
+            packed[at, n * width : (n + 1) * width] = dot(
+                tile, wq[:, n * width : (n + 1) * width], 1, 0
+            ).astype(BF)
+        return carry
+
+    lax.fori_loop(0, rows // big, project, 0)
+    gather_forward(OUT)
+
+    def xb_wait(source, carry):
+        xb_copy(source, flip(mt, 1), 0).wait_recv()
+        return carry
+
+    lax.fori_loop(0, mt, xb_wait, 0)
+    mean_rows = total * groups
+    arrived = xb_all[...].astype(F32)
+    arrived = jnp.concatenate([arrived[:, 0:groups, :], arrived[:, groups:, :]], axis=2)
+    arrived = arrived.reshape(mean_rows, width)
+    new_row = lax.broadcasted_iota(jnp.int32, (mean_rows, mean_rows), 0)
+    old_row = lax.broadcasted_iota(jnp.int32, (mean_rows, mean_rows), 1)
+    wanted = (
+        lax.rem(new_row, spans_all) // spans_here * groups
+        + new_row // spans_all * spans_here
+        + lax.rem(new_row, spans_here)
+    )
+    order = (old_row == wanted).astype(BF)
+    nbar[...] = dot(order, (arrived * gain1 + bias1).astype(BF), 1, 0).astype(BF)
+    for n in range(2):
+        kv_mean[:, n * width : (n + 1) * width] = dot(
+            nbar[...], wq[:, (n + 1) * width : (n + 2) * width], 1, 0
+        ).astype(BF)
+    gather_last(OUT)
+    gather_own(DOWN)
+    gather_forward(UP)
+
+    factor = HD ** (-0.5)
+    keys = SPAN + spans_all
+
+    def head_pair(ref_rows):
+        low = lax.broadcasted_iota(jnp.int32, (SPAN, lanes), 1) < HD
+        zero = jnp.zeros_like(ref_rows)
+        return jnp.concatenate(
+            [jnp.where(low, ref_rows, zero), jnp.where(low, zero, ref_rows)], axis=0
+        )
+
+    def score_shift(g):
+        j = lax.broadcasted_iota(jnp.int32, (SPAN, SPAN), 0)
+        i = lax.broadcasted_iota(jnp.int32, (SPAN, SPAN), 1)
+        near = jnp.where(j <= i, 0.0, -jnp.inf).astype(F32)
+        f = lax.broadcasted_iota(jnp.int32, (spans_all, SPAN), 0)
+        here = mt * spans_here + lax.rem(g, spans_here)
+        far = jnp.where(f < here, math.log(SPAN), -jnp.inf).astype(F32)
+        both = jnp.concatenate([near, far], axis=0)
+        return jnp.concatenate([both, both], axis=1)
+
+    low_out = lax.broadcasted_iota(jnp.int32, (SPAN, lanes), 1) < HD
+
+    def attend(g, carry):
+        at = rows_of(g, SPAN)
+        mean_at = rows_of(g // spans_here, spans_all)
+        shift = score_shift(g)
+        for p in range(pairs):
+            lo = p * lanes
+            q = packed[at, lo : lo + lanes]
+            k = jnp.concatenate(
+                [
+                    packed[at, width + lo : width + lo + lanes],
+                    kv_mean[mean_at, lo : lo + lanes],
+                ],
+                axis=0,
+            )
+            v = jnp.concatenate(
+                [
+                    packed[at, 2 * width + lo : 2 * width + lo + lanes],
+                    kv_mean[mean_at, width + lo : width + lo + lanes],
+                ],
+                axis=0,
+            )
+            scores = dot(k, head_pair(q * factor), 1, 1) + shift
+            expo = jnp.exp(scores - jnp.max(scores, axis=0, keepdims=True))
+            weights = (expo * (1.0 / jnp.sum(expo, axis=0, keepdims=True))).astype(BF)
+            probs[g * pairs + p] = weights
+            mixed = dot(weights, v, 0, 0)
+            att[at, lo : lo + lanes] = jnp.where(
+                low_out, mixed[0:SPAN], mixed[SPAN : 2 * SPAN]
+            ).astype(BF)
+        return carry
+
+    lax.fori_loop(0, groups, attend, 0)
+    gather_done(OUT)
+    gather_last(UP)
+    gather_forward(DOWN)
+
+    def second_norm(i, carry):
+        at = rows_of(i, 256)
+        mid = tok[at, :].astype(F32) + dot(att[at, :], wo[...], 1, 0) + out_shift
+        middle[at, :] = mid
+        xhat, inverse = norm_stats(mid)
+        xhat2[at, :] = xhat
+        inv2[at, :] = inverse
+        second[at, :] = (xhat * gain2 + bias2).astype(BF)
+        return carry
+
+    lax.fori_loop(0, rows // 256, second_norm, 0)
+    gather_done(UP)
+    gather_last(DOWN)
+
+    def feed_up(i, carry):
+        at = rows_of(i // (ff // 512), big)
+        cols = rows_of(lax.rem(i, ff // 512), 512)
+        before = dot(second[at, :], wu[:, cols], 1, 0) + up_bias[0:1, cols]
+        cdf = 0.5 + 0.5 * lax.erf(before * math.sqrt(0.5))
+        density = jnp.exp(before * before * -0.5) * (1.0 / math.sqrt(2.0 * math.pi))
+        hidden[at, cols] = (before * cdf).astype(BF)
+        gbefore[at, cols] = (cdf + before * density).astype(BF)
+        return carry
+
+    lax.fori_loop(0, rows // big * (ff // 512), feed_up, 0)
+    gather_done(DOWN)
+    cot_in.wait()
+
+    def chunk(which):
+        if which == GD:
+            return (g_down, r1_down, r2_down, r3_down, r4_down, own_down)
+        if which == GU:
+            return (g_up, r1_up, r2_up, r3_up, r4_up, own_up)
+        n = which - GO
+        return tuple(
+            ref.at[n] for ref in (g_rest, r1_rest, r2_rest, r3_rest, r4_rest, own_rest)
+        )
+
+    here, x_blk, y_blk, d_blk = yx, flip(yx, 1), flip(yx, 2), flip(flip(yx, 1), 2)
+    z_dev = (ms, flip(mq, 1))
+    z_mid = (ms, seq_count - 1 - mq)
+
+    def reduce_copies(which):
+        g, r1, r2, r3, r4, own = chunk(which)
+        half = g.shape[2] // 2
+        base = which * REDUCE_STEPS
+        plan = (
+            (g.at[1 - core], r1, core_dev),
+            (g.at[core, d_blk, pl.ds(0, half)], r2.at[0], x_dev),
+            (g.at[core, d_blk, pl.ds(half, half)], r2.at[1], y_dev),
+            (g.at[core, x_blk], r3.at[0], x_dev),
+            (g.at[core, y_blk], r3.at[1], y_dev),
+            (own, r4.at[0], z_dev),
+            (own, r4.at[1], z_mid),
+            (own, r4.at[0], z_dev),
+        )
+        copies = [
+            pltpu.make_async_remote_copy(
+                src_ref=src,
+                dst_ref=dst,
+                send_sem=red_s.at[base + step],
+                recv_sem=red_r.at[base + step],
+                device_id=dev,
+                device_id_type=MESH,
+            )
+            for step, (src, dst, dev) in enumerate(plan)
+        ]
+        return copies
+
+    r_copies = [reduce_copies(which) for which in range(6)]
+    edge = jnp.logical_or(mq == 0, mq == seq_count - 1)
+    inner = jnp.logical_not(edge)
+
+    def add_rows(target, *sources):
+        count = target.shape[0]
+        step = min(count, 32)
+
+        def one(i, carry):
+            at = rows_of(i, step)
+            value = target[at, :].astype(F32)
+            for source in sources:
+                value = value + source[at, :].astype(F32)
+            target[at, :] = value.astype(BF)
+            return carry
+
+        lax.fori_loop(0, count // step, one, 0)
+
+    def reduce_a(which):
+        r_copies[which][0].start()
+
+    def reduce_b(which):
+        g, r1, r2, r3, r4, own = chunk(which)
+        c = r_copies[which]
+        c[0].wait_recv()
+        add_rows(g.at[core, d_blk], r1.at[d_blk])
+        c[1].start()
+        c[2].start()
+        for blk in (x_blk, y_blk, here):
+            add_rows(g.at[core, blk], r1.at[blk])
+
+    def reduce_c(which):
+        g, r1, r2, r3, r4, own = chunk(which)
+        half = g.shape[2] // 2
+        c = r_copies[which]
+        c[1].wait_recv()
+        add_rows(g.at[core, y_blk, pl.ds(0, half)], r2.at[0])
+        c[4].start()
+        c[2].wait_recv()
+        add_rows(g.at[core, x_blk, pl.ds(half, half)], r2.at[1])
+        c[3].start()
+
+    def reduce_d(which):
+        g, r1, r2, r3, r4, own = chunk(which)
+        c = r_copies[which]
+        c[3].wait_recv()
+        c[4].wait_recv()
+        count = own.shape[0]
+
+        def one(i, carry):
+            at = rows_of(i, 32)
+            value = (
+                g[core, here, at, :].astype(F32)
+                + r3[0, at, :].astype(F32)
+                + r3[1, at, :].astype(F32)
+            )
+            own[at, :] = value.astype(BF)
+            return carry
+
+        lax.fori_loop(0, count // 32, one, 0)
+
+        @pl.when(edge)
+        def _():
+            c[5].start()
+
+    def reduce_e(which):
+        g, r1, r2, r3, r4, own = chunk(which)
+        c = r_copies[which]
+
+        @pl.when(inner)
+        def _():
+            c[5].wait_recv()
+            add_rows(own, r4.at[0])
+            c[6].start()
+
+    g_out = (gd_hbm, gu_hbm, go_hbm)
+
+    def emit(which, source):
+        if which <= GO:
+            target = g_out[which]
+        else:
+            target = gq_hbm.at[:, pl.ds((which - GQ) * width, width)]
+        return pltpu.make_async_copy(source, target, out_sem.at[which])
+
+    def reduce_f(which):
+        g, r1, r2, r3, r4, own = chunk(which)
+        c = r_copies[which]
+
+        @pl.when(inner)
+        def _():
+            c[6].wait_recv()
+            c[6].wait_send()
+            add_rows(own, r4.at[1])
+            c[7].start()
+            emit(which, own).start()
+
+    def reduce_g(which):
+        g, r1, r2, r3, r4, own = chunk(which)
+        c = r_copies[which]
+
+        @pl.when(edge)
+        def _():
+            c[5].wait_send()
+            c[7].wait_recv()
+            emit(which, r4.at[0]).start()
+
+        @pl.when(inner)
+        def _():
+            c[7].wait_send()
+
+        for step in range(5):
+            c[step].wait_send()
+        emit(which, own).wait()
+
+    def down_grad(o, carry):
+        g_down[lax.rem(o, 2), o // 2] = dot(
+            hidden[:, rows_of(o, ff // shard_count)], cot[...], 0, 0
+        ).astype(BF)
+        return carry
+
+    lax.fori_loop(0, shard_count, down_grad, 0)
+    reduce_a(GD)
+
+    def back_down(i, carry):
+        at = rows_of(i // (ff // 512), big)
+        cols = rows_of(lax.rem(i, ff // 512), 512)
+        grad = dot(cot[at, :], wd[cols, :], 1, 1)
+        grad = (grad * gbefore[at, cols].astype(F32)).astype(BF)
+        gbefore[at, cols] = grad
+        return carry
+
+    lax.fori_loop(0, rows // big * (ff // 512), back_down, 0)
+    reduce_b(GD)
+
+    shard_rows = width // shard_count
+
+    def up_grad(n, carry):
+        cols = rows_of(n, 512)
+        piece = dot(second[...], gbefore[:, cols], 0, 0).astype(BF)
+        for owner in range(shard_count):
+            g_up[owner % 2, owner // 2, :, cols] = piece[
+                owner * shard_rows : (owner + 1) * shard_rows
+            ]
+        upsum[0:1, cols] = jnp.sum(gbefore[:, cols].astype(F32), axis=0, keepdims=True)
+        return carry
+
+    lax.fori_loop(0, ff // 512, up_grad, 0)
+    reduce_c(GD)
+    reduce_a(GU)
+
+    vsum[...] = jnp.zeros_like(vsum)
+
+    def out_block(i, carry):
+        at = rows_of(i, 256)
+        bout[at, :] = (
+            middle[at, :] + dot(hidden[at, :], wd[...], 1, 0) + down_shift
+        ).astype(BF)
+        vsum[5:6, :] += jnp.sum(cot[at, :].astype(F32), axis=0, keepdims=True)
+        return carry
+
+    lax.fori_loop(0, rows // 256, out_block, 0)
+    bout_out = pltpu.make_async_copy(bout, block_out_hbm, io_sem.at[2])
+    bout_out.start()
+    reduce_b(GU)
+    reduce_d(GD)
+
+    def back_second(i, carry):
+        at = rows_of(i, 256)
+        grad = dot(gbefore[at, :], wu[...], 1, 1)
+        xhat = xhat2[at, :]
+        vsum[3:4, :] += jnp.sum(grad * xhat, axis=0, keepdims=True)
+        vsum[4:5, :] += jnp.sum(grad, axis=0, keepdims=True)
+        grad_mid = cot[at, :].astype(F32) + norm_back(grad, xhat, inv2[at, :], gain2)
+        middle[at, :] = grad_mid
+        branch = grad_mid.astype(BF)
+        gbranch[at, :] = branch
+        vsum[2:3, :] += jnp.sum(branch.astype(F32), axis=0, keepdims=True)
+        gatt[at, :] = dot(branch, wo[...], 1, 1).astype(BF)
+        return carry
+
+    lax.fori_loop(0, rows // 256, back_second, 0)
+    reduce_c(GU)
+    reduce_e(GD)
+
+    def put_rest(which, piece):
+        for owner in range(shard_count):
+            g_rest[which - GO, owner % 2, owner // 2] = piece[
+                owner * shard_rows : (owner + 1) * shard_rows
+            ]
+
+    put_rest(GO, dot(att[...], gbranch[...], 0, 0).astype(BF))
+    reduce_a(GO)
+
+    gkv[...] = jnp.zeros_like(gkv)
+    low_keys = lax.broadcasted_iota(jnp.int32, (SPAN, lanes), 1) < HD
+
+    def attend_back(g, carry):
+        at = rows_of(g, SPAN)
+        mean_at = rows_of(g // spans_here, spans_all)
+        for p in range(pairs):
+            lo = p * lanes
+            q = head_pair(packed[at, lo : lo + lanes])
+            k = jnp.concatenate(
+                [
+                    packed[at, width + lo : width + lo + lanes],
+                    kv_mean[mean_at, lo : lo + lanes],
+                ],
+                axis=0,
+            )
+            v = jnp.concatenate(
+                [
+                    packed[at, 2 * width + lo : 2 * width + lo + lanes],
+                    kv_mean[mean_at, width + lo : width + lo + lanes],
+                ],
+                axis=0,
+            )
+            go = head_pair(gatt[at, lo : lo + lanes])
+            weights = probs[g * pairs + p]
+            gw = dot(v, go, 1, 1)
+            prob = weights.astype(F32)
+            row_inner = jnp.sum(prob * gw, axis=0, keepdims=True)
+            gs = (prob * (gw - row_inner)).astype(BF)
+            gq = dot(gs, k, 0, 0)
+            gk = dot(gs, q, 1, 0) * factor
+            gv = dot(weights, go, 1, 0)
+            packed[at, lo : lo + lanes] = (
+                jnp.where(low_keys, gq[0:SPAN], gq[SPAN : 2 * SPAN]) * factor
+            ).astype(BF)
+            packed[at, width + lo : width + lo + lanes] = gk[0:SPAN].astype(BF)
+            packed[at, 2 * width + lo : 2 * width + lo + lanes] = gv[0:SPAN].astype(BF)
+            gkv[mean_at, lo : lo + lanes] += gk[SPAN:]
+            gkv[mean_at, width + lo : width + lo + lanes] += gv[SPAN:]
+        return carry
+
+    half_groups = groups // 2
+    lax.fori_loop(0, half_groups, attend_back, 0)
+    reduce_b(GO)
+    reduce_d(GU)
+    reduce_f(GD)
+    lax.fori_loop(half_groups, groups, attend_back, 0)
+    reduce_c(GO)
+    reduce_e(GU)
+
+    gkv_low = gkv[...].astype(BF)
+    gmean = dot(gkv_low, wq[:, width : 3 * width], 1, 1).astype(BF)
+    gmean = dot(order, gmean, 0, 0).reshape(total, groups, width)
+    gn_send[...] = jnp.concatenate(
+        [gmean[:, :, :half_width], gmean[:, :, half_width:]], axis=1
+    ).astype(BF)
+
+    def gn_copy(source, target, send_at):
+        return pltpu.make_async_remote_copy(
+            src_ref=gn_send.at[target],
+            dst_ref=gn_recv.at[source],
+            send_sem=gn_s.at[send_at],
+            recv_sem=gn_r.at[source],
+            device_id=place(target),
+            device_id_type=MESH,
+        )
+
+    def gn_start(target, carry):
+        gn_copy(mt, target, target).start()
+        return carry
+
+    lax.fori_loop(0, mt, gn_start, 0)
+
+    put_rest(GQ, dot(normed[...], packed[:, 0:width], 0, 0).astype(BF))
+    reduce_a(GQ)
+    put_rest(
+        GK,
+        (
+            dot(normed[...], packed[:, width : 2 * width], 0, 0)
+            + dot(nbar[...], gkv_low[:, 0:width], 0, 0)
+        ).astype(BF),
+    )
+    reduce_a(GK)
+    reduce_b(GQ)
+    put_rest(
+        GV,
+        (
+            dot(normed[...], packed[:, 2 * width :], 0, 0)
+            + dot(nbar[...], gkv_low[:, width:], 0, 0)
+        ).astype(BF),
+    )
+    reduce_a(GV)
+    reduce_b(GK)
+    reduce_c(GQ)
+    reduce_b(GV)
+    reduce_d(GO)
+    reduce_f(GU)
+
+    def gn_wait(source, carry):
+        make = gn_copy(source, flip(mt, 1), 0)
+        make.wait_recv()
+        gnbar[...] += gn_recv[source].astype(F32)
+        return carry
+
+    gnbar[...] = gn_send[mt].astype(F32)
+    lax.fori_loop(mt + 1, total, gn_wait, 0)
+    reduce_c(GK)
+    reduce_e(GO)
+    reduce_c(GV)
+    reduce_d(GQ)
+
+    def back_first(g, carry):
+        at = rows_of(g, SPAN)
+        share = jnp.concatenate(
+            [gnbar[pl.ds(g, 1), :], gnbar[pl.ds(groups + g, 1), :]], axis=1
+        ) * (1.0 / SPAN)
+        grad = dot(packed[at, :], wq[...], 1, 1) + share
+        xhat = xhat1[at, :]
+        vsum[0:1, :] += jnp.sum(grad * xhat, axis=0, keepdims=True)
+        vsum[1:2, :] += jnp.sum(grad, axis=0, keepdims=True)
+        middle[at, :] = middle[at, :] + norm_back(grad, xhat, inv1[at, :], gain1)
+        return carry
+
+    lax.fori_loop(0, groups, back_first, 0)
+    tok_out = pltpu.make_async_copy(middle, grad_tok_hbm, io_sem.at[3])
+    tok_out.start()
+
+    for owner in range(shard_count):
+        at = owner // 2
+        piece = vsum[:, at * lanes : (at + 1) * lanes]
+        if owner % 2 == 1:
+            piece = pltpu.roll(piece, HD, axis=1)
+        vec_send[owner, 0:8, :] = piece
+        vec_send[owner, 8:16, :] = jnp.zeros((8, lanes), F32)
+        for r in range(up_here // lanes):
+            start = owner * up_here + r * lanes
+            vec_send[owner, 8 + r : 9 + r, :] = upsum[0:1, start : start + lanes]
+
+    def vo_copy(source, target, send_at):
+        return pltpu.make_async_remote_copy(
+            src_ref=vec_send.at[target // seq_count],
+            dst_ref=vec_recv.at[source],
+            send_sem=vo_s.at[send_at],
+            recv_sem=vo_r.at[source],
+            device_id=place(target),
+            device_id_type=MESH,
+        )
+
+    def vo_start(step, carry):
+        target = lax.rem(mt + step, total)
+        vo_copy(mt, target, target).start()
+        return carry
+
+    lax.fori_loop(1, total, vo_start, 0)
+    vec_recv[mt] = vec_send[ms]
+    reduce_d(GK)
+    reduce_e(GQ)
+    reduce_d(GV)
+    reduce_e(GK)
+    reduce_f(GO)
+    reduce_e(GV)
+    reduce_f(GQ)
+    reduce_f(GK)
+    reduce_f(GV)
+
+    def vo_wait(step, carry):
+        source = lax.rem(mt + step, total)
+        vo_copy(source, flip(mt, 1), 0).wait_recv()
+        return carry
+
+    lax.fori_loop(1, total, vo_wait, 0)
+    vec_out_ref[...] = jnp.sum(vec_recv[...], axis=0)
+
+    for which in (GD, GU, GO, GQ, GK, GV):
+        reduce_g(which)
+
+    def xb_sent(target, carry):
+        xb_copy(mt, target, target).wait_send()
+        return carry
+
+    lax.fori_loop(mt + 1, total, xb_sent, 0)
+
+    def gn_sent(target, carry):
+        gn_copy(mt, target, target).wait_send()
+        return carry
+
+    lax.fori_loop(0, mt, gn_sent, 0)
+
+    def vo_sent(step, carry):
+        target = lax.rem(mt + step, total)
+        vo_copy(mt, target, target).wait_send()
+        return carry
+
+    lax.fori_loop(1, total, vo_sent, 0)
+    for c in vec_copies:
+        c.wait_send()
+    for which in range(4):
+        for c in w_copies[which]:
+            c.wait_send()
+    bout_out.wait()
+    tok_out.wait()
+
+
+def local_block(
+    tokens,
+    ln1_gain,
+    ln1_bias,
+    qkv_weight,
+    out_weight,
+    out_bias,
+    ln2_gain,
+    ln2_bias,
+    up_weight,
+    up_bias,
+    down_weight,
+    down_bias,
+    cotangent,
+):
+    seq_count = lax.axis_size("seq")
+    shard_count = lax.axis_size("shard")
+    total = seq_count * shard_count
+    batch, local_len, width = tokens.shape
+    rows = batch * local_len
+    groups = rows // SPAN
+    spans_all = local_len // SPAN * total
+    keys = SPAN + spans_all
+    ff = up_weight.shape[1]
+    lanes = 2 * HD
+    shard_rows = width // shard_count
+    down_rows = ff // shard_count
+    narrow = jnp.stack([ln1_gain, ln1_bias, out_bias, ln2_gain, ln2_bias, down_bias])
+    narrow = jnp.pad(narrow, ((0, 2), (0, lanes - shard_rows)))
+    wide = jnp.pad(up_bias.reshape(-1, lanes), ((0, 8 - down_rows // lanes), (0, 0)))
+    vecs = jnp.concatenate([narrow, wide]).astype(F32)
+    vmem = pl.BlockSpec(memory_space=pltpu.VMEM)
+    hbm = pl.BlockSpec(memory_space=pl.ANY)
+    dma = pltpu.SemaphoreType.DMA
+    half_yx = shard_count // 2
+
+    def grads(count, columns, lead=()):
+        half = count // 2
+        return (
+            pltpu.VMEM(lead + (2, half_yx, count, columns), BF),
+            pltpu.VMEM(lead + (half_yx, count, columns), BF),
+            pltpu.VMEM(lead + (2, half, columns), BF),
+            pltpu.VMEM(lead + (2, count, columns), BF),
+            pltpu.VMEM(lead + (2, count, columns), BF),
+            pltpu.VMEM(lead + (count, columns), BF),
+        )
+
+    down_bufs = grads(down_rows, width)
+    up_bufs = grads(shard_rows, ff)
+    rest_bufs = grads(shard_rows, width, (4,))
+    grad_bufs = [buf for trio in zip(down_bufs, up_bufs, rest_bufs) for buf in trio]
+    scratch = [
+        pltpu.VMEM((rows, width), BF),
+        pltpu.VMEM((rows, width), BF),
+        pltpu.VMEM((width, 3 * width), BF),
+        pltpu.VMEM((width, width), BF),
+        pltpu.VMEM((width, ff), BF),
+        pltpu.VMEM((ff, width), BF),
+        pltpu.VMEM((shard_count, 16, lanes), F32),
+        pltpu.VMEM((rows, width), F32),
+        pltpu.VMEM((rows, 1), F32),
+        pltpu.VMEM((groups, width), F32),
+        pltpu.VMEM((total, 2 * groups, width // 2), BF),
+        pltpu.VMEM((8, width), F32),
+        pltpu.VMEM((8, ff), F32),
+        pltpu.VMEM((rows, width), BF),
+        pltpu.VMEM((rows, 3 * width), BF),
+        pltpu.VMEM((batch * spans_all, width), BF),
+        pltpu.VMEM((batch * spans_all, 2 * width), BF),
+        pltpu.VMEM((groups * H // 2, keys, 2 * SPAN), BF),
+        pltpu.VMEM((rows, width), BF),
+        pltpu.VMEM((rows, width), F32),
+        pltpu.VMEM((rows, 1), F32),
+        pltpu.VMEM((rows, width), BF),
+        pltpu.VMEM((rows, width), F32),
+        pltpu.VMEM((rows, ff), BF),
+        pltpu.VMEM((rows, ff), BF),
+        pltpu.VMEM((rows, width), BF),
+        pltpu.VMEM((rows, width), BF),
+        pltpu.VMEM((rows, width), BF),
+        pltpu.VMEM((batch * spans_all, 2 * width), F32),
+        pltpu.VMEM((total, 2 * groups, width // 2), BF),
+        pltpu.VMEM((total, 2 * groups, width // 2), BF),
+        pltpu.VMEM((2 * groups, width // 2), F32),
+        pltpu.VMEM((8, width), F32),
+        pltpu.VMEM((8, ff), F32),
+        pltpu.VMEM((shard_count, 16, lanes), F32),
+        pltpu.VMEM((total, 16, lanes), F32),
+        *grad_bufs,
+        dma((4 * GATHER_STEPS,)),
+        dma((4 * GATHER_STEPS,)),
+        dma((4,)),
+        dma((4,)),
+        dma((shard_count,)),
+        dma((shard_count,)),
+        dma((total,)),
+        dma((total,)),
+        dma((total,)),
+        dma((total,)),
+        dma((total,)),
+        dma((total,)),
+        dma((6 * REDUCE_STEPS,)),
+        dma((6 * REDUCE_STEPS,)),
+        dma((6,)),
+    ]
+    outs = pl.pallas_call(
+        functools.partial(block_kernel, batch, shard_count, seq_count),
+        out_shape=(
+            jax.ShapeDtypeStruct((rows, width), BF),
+            jax.ShapeDtypeStruct((rows, width), F32),
+            jax.ShapeDtypeStruct((shard_rows, 3 * width), BF),
+            jax.ShapeDtypeStruct((shard_rows, width), BF),
+            jax.ShapeDtypeStruct((shard_rows, ff), BF),
+            jax.ShapeDtypeStruct((down_rows, width), BF),
+            jax.ShapeDtypeStruct((16, lanes), F32),
+        ),
+        in_specs=[hbm, hbm, vmem, hbm, hbm, hbm, hbm],
+        out_specs=(hbm, hbm, hbm, hbm, hbm, hbm, vmem),
+        scratch_shapes=scratch,
+        compiler_params=pltpu.CompilerParams(
+            collective_id=0, has_side_effects=True, vmem_limit_bytes=63 * 2**20
+        ),
+        name="block",
+    )(
+        tokens.reshape(rows, width),
+        cotangent.reshape(rows, width),
+        vecs,
+        qkv_weight,
+        out_weight,
+        up_weight,
+        down_weight,
+    )
+    block_out, grad_tokens, g_qkv, g_out, g_up, g_down, g_vec = outs
+    return (
+        block_out.reshape(tokens.shape),
+        grad_tokens.reshape(tokens.shape),
+        g_vec[0, :shard_rows],
+        g_vec[1, :shard_rows],
+        g_qkv.astype(F32),
+        g_out.astype(F32),
+        g_vec[2, :shard_rows],
+        g_vec[3, :shard_rows],
+        g_vec[4, :shard_rows],
+        g_up.astype(F32),
+        g_vec[8 : 8 + down_rows // lanes].reshape(down_rows),
+        g_down.astype(F32),
+        g_vec[5, :shard_rows],
+    )
 
 
 def layer_norm(values, norm_gain, norm_shift):
@@ -116,7 +1144,7 @@
     return (grad_query, grad_key, grad_value, grad_key_all, grad_value_all)
 
 
-def local(
+def local_general(
     tokens,
     ln1_gain,
     ln1_bias,
@@ -358,6 +1386,13 @@
     )
 
 
+def local(tokens, *rest):
+    whole_spans = tokens.shape[1] % SPAN == 0
+    if whole_spans and lax.axis_size("shard") == 8 and lax.axis_size("seq") == 4:
+        return local_block(tokens, *rest)
+    return local_general(tokens, *rest)
+
+
 def solution(mesh):
     return jax.shard_map(
         local,

time: 627 us -> 135 us (0.22); the launches traced: 618 us -> 135 us
  waiting for transfers between devices: 262 us -> 0 us
  Pallas kernels: 0 us -> 121 us
  matrix products: 96.5 us -> 0 us
  local copies, waits for them, and re-layouts: 99.5 us -> 5.74 us
  blocking collectives: 88.8 us -> 0 us
  other arithmetic: 35 us -> 7.35 us
  starting transfers between devices: 18.3 us -> 0 us
  between operations: 17.4 us -> 0.68 us
    all_to_all x4 -> x0, waiting for transfers between devices: 165 us -> none  [the longest x1 70.6 us: local(): lax.all_to_all(packed_heads, 'seq', split_axis=3, concat_axis=1, tiled=True)]
    pallas_call x0 -> x1, Pallas kernels: none -> 121 us  [local_block(): pl.pallas_call(functools.partial(block_kernel, batch, shard_count, seq_co...]
    dot_general x24 -> x0, matrix products: 96.5 us -> none  [the longest x1 24.8 us: local(): jnp.dot(second, up_full, preferred_element_type=jnp.float32)]
    reduce_scatter x4 -> x0, waiting for transfers between devices: 52.1 us -> none  [the longest x1 42.2 us: local(): lax.psum_scatter(all_grads[2].astype(jnp.bfloat16), 'shard', scatter_dime...]
    unnamed x12 -> x0, waiting for transfers between devices: 41.2 us -> none
    reshape x9 -> x1, local copies, waits for them, and re-layouts: 42.3 us -> 1.24 us  [local_block(): g_vec[8:8 + down_rows // lanes].reshape(down_rows)]
    unnamed x2 -> x0, blocking collectives: 39.9 us -> none
    all_gather x4 -> x0, blocking collectives: 36.9 us -> none  [the longest x1 10.7 us: local(): lax.all_gather(shards[3], 'shard', axis=0, tiled=True)]
  transfers between devices with their start and end apart: 14 -> 0, of which waited for: 9 -> 0; matrix products, arithmetic and copies ran while one was open for 26% -> 0% of each run, Pallas kernels for 0% -> 0%
where the time goes in v1:
time: 135 us
  Pallas kernels  121 us (90%)
  other arithmetic  7.35 us (5%)
  local copies, waits for them, and re-layouts  5.74 us (4%)
    pallas_call x1, Pallas kernels, local_block(): pl.pallas_call(functools.partial(block_kernel, batch, shard_count, seq_co...  121 us

profile of v1, /device:TPU:0, one launch (start us, length us, event | category | flops | bytes accessed | tf_op | source)
XLA Modules:
  0.0 134.9 jit_solution(8264289727481251231)
XLA Ops:
  0.6 0.8 stack.27
  1.4 1.3 fusion.3.vecs_ref
  2.7 121.1 %block.1 = (bf16[1024,512]{1,0:T(8,128)(2,1)}, f32[1024,512]{1,0:T(8,128)}, bf16[64,1536]{1,0:T(8,128)(2,1)}, bf16[64,512]{1,0:T(8,128)(2,1)}, bf16[64,2048]{1,0...) custom-call(bf16[1024,512]{1,0:T(8,128)(2,1)} %bitcast.27, bf16[1024,512]{1,0:T(8,128)(2,1)} %bitcast.28, ...), custom_call_target="tpu_custom_call" | custom-call | tf_op jit(solution)/shard_map/block/pallas_call | solution.py:999
  123.8 0.0 copy-start.2
  123.8 0.0 copy-start.1
  123.8 1.4 %slice_bitcast_fusion.1 = (f32[64]{0:T(128)}, f32[64]{0:T(128)}, f32[64]{0:T(128)}, f32[64]{0:T(128)}, f32[64]{0:T(128)}, /*index=5*/f32[64]{0:T(128)}) fusion(f32[16,128]{1,0:T(8,128)} %get-tuple-element.22), kind=kLoop, calls=%fused_computation.7 | loop fusion | bytes 3072 | tf_op jit(solution)/shard_map/squeeze | solution.py:1040
  125.2 1.2 slice_bitcast_fusion
  126.5 0.0 copy-start
  126.5 1.9 %convert_element_type.22 = f32[64,2048]{1,0:T(8,128)} convert(bf16[64,2048]{1,0:T(8,128)(2,1)} %get-tuple-element.25) | non-fusion elementwise | flops 131072 | bytes 786432 | tf_op jit(solution)/shard_map/convert_element_type | solution.py:1037
  128.4 1.8 %convert_element_type.23 = f32[256,512]{1,0:T(8,128)} convert(bf16[256,512]{1,0:T(8,128)(2,1)} %get-tuple-element.26) | non-fusion elementwise | flops 131072 | bytes 786432 | tf_op jit(solution)/shard_map/convert_element_type | solution.py:1039
  130.2 1.7 %convert_element_type.20 = f32[64,1536]{1,0:T(8,128)} convert(bf16[64,1536]{1,0:T(8,128)(2,1)} %get-tuple-element.23) | non-fusion elementwise | flops 98304 | bytes 589824 | tf_op jit(solution)/shard_map/convert_element_type | solution.py:1032
  131.9 0.0 copy-done.2
  131.9 0.7 convert_element_type.21
  132.6 0.0 copy-done.1
  132.6 1.0 copy.28
  133.5 0.0 copy-done
  133.5 1.3 copy.29
Async XLA Ops:
  123.8 8.1 %copy-start.2 = (bf16[64,512]{1,0:T(8,128)(2,1)S(1)}, bf16[64,512]{1,0:T(8,128)(2,1)}, u32[]{:S(2)}) copy-start(bf16[64,512]{1,0:T(8,128)(2,1)} %get-tuple-element.24) | copy-start | bytes 196612
  123.8 8.8 %copy-start.1 = (bf16[1024,512]{1,0:T(8,128)(2,1)S(1)}, bf16[1024,512]{1,0:T(8,128)(2,1)}, u32[]{:S(2)}) copy-start(bf16[1024,512]{1,0:T(8,128)(2,1)} %get-tuple-element.20) | copy-start | bytes 3145732
  126.5 7.1 %copy-start = (f32[1024,512]{1,0:T(8,128)S(1)}, f32[1024,512]{1,0:T(8,128)}, u32[]{:S(2)}) copy-start(f32[1024,512]{1,0:T(8,128)} %get-tuple-element.21) | copy-start | bytes 6291460

commit v2 on v1

--- a/solution.py
+++ b/solution.py
@@ -43,8 +43,8 @@
 
 
 QKV, OUT, UP, DOWN = range(4)
-GD, GU, GO, GQ, GK, GV = range(6)
-GATHER_STEPS = 9
+GD, GU, GO, GP = range(4)
+GATHER_STEPS = 11
 REDUCE_STEPS = 8
 
 
@@ -54,7 +54,8 @@
     seq_count,
     tok_hbm,
     cot_hbm,
-    vecs_ref,
+    vec_refs,
+    up_bias_ref,
     wq_hbm,
     wo_hbm,
     wu_hbm,
@@ -72,6 +73,7 @@
     wo,
     wu,
     wd,
+    vec_own,
     vec_all,
     xhat1,
     inv1,
@@ -86,12 +88,12 @@
     probs,
     att,
     middle,
+    gmid,
     inv2,
     second,
     xhat2,
     hidden,
     gbefore,
-    bout,
     gatt,
     gbranch,
     gkv,
@@ -102,24 +104,31 @@
     upsum,
     vec_send,
     vec_recv,
+    vec_line,
     g_down,
     g_up,
-    g_rest,
+    g_out,
+    g_qkv,
     r1_down,
     r1_up,
-    r1_rest,
+    r1_out,
+    r1_qkv,
     r2_down,
     r2_up,
-    r2_rest,
+    r2_out,
+    r2_qkv,
     r3_down,
     r3_up,
-    r3_rest,
+    r3_out,
+    r3_qkv,
     r4_down,
     r4_up,
-    r4_rest,
+    r4_out,
+    r4_qkv,
     own_down,
     own_up,
-    own_rest,
+    own_out,
+    own_qkv,
     w_send,
     w_recv,
     w_local,
@@ -132,6 +141,8 @@
     gn_r,
     vo_s,
     vo_r,
+    vz_s,
+    vz_r,
     red_s,
     red_r,
     out_sem,
@@ -191,15 +202,20 @@
         def part(owner, side):
             return full.at[pl.ds(pl.multiple_of(owner * depth + side * half, half), half)]
 
+        def own_part(side):
+            return w_hbm[which].at[pl.ds(side * half, half)]
+
         x_own, y_own, d_own = flip(ms, 2), flip(ms, 4), flip(flip(ms, 2), 4)
         plan = (
-            (w_hbm[which], block(ms), x_dev),
-            (w_hbm[which], block(ms), y_dev),
+            (own_part(0), part(ms, 0), x_dev),
+            (own_part(1), part(ms, 1), y_dev),
+            (own_part(1), part(ms, 1), x_dev),
+            (own_part(0), part(ms, 0), y_dev),
             (w_hbm[which], block(ms), core_dev),
+            (part(x_own, 0), part(x_own, 0), y_dev),
+            (part(y_own, 1), part(y_own, 1), x_dev),
             (block(x_own), block(x_own), core_dev),
             (block(y_own), block(y_own), core_dev),
-            (part(x_own, 0), part(x_own, 0), y_dev),
-            (part(y_own, 1), part(y_own, 1), x_dev),
             (part(d_own, 0), part(d_own, 0), core_dev),
             (part(d_own, 1), part(d_own, 1), core_dev),
         )
@@ -224,7 +240,7 @@
         )
 
     def gather_own(which):
-        for step in (0, 1, 2):
+        for step in range(5):
             w_copies[which][step].start()
         own_copy(which).start()
 
@@ -232,21 +248,26 @@
         c = w_copies[which]
         c[0].wait_recv()
         c[5].start()
-        c[3].start()
         c[1].wait_recv()
         c[6].start()
-        c[4].start()
+
+    def gather_core(which):
+        c = w_copies[which]
+        c[2].wait_recv()
+        c[7].start()
+        c[3].wait_recv()
+        c[8].start()
 
     def gather_last(which):
         c = w_copies[which]
         c[5].wait_recv()
-        c[7].start()
+        c[9].start()
         c[6].wait_recv()
-        c[8].start()
+        c[10].start()
 
     def gather_done(which):
         c = w_copies[which]
-        for step in (2, 3, 4, 7, 8):
+        for step in (4, 7, 8, 9, 10):
             c[step].wait_recv()
         own_copy(which).wait()
 
@@ -266,6 +287,11 @@
         [xb_stage[:, :half_width], xb_stage[:, half_width:]], axis=0
     ).astype(BF)
 
+    shard_rows = width // shard_count
+    for at, ref in enumerate(vec_refs):
+        vec_own[at : at + 1, 0:shard_rows] = ref[...].astype(F32)
+    vec_own[8 : 8 + up_bias_ref.shape[0], :] = up_bias_ref[...].astype(F32)
+
     pl.semaphore_wait(barrier, total - 1)
 
     vec_copies = []
@@ -273,7 +299,7 @@
         target = lax.rem(ms + step, shard_count)
         vec_copies.append(
             pltpu.make_async_remote_copy(
-                src_ref=vecs_ref,
+                src_ref=vec_own,
                 dst_ref=vec_all.at[ms],
                 send_sem=vec_s.at[step],
                 recv_sem=vec_r.at[step],
@@ -284,7 +310,7 @@
     gather_own(QKV)
     for c in vec_copies:
         c.start()
-    vec_all[ms] = vecs_ref[...]
+    vec_all[ms] = vec_own[...]
 
     def xb_copy(source, target, send_at):
         return pltpu.make_async_remote_copy(
@@ -302,8 +328,10 @@
 
     lax.fori_loop(mt + 1, total, xb_start, 0)
 
+    gather_forward(QKV)
     gather_own(OUT)
-    gather_forward(QKV)
+    gather_own(UP)
+    gather_core(QKV)
     for c in vec_copies:
         c.wait_recv()
     low_lane = lax.broadcasted_iota(jnp.int32, (8, lanes), 1) < HD
@@ -320,7 +348,6 @@
             start = owner * up_here + r * lanes
             up_bias[0:1, start : start + lanes] = piece[8 + r : 9 + r, :]
     gather_last(QKV)
-    gather_own(UP)
     gather_done(QKV)
     gain1, bias1 = vfull[0:1, :], vfull[1:2, :]
     out_shift = vfull[2:3, :]
@@ -341,6 +368,9 @@
 
     lax.fori_loop(0, rows // big, project, 0)
     gather_forward(OUT)
+    gather_forward(UP)
+    gather_own(DOWN)
+    gather_core(OUT)
 
     def xb_wait(source, carry):
         xb_copy(source, flip(mt, 1), 0).wait_recv()
@@ -364,9 +394,6 @@
         kv_mean[:, n * width : (n + 1) * width] = dot(
             nbar[...], wq[:, (n + 1) * width : (n + 2) * width], 1, 0
         ).astype(BF)
-    gather_last(OUT)
-    gather_own(DOWN)
-    gather_forward(UP)
 
     factor = HD ** (-0.5)
     keys = SPAN + spans_all
@@ -390,41 +417,48 @@
 
     low_out = lax.broadcasted_iota(jnp.int32, (SPAN, lanes), 1) < HD
 
+    def pair_rows(at, mean_at, part, p):
+        lo = p * lanes
+        start = part * width + lo
+        mean_lo = (part - 1) * width + lo
+        return jnp.concatenate(
+            [packed[at, start : start + lanes], kv_mean[mean_at, mean_lo : mean_lo + lanes]],
+            axis=0,
+        )
+
     def attend(g, carry):
         at = rows_of(g, SPAN)
         mean_at = rows_of(g // spans_here, spans_all)
         shift = score_shift(g)
+        scores = [
+            dot(
+                pair_rows(at, mean_at, 1, p),
+                head_pair(packed[at, p * lanes : (p + 1) * lanes] * factor),
+                1,
+                1,
+            )
+            for p in range(pairs)
+        ]
+        weights = []
         for p in range(pairs):
-            lo = p * lanes
-            q = packed[at, lo : lo + lanes]
-            k = jnp.concatenate(
-                [
-                    packed[at, width + lo : width + lo + lanes],
-                    kv_mean[mean_at, lo : lo + lanes],
-                ],
-                axis=0,
-            )
-            v = jnp.concatenate(
-                [
-                    packed[at, 2 * width + lo : 2 * width + lo + lanes],
-                    kv_mean[mean_at, width + lo : width + lo + lanes],
-                ],
-                axis=0,
-            )
-            scores = dot(k, head_pair(q * factor), 1, 1) + shift
-            expo = jnp.exp(scores - jnp.max(scores, axis=0, keepdims=True))
-            weights = (expo * (1.0 / jnp.sum(expo, axis=0, keepdims=True))).astype(BF)
-            probs[g * pairs + p] = weights
-            mixed = dot(weights, v, 0, 0)
-            att[at, lo : lo + lanes] = jnp.where(
+            shifted = scores[p] + shift
+            expo = jnp.exp(shifted - jnp.max(shifted, axis=0, keepdims=True))
+            total_row = jnp.sum(expo, axis=0, keepdims=True)
+            weights.append((expo * (1.0 / total_row)).astype(BF))
+            probs[g * pairs + p] = weights[p]
+        for p in range(pairs):
+            mixed = dot(weights[p], pair_rows(at, mean_at, 2, p), 0, 0)
+            att[at, p * lanes : (p + 1) * lanes] = jnp.where(
                 low_out, mixed[0:SPAN], mixed[SPAN : 2 * SPAN]
             ).astype(BF)
         return carry
 
-    lax.fori_loop(0, groups, attend, 0)
+    lax.fori_loop(0, groups // 2, attend, 0)
+    gather_last(OUT)
+    gather_core(UP)
+    gather_last(UP)
+    lax.fori_loop(groups // 2, groups, attend, 0)
     gather_done(OUT)
-    gather_last(UP)
-    gather_forward(DOWN)
 
     def second_norm(i, carry):
         at = rows_of(i, 256)
@@ -437,8 +471,8 @@
         return carry
 
     lax.fori_loop(0, rows // 256, second_norm, 0)
+    gather_forward(DOWN)
     gather_done(UP)
-    gather_last(DOWN)
 
     def feed_up(i, carry):
         at = rows_of(i // (ff // 512), big)
@@ -450,7 +484,11 @@
         gbefore[at, cols] = (cdf + before * density).astype(BF)
         return carry
 
-    lax.fori_loop(0, rows // big * (ff // 512), feed_up, 0)
+    feed_steps = rows // big * (ff // 512)
+    lax.fori_loop(0, feed_steps // 2, feed_up, 0)
+    gather_core(DOWN)
+    gather_last(DOWN)
+    lax.fori_loop(feed_steps // 2, feed_steps, feed_up, 0)
     gather_done(DOWN)
     cot_in.wait()
 
@@ -459,10 +497,10 @@
             return (g_down, r1_down, r2_down, r3_down, r4_down, own_down)
         if which == GU:
             return (g_up, r1_up, r2_up, r3_up, r4_up, own_up)
-        n = which - GO
-        return tuple(
-            ref.at[n] for ref in (g_rest, r1_rest, r2_rest, r3_rest, r4_rest, own_rest)
-        )
+        if which == GO:
+            return (g_out, r1_out, r2_out, r3_out, r4_out, own_out)
+        n = which - GP
+        return tuple(ref.at[n] for ref in (g_qkv, r1_qkv, r2_qkv, r3_qkv, r4_qkv, own_qkv))
 
     here, x_blk, y_blk, d_blk = yx, flip(yx, 1), flip(yx, 2), flip(flip(yx, 1), 2)
     z_dev = (ms, flip(mq, 1))
@@ -495,7 +533,7 @@
         ]
         return copies
 
-    r_copies = [reduce_copies(which) for which in range(6)]
+    r_copies = [reduce_copies(which) for which in range(GP + pairs)]
     edge = jnp.logical_or(mq == 0, mq == seq_count - 1)
     inner = jnp.logical_not(edge)
 
@@ -570,13 +608,13 @@
             add_rows(own, r4.at[0])
             c[6].start()
 
-    g_out = (gd_hbm, gu_hbm, go_hbm)
+    out_hbm = (gd_hbm, gu_hbm, go_hbm)
 
     def emit(which, source):
         if which <= GO:
-            target = g_out[which]
+            target = out_hbm[which]
         else:
-            target = gq_hbm.at[:, pl.ds((which - GQ) * width, width)]
+            target = gq_hbm.at[which - GP]
         return pltpu.make_async_copy(source, target, out_sem.at[which])
 
     def reduce_f(which):
@@ -609,13 +647,15 @@
             c[step].wait_send()
         emit(which, own).wait()
 
+    down_rows = ff // shard_count
+
     def down_grad(o, carry):
-        g_down[lax.rem(o, 2), o // 2] = dot(
-            hidden[:, rows_of(o, ff // shard_count)], cot[...], 0, 0
-        ).astype(BF)
-        return carry
-
-    lax.fori_loop(0, shard_count, down_grad, 0)
+        piece = dot(hidden[:, rows_of(o, 2 * down_rows)], cot[...], 0, 0).astype(BF)
+        g_down[0, o] = piece[0:down_rows]
+        g_down[1, o] = piece[down_rows:]
+        return carry
+
+    lax.fori_loop(0, shard_count // 2, down_grad, 0)
     reduce_a(GD)
 
     def back_down(i, carry):
@@ -626,10 +666,8 @@
         gbefore[at, cols] = grad
         return carry
 
-    lax.fori_loop(0, rows // big * (ff // 512), back_down, 0)
+    lax.fori_loop(0, feed_steps, back_down, 0)
     reduce_b(GD)
-
-    shard_rows = width // shard_count
 
     def up_grad(n, carry):
         cols = rows_of(n, 512)
@@ -642,24 +680,10 @@
         return carry
 
     lax.fori_loop(0, ff // 512, up_grad, 0)
+    reduce_a(GU)
     reduce_c(GD)
-    reduce_a(GU)
 
     vsum[...] = jnp.zeros_like(vsum)
-
-    def out_block(i, carry):
-        at = rows_of(i, 256)
-        bout[at, :] = (
-            middle[at, :] + dot(hidden[at, :], wd[...], 1, 0) + down_shift
-        ).astype(BF)
-        vsum[5:6, :] += jnp.sum(cot[at, :].astype(F32), axis=0, keepdims=True)
-        return carry
-
-    lax.fori_loop(0, rows // 256, out_block, 0)
-    bout_out = pltpu.make_async_copy(bout, block_out_hbm, io_sem.at[2])
-    bout_out.start()
-    reduce_b(GU)
-    reduce_d(GD)
 
     def back_second(i, carry):
         at = rows_of(i, 256)
@@ -667,8 +691,10 @@
         xhat = xhat2[at, :]
         vsum[3:4, :] += jnp.sum(grad * xhat, axis=0, keepdims=True)
         vsum[4:5, :] += jnp.sum(grad, axis=0, keepdims=True)
-        grad_mid = cot[at, :].astype(F32) + norm_back(grad, xhat, inv2[at, :], gain2)
-        middle[at, :] = grad_mid
+        incoming = cot[at, :].astype(F32)
+        vsum[5:6, :] += jnp.sum(incoming, axis=0, keepdims=True)
+        grad_mid = incoming + norm_back(grad, xhat, inv2[at, :], gain2)
+        gmid[at, :] = grad_mid
         branch = grad_mid.astype(BF)
         gbranch[at, :] = branch
         vsum[2:3, :] += jnp.sum(branch.astype(F32), axis=0, keepdims=True)
@@ -676,70 +702,92 @@
         return carry
 
     lax.fori_loop(0, rows // 256, back_second, 0)
-    reduce_c(GU)
-    reduce_e(GD)
-
-    def put_rest(which, piece):
+    reduce_b(GU)
+    reduce_d(GD)
+
+    def put_rows(target, piece):
         for owner in range(shard_count):
-            g_rest[which - GO, owner % 2, owner // 2] = piece[
+            target[owner % 2, owner // 2] = piece[
                 owner * shard_rows : (owner + 1) * shard_rows
             ]
 
-    put_rest(GO, dot(att[...], gbranch[...], 0, 0).astype(BF))
+    put_rows(g_out, dot(att[...], gbranch[...], 0, 0).astype(BF))
     reduce_a(GO)
-
-    gkv[...] = jnp.zeros_like(gkv)
+    reduce_c(GU)
+
     low_keys = lax.broadcasted_iota(jnp.int32, (SPAN, lanes), 1) < HD
-
-    def attend_back(g, carry):
-        at = rows_of(g, SPAN)
-        mean_at = rows_of(g // spans_here, spans_all)
-        for p in range(pairs):
-            lo = p * lanes
-            q = head_pair(packed[at, lo : lo + lanes])
-            k = jnp.concatenate(
-                [
-                    packed[at, width + lo : width + lo + lanes],
-                    kv_mean[mean_at, lo : lo + lanes],
-                ],
-                axis=0,
-            )
-            v = jnp.concatenate(
-                [
-                    packed[at, 2 * width + lo : 2 * width + lo + lanes],
-                    kv_mean[mean_at, width + lo : width + lo + lanes],
-                ],
-                axis=0,
-            )
+    together = 2 * spans_here
+
+    def attend_back(p, i, carry):
+        lo = p * lanes
+        members = []
+        for u in range(together):
+            g = i * together + u
+            at = rows_of(g, SPAN)
+            mean_at = rows_of(g // spans_here, spans_all)
             go = head_pair(gatt[at, lo : lo + lanes])
             weights = probs[g * pairs + p]
-            gw = dot(v, go, 1, 1)
+            gw = dot(pair_rows(at, mean_at, 2, p), go, 1, 1)
+            gv = dot(weights, go, 1, 0)
+            members.append((at, mean_at, weights, gw, gv))
+        scores = []
+        for at, mean_at, weights, gw, gv in members:
             prob = weights.astype(F32)
             row_inner = jnp.sum(prob * gw, axis=0, keepdims=True)
-            gs = (prob * (gw - row_inner)).astype(BF)
-            gq = dot(gs, k, 0, 0)
-            gk = dot(gs, q, 1, 0) * factor
-            gv = dot(weights, go, 1, 0)
+            scores.append((prob * (gw - row_inner)).astype(BF))
+        far_k, far_v = None, None
+        for u in range(together):
+            at, mean_at, weights, gw, gv = members[u]
+            q = head_pair(packed[at, lo : lo + lanes])
+            gq = dot(scores[u], pair_rows(at, mean_at, 1, p), 0, 0)
+            gk = dot(scores[u], q, 1, 0) * factor
             packed[at, lo : lo + lanes] = (
                 jnp.where(low_keys, gq[0:SPAN], gq[SPAN : 2 * SPAN]) * factor
             ).astype(BF)
             packed[at, width + lo : width + lo + lanes] = gk[0:SPAN].astype(BF)
             packed[at, 2 * width + lo : 2 * width + lo + lanes] = gv[0:SPAN].astype(BF)
-            gkv[mean_at, lo : lo + lanes] += gk[SPAN:]
-            gkv[mean_at, width + lo : width + lo + lanes] += gv[SPAN:]
-        return carry
-
-    half_groups = groups // 2
-    lax.fori_loop(0, half_groups, attend_back, 0)
+            first = u % spans_here == 0
+            far_k = gk[SPAN:] if first else far_k + gk[SPAN:]
+            far_v = gv[SPAN:] if first else far_v + gv[SPAN:]
+            if u % spans_here == spans_here - 1:
+                gkv[mean_at, lo : lo + lanes] = far_k.astype(BF)
+                gkv[mean_at, width + lo : width + lo + lanes] = far_v.astype(BF)
+        return carry
+
+    def pair_back(p):
+        lo = p * lanes
+        lax.fori_loop(0, groups // together, functools.partial(attend_back, p), 0)
+        grads = [packed[:, n * width + lo : n * width + lo + lanes] for n in range(3)]
+        means = [gkv[:, n * width + lo : n * width + lo + lanes] for n in range(2)]
+        local_part = dot(normed[...], jnp.concatenate(grads, axis=1), 0, 0)
+        mean_part = dot(nbar[...], jnp.concatenate(means, axis=1), 0, 0)
+        piece = jnp.concatenate(
+            [local_part[:, 0:lanes], local_part[:, lanes:] + mean_part], axis=1
+        )
+        put_rows(g_qkv.at[p], piece.astype(BF))
+        reduce_a(GP + p)
+
+    pair_back(0)
     reduce_b(GO)
     reduce_d(GU)
-    reduce_f(GD)
-    lax.fori_loop(half_groups, groups, attend_back, 0)
+    reduce_e(GD)
+    pair_back(1)
+    reduce_b(GP)
     reduce_c(GO)
     reduce_e(GU)
-
-    gkv_low = gkv[...].astype(BF)
-    gmean = dot(gkv_low, wq[:, width : 3 * width], 1, 1).astype(BF)
+    reduce_f(GD)
+    pair_back(2)
+    reduce_b(GP + 1)
+    reduce_c(GP)
+    reduce_d(GO)
+    reduce_f(GU)
+    pair_back(3)
+    reduce_b(GP + 2)
+    reduce_c(GP + 1)
+    reduce_d(GP)
+    reduce_e(GO)
+
+    gmean = dot(gkv[...], wq[:, width : 3 * width], 1, 1).astype(BF)
     gmean = dot(order, gmean, 0, 0).reshape(total, groups, width)
     gn_send[...] = jnp.concatenate(
         [gmean[:, :, :half_width], gmean[:, :, half_width:]], axis=1
@@ -760,59 +808,60 @@
         return carry
 
     lax.fori_loop(0, mt, gn_start, 0)
-
-    put_rest(GQ, dot(normed[...], packed[:, 0:width], 0, 0).astype(BF))
-    reduce_a(GQ)
-    put_rest(
-        GK,
-        (
-            dot(normed[...], packed[:, width : 2 * width], 0, 0)
-            + dot(nbar[...], gkv_low[:, 0:width], 0, 0)
-        ).astype(BF),
-    )
-    reduce_a(GK)
-    reduce_b(GQ)
-    put_rest(
-        GV,
-        (
-            dot(normed[...], packed[:, 2 * width :], 0, 0)
-            + dot(nbar[...], gkv_low[:, width:], 0, 0)
-        ).astype(BF),
-    )
-    reduce_a(GV)
-    reduce_b(GK)
-    reduce_c(GQ)
-    reduce_b(GV)
-    reduce_d(GO)
-    reduce_f(GU)
+    reduce_b(GP + 3)
+    reduce_c(GP + 2)
+    reduce_d(GP + 1)
+    reduce_e(GP)
+    reduce_f(GO)
+
+    def out_block(i, carry):
+        at = rows_of(i, 256)
+        gbranch[at, :] = (
+            middle[at, :] + dot(hidden[at, :], wd[...], 1, 0) + down_shift
+        ).astype(BF)
+        return carry
+
+    lax.fori_loop(0, rows // 512, out_block, 0)
+    reduce_c(GP + 3)
+    reduce_d(GP + 2)
+    reduce_e(GP + 1)
+    reduce_f(GP)
+    lax.fori_loop(rows // 512, rows // 256, out_block, 0)
+    bout_out = pltpu.make_async_copy(gbranch, block_out_hbm, io_sem.at[2])
+    bout_out.start()
 
     def gn_wait(source, carry):
-        make = gn_copy(source, flip(mt, 1), 0)
-        make.wait_recv()
+        gn_copy(source, flip(mt, 1), 0).wait_recv()
         gnbar[...] += gn_recv[source].astype(F32)
         return carry
 
     gnbar[...] = gn_send[mt].astype(F32)
     lax.fori_loop(mt + 1, total, gn_wait, 0)
-    reduce_c(GK)
-    reduce_e(GO)
-    reduce_c(GV)
-    reduce_d(GQ)
-
-    def back_first(g, carry):
-        at = rows_of(g, SPAN)
-        share = jnp.concatenate(
-            [gnbar[pl.ds(g, 1), :], gnbar[pl.ds(groups + g, 1), :]], axis=1
-        ) * (1.0 / SPAN)
-        grad = dot(packed[at, :], wq[...], 1, 1) + share
+    reduce_d(GP + 3)
+    reduce_e(GP + 2)
+    reduce_f(GP + 1)
+
+    def back_first(i, carry):
+        at = rows_of(i, 2 * SPAN)
+        shares = []
+        for u in range(2):
+            g = 2 * i + u
+            share = jnp.concatenate(
+                [gnbar[pl.ds(g, 1), :], gnbar[pl.ds(groups + g, 1), :]], axis=1
+            ) * (1.0 / SPAN)
+            shares.append(jnp.broadcast_to(share, (SPAN, width)))
+        grad = dot(packed[at, :], wq[...], 1, 1) + jnp.concatenate(shares, axis=0)
         xhat = xhat1[at, :]
         vsum[0:1, :] += jnp.sum(grad * xhat, axis=0, keepdims=True)
         vsum[1:2, :] += jnp.sum(grad, axis=0, keepdims=True)
-        middle[at, :] = middle[at, :] + norm_back(grad, xhat, inv1[at, :], gain1)
-        return carry
-
-    lax.fori_loop(0, groups, back_first, 0)
-    tok_out = pltpu.make_async_copy(middle, grad_tok_hbm, io_sem.at[3])
+        gmid[at, :] = gmid[at, :] + norm_back(grad, xhat, inv1[at, :], gain1)
+        return carry
+
+    lax.fori_loop(0, groups // 4, back_first, 0)
+    reduce_e(GP + 3)
+    reduce_f(GP + 2)
+    lax.fori_loop(groups // 4, groups // 2, back_first, 0)
+    tok_out = pltpu.make_async_copy(gmid, grad_tok_hbm, io_sem.at[3])
     tok_out.start()
 
     for owner in range(shard_count):
@@ -825,44 +874,47 @@
         for r in range(up_here // lanes):
             start = owner * up_here + r * lanes
             vec_send[owner, 8 + r : 9 + r, :] = upsum[0:1, start : start + lanes]
-
-    def vo_copy(source, target, send_at):
-        return pltpu.make_async_remote_copy(
-            src_ref=vec_send.at[target // seq_count],
-            dst_ref=vec_recv.at[source],
-            send_sem=vo_s.at[send_at],
-            recv_sem=vo_r.at[source],
-            device_id=place(target),
-            device_id_type=MESH,
+    vo_copies = []
+    for step in range(1, shard_count):
+        target = lax.rem(ms + step, shard_count)
+        vo_copies.append(
+            pltpu.make_async_remote_copy(
+                src_ref=vec_send.at[target],
+                dst_ref=vec_recv.at[ms],
+                send_sem=vo_s.at[step],
+                recv_sem=vo_r.at[step],
+                device_id=(target, mq),
+                device_id_type=MESH,
+            )
         )
-
-    def vo_start(step, carry):
-        target = lax.rem(mt + step, total)
-        vo_copy(mt, target, target).start()
-        return carry
-
-    lax.fori_loop(1, total, vo_start, 0)
-    vec_recv[mt] = vec_send[ms]
-    reduce_d(GK)
-    reduce_e(GQ)
-    reduce_d(GV)
-    reduce_e(GK)
-    reduce_f(GO)
-    reduce_e(GV)
-    reduce_f(GQ)
-    reduce_f(GK)
-    reduce_f(GV)
-
-    def vo_wait(step, carry):
-        source = lax.rem(mt + step, total)
-        vo_copy(source, flip(mt, 1), 0).wait_recv()
-        return carry
-
-    lax.fori_loop(1, total, vo_wait, 0)
-    vec_out_ref[...] = jnp.sum(vec_recv[...], axis=0)
-
-    for which in (GD, GU, GO, GQ, GK, GV):
+    for c in vo_copies:
+        c.start()
+    vec_recv[ms] = vec_send[ms]
+    reduce_f(GP + 3)
+    for which in range(GP):
         reduce_g(which)
+    for c in vo_copies:
+        c.wait_recv()
+    vec_line[mq] = jnp.sum(vec_recv[...], axis=0)
+    vz_copies = []
+    for step in range(1, seq_count):
+        vz_copies.append(
+            pltpu.make_async_remote_copy(
+                src_ref=vec_line.at[mq],
+                dst_ref=vec_line.at[mq],
+                send_sem=vz_s.at[step],
+                recv_sem=vz_r.at[step],
+                device_id=(ms, lax.rem(mq + step, seq_count)),
+                device_id_type=MESH,
+            )
+        )
+    for c in vz_copies:
+        c.start()
+    for which in range(GP, GP + pairs):
+        reduce_g(which)
+    for c in vz_copies:
+        c.wait_recv()
+    vec_out_ref[...] = jnp.sum(vec_line[...], axis=0)
 
     def xb_sent(target, carry):
         xb_copy(mt, target, target).wait_send()
@@ -875,20 +927,46 @@
         return carry
 
     lax.fori_loop(0, mt, gn_sent, 0)
-
-    def vo_sent(step, carry):
-        target = lax.rem(mt + step, total)
-        vo_copy(mt, target, target).wait_send()
-        return carry
-
-    lax.fori_loop(1, total, vo_sent, 0)
-    for c in vec_copies:
+    for c in vec_copies + vo_copies + vz_copies:
         c.wait_send()
     for which in range(4):
         for c in w_copies[which]:
             c.wait_send()
     bout_out.wait()
     tok_out.wait()
+
+
+def finish_kernel(*refs):
+    raw, vec, outs, vec_outs = refs[0:6], refs[6], refs[7:13], refs[13:20]
+    low_refs, high_refs, in_sem, out_sem = refs[20:26], refs[26:30], refs[30], refs[31]
+    order = (2, 4, 5, 3, 1, 0)
+    loads = [pltpu.make_async_copy(raw[n], low_refs[n], in_sem.at[n]) for n in range(6)]
+    for n in order:
+        loads[n].start()
+    for n, ref in enumerate(vec_outs[0:6]):
+        ref[...] = vec[n : n + 1, 0 : ref.shape[1]]
+    vec_outs[6][...] = vec[8 : 8 + vec_outs[6].shape[0], :]
+    stores = []
+    for n in order:
+        loads[n].wait()
+        ready = low_refs[n]
+        if n == 2:
+            ready = high_refs[0]
+            pairs = low_refs[2].shape[0]
+            lanes = low_refs[2].shape[2] // 3
+            for part in range(3):
+                for p in range(pairs):
+                    start = (part * pairs + p) * lanes
+                    ready[:, start : start + lanes] = low_refs[2][
+                        p, :, part * lanes : (part + 1) * lanes
+                    ].astype(F32)
+        elif n > 2:
+            ready = high_refs[n - 2]
+            ready[...] = low_refs[n][...].astype(F32)
+        stores.append(pltpu.make_async_copy(ready, outs[n], out_sem.at[n]))
+        stores[-1].start()
+    for c in stores:
+        c.wait()
 
 
 def local_block(
@@ -918,10 +996,6 @@
     lanes = 2 * HD
     shard_rows = width // shard_count
     down_rows = ff // shard_count
-    narrow = jnp.stack([ln1_gain, ln1_bias, out_bias, ln2_gain, ln2_bias, down_bias])
-    narrow = jnp.pad(narrow, ((0, 2), (0, lanes - shard_rows)))
-    wide = jnp.pad(up_bias.reshape(-1, lanes), ((0, 8 - down_rows // lanes), (0, 0)))
-    vecs = jnp.concatenate([narrow, wide]).astype(F32)
     vmem = pl.BlockSpec(memory_space=pltpu.VMEM)
     hbm = pl.BlockSpec(memory_space=pl.ANY)
     dma = pltpu.SemaphoreType.DMA
@@ -940,8 +1014,9 @@
 
     down_bufs = grads(down_rows, width)
     up_bufs = grads(shard_rows, ff)
-    rest_bufs = grads(shard_rows, width, (4,))
-    grad_bufs = [buf for trio in zip(down_bufs, up_bufs, rest_bufs) for buf in trio]
+    out_bufs = grads(shard_rows, width)
+    qkv_bufs = grads(shard_rows, 3 * lanes, (H // 2,))
+    grad_bufs = [buf for four in zip(down_bufs, up_bufs, out_bufs, qkv_bufs) for buf in four]
     scratch = [
         pltpu.VMEM((rows, width), BF),
         pltpu.VMEM((rows, width), BF),
@@ -949,6 +1024,7 @@
         pltpu.VMEM((width, width), BF),
         pltpu.VMEM((width, ff), BF),
         pltpu.VMEM((ff, width), BF),
+        pltpu.VMEM((16, lanes), F32),
         pltpu.VMEM((shard_count, 16, lanes), F32),
         pltpu.VMEM((rows, width), F32),
         pltpu.VMEM((rows, 1), F32),
@@ -963,6 +1039,7 @@
         pltpu.VMEM((groups * H // 2, keys, 2 * SPAN), BF),
         pltpu.VMEM((rows, width), BF),
         pltpu.VMEM((rows, width), F32),
+        pltpu.VMEM((rows, width), F32),
         pltpu.VMEM((rows, 1), F32),
         pltpu.VMEM((rows, width), BF),
         pltpu.VMEM((rows, width), F32),
@@ -970,15 +1047,15 @@
         pltpu.VMEM((rows, ff), BF),
         pltpu.VMEM((rows, width), BF),
         pltpu.VMEM((rows, width), BF),
-        pltpu.VMEM((rows, width), BF),
-        pltpu.VMEM((batch * spans_all, 2 * width), F32),
+        pltpu.VMEM((batch * spans_all, 2 * width), BF),
         pltpu.VMEM((total, 2 * groups, width // 2), BF),
         pltpu.VMEM((total, 2 * groups, width // 2), BF),
         pltpu.VMEM((2 * groups, width // 2), F32),
         pltpu.VMEM((8, width), F32),
         pltpu.VMEM((8, ff), F32),
         pltpu.VMEM((shard_count, 16, lanes), F32),
-        pltpu.VMEM((total, 16, lanes), F32),
+        pltpu.VMEM((shard_count, 16, lanes), F32),
+        pltpu.VMEM((seq_count, 16, lanes), F32),
         *grad_bufs,
         dma((4 * GATHER_STEPS,)),
         dma((4 * GATHER_STEPS,)),
@@ -990,24 +1067,30 @@
         dma((total,)),
         dma((total,)),
         dma((total,)),
-        dma((total,)),
-        dma((total,)),
-        dma((6 * REDUCE_STEPS,)),
-        dma((6 * REDUCE_STEPS,)),
-        dma((6,)),
+        dma((shard_count,)),
+        dma((shard_count,)),
+        dma((seq_count,)),
+        dma((seq_count,)),
+        dma(((GP + H // 2) * REDUCE_STEPS,)),
+        dma(((GP + H // 2) * REDUCE_STEPS,)),
+        dma((GP + H // 2,)),
     ]
-    outs = pl.pallas_call(
+    vectors = [
+        v.reshape(1, shard_rows)
+        for v in (ln1_gain, ln1_bias, out_bias, ln2_gain, ln2_bias, down_bias)
+    ]
+    raw = pl.pallas_call(
         functools.partial(block_kernel, batch, shard_count, seq_count),
         out_shape=(
             jax.ShapeDtypeStruct((rows, width), BF),
             jax.ShapeDtypeStruct((rows, width), F32),
-            jax.ShapeDtypeStruct((shard_rows, 3 * width), BF),
+            jax.ShapeDtypeStruct((H // 2, shard_rows, 3 * lanes), BF),
             jax.ShapeDtypeStruct((shard_rows, width), BF),
             jax.ShapeDtypeStruct((shard_rows, ff), BF),
             jax.ShapeDtypeStruct((down_rows, width), BF),
             jax.ShapeDtypeStruct((16, lanes), F32),
         ),
-        in_specs=[hbm, hbm, vmem, hbm, hbm, hbm, hbm],
+        in_specs=[hbm, hbm, [vmem] * 6, vmem, hbm, hbm, hbm, hbm],
         out_specs=(hbm, hbm, hbm, hbm, hbm, hbm, vmem),
         scratch_shapes=scratch,
         compiler_params=pltpu.CompilerParams(
@@ -1017,27 +1100,58 @@
     )(
         tokens.reshape(rows, width),
         cotangent.reshape(rows, width),
-        vecs,
+        vectors,
+        up_bias.reshape(-1, lanes),
         qkv_weight,
         out_weight,
         up_weight,
         down_weight,
     )
-    block_out, grad_tokens, g_qkv, g_out, g_up, g_down, g_vec = outs
+    low_shapes = [
+        (H // 2, shard_rows, 3 * lanes),
+        (shard_rows, width),
+        (shard_rows, ff),
+        (down_rows, width),
+    ]
+    high_shapes = [(shard_rows, 3 * width)] + low_shapes[1:]
+    done = pl.pallas_call(
+        finish_kernel,
+        out_shape=(
+            jax.ShapeDtypeStruct((rows, width), BF),
+            jax.ShapeDtypeStruct((rows, width), F32),
+            *(jax.ShapeDtypeStruct(shape, F32) for shape in high_shapes),
+            *(jax.ShapeDtypeStruct((1, shard_rows), F32) for _ in range(6)),
+            jax.ShapeDtypeStruct((down_rows // lanes, lanes), F32),
+        ),
+        in_specs=[hbm] * 6 + [vmem],
+        out_specs=(hbm,) * 6 + (vmem,) * 7,
+        scratch_shapes=[
+            pltpu.VMEM((rows, width), BF),
+            pltpu.VMEM((rows, width), F32),
+            *(pltpu.VMEM(shape, BF) for shape in low_shapes),
+            *(pltpu.VMEM(shape, F32) for shape in high_shapes),
+            dma((6,)),
+            dma((6,)),
+        ],
+        compiler_params=pltpu.CompilerParams(vmem_limit_bytes=62 * 2**20),
+        name="finish",
+    )(*raw)
+    block_out, grad_tokens, g_qkv, g_out, g_up, g_down = done[0:6]
+    vec_grads = [v.reshape(shard_rows) for v in done[6:12]]
     return (
         block_out.reshape(tokens.shape),
         grad_tokens.reshape(tokens.shape),
-        g_vec[0, :shard_rows],
-        g_vec[1, :shard_rows],
-        g_qkv.astype(F32),
-        g_out.astype(F32),
-        g_vec[2, :shard_rows],
-        g_vec[3, :shard_rows],
-        g_vec[4, :shard_rows],
-        g_up.astype(F32),
-        g_vec[8 : 8 + down_rows // lanes].reshape(down_rows),
-        g_down.astype(F32),
-        g_vec[5, :shard_rows],
+        vec_grads[0],
+        vec_grads[1],
+        g_qkv,
+        g_out,
+        vec_grads[2],
+        vec_grads[3],
+        vec_grads[4],
+        g_up,
+        done[12].reshape(down_rows),
+        g_down,
+        vec_grads[5],
     )
 
 

time: 135 us -> 114 us (0.84)
  Pallas kernels: 121 us -> 113 us
  other arithmetic: 7.35 us -> 0 us
  local copies, waits for them, and re-layouts: 5.74 us -> 0 us
    pallas_call x1, Pallas kernels: 121 us -> 108 us  [local_block(): pl.pallas_call(functools.partial(block_kernel, batch, shard_count, seq_co...]
    convert_element_type x5 -> x0, other arithmetic: 7.35 us -> none  [the longest x1 1.93 us: local_block(): g_up.astype(F32)]
    pallas_call x0 -> x1, Pallas kernels: none -> 5.08 us  [local_block(): pl.pallas_call(finish_kernel, out_shape=(jax.ShapeDtypeStruct((rows, widt...]
    unnamed x8 -> x0, local copies, waits for them, and re-layouts: 2.3 us -> none
    squeeze x1 -> x0, local copies, waits for them, and re-layouts: 1.44 us -> none  [local_block(): g_vec[5, :shard_rows]]
where the time goes in v2:
time: 114 us
  Pallas kernels  113 us (99%)
    pallas_call x1, Pallas kernels, local_block(): pl.pallas_call(functools.partial(block_kernel, batch, shard_count, seq_co...  108 us
    pallas_call x1, Pallas kernels, local_block(): pl.pallas_call(finish_kernel, out_shape=(jax.ShapeDtypeStruct((rows, widt...  5.08 us

profile of v2, /device:TPU:0, one launch (start us, length us, event | category | flops | bytes accessed | tf_op | source)
XLA Modules:
  0.0 114.0 jit_solution(17029827996946392790)
XLA Ops:
  0.6 108.1 %block.1 = (bf16[1024,512]{1,0:T(8,128)(2,1)}, f32[1024,512]{1,0:T(8,128)}, bf16[4,64,384]{2,1,0:T(8,128)(2,1)}, bf16[64,512]{1,0:T(8,128)(2,1)}, bf16[64,2048]{...) custom-call(bf16[1024,512]{1,0:T(8,128)(2,1)} %bitcast.18, bf16[1024,512]{1,0:T(8,128)(2,1)} %bitcast.19, ...), custom_call_target="tpu_custom_call" | custom-call | tf_op jit(solution)/shard_map/block/pallas_call | solution.py:1082
  108.8 5.1 %finish.1 = (bf16[1024,512]{1,0:T(8,128)(2,1)}, f32[1024,512]{1,0:T(8,128)}, f32[64,1536]{1,0:T(8,128)}, f32[64,512]{1,0:T(8,128)}, f32[64,2048]{1,0:T(8,128)}, ...) custom-call(bf16[1024,512]{1,0:T(8,128)(2,1)} %get-tuple-element.33., ...), custom_call_target="tpu_custom_call" | custom-call | tf_op jit(solution)/shard_map/finish/pallas_call | solution.py:1117

commit v3 on v2

--- a/solution.py
+++ b/solution.py
@@ -26,6 +26,8 @@
 
 
 def rows_of(index, count):
+    if isinstance(index, int):
+        return pl.ds(index * count, count)
     return pl.ds(pl.multiple_of(index * count, count), count)
 
 
@@ -43,7 +45,8 @@
 
 
 QKV, OUT, UP, DOWN = range(4)
-GD, GU, GO, GP = range(4)
+D0, D1, U0, U1, GO, QA, Q2, Q3 = range(8)
+CHUNKS = 8
 GATHER_STEPS = 11
 REDUCE_STEPS = 8
 
@@ -62,7 +65,8 @@
     wd_hbm,
     block_out_hbm,
     grad_tok_hbm,
-    gq_hbm,
+    gt_hbm,
+    gs_hbm,
     go_hbm,
     gu_hbm,
     gd_hbm,
@@ -79,6 +83,7 @@
     inv1,
     xb_stage,
     xb_all,
+    order,
     vfull,
     up_bias,
     normed,
@@ -99,6 +104,8 @@
     gkv,
     gn_send,
     gn_recv,
+    gz_send,
+    gz_recv,
     gnbar,
     vsum,
     upsum,
@@ -108,37 +115,47 @@
     g_down,
     g_up,
     g_out,
-    g_qkv,
+    g_two,
+    g_one,
     r1_down,
     r1_up,
     r1_out,
-    r1_qkv,
+    r1_two,
+    r1_one,
     r2_down,
     r2_up,
     r2_out,
-    r2_qkv,
+    r2_two,
+    r2_one,
     r3_down,
     r3_up,
     r3_out,
-    r3_qkv,
+    r3_two,
+    r3_one,
     r4_down,
     r4_up,
     r4_out,
-    r4_qkv,
+    r4_two,
+    r4_one,
     own_down,
     own_up,
     own_out,
-    own_qkv,
+    own_two,
+    own_one,
     w_send,
     w_recv,
     w_local,
     io_sem,
     vec_s,
     vec_r,
-    xb_s,
-    xb_r,
-    gn_s,
-    gn_r,
+    xz_s,
+    xz_r,
+    xs_s,
+    xs_r,
+    gs_s,
+    gs_r,
+    gz_s,
+    gz_r,
     vo_s,
     vo_r,
     vz_s,
@@ -168,9 +185,6 @@
     x_dev = (flip(ms, 2), mq)
     y_dev = (flip(ms, 4), mq)
 
-    def place(index):
-        return (index // seq_count, lax.rem(index, seq_count))
-
     tok_in = pltpu.make_async_copy(tok_hbm, tok, io_sem.at[0])
     cot_in = pltpu.make_async_copy(cot_hbm, cot, io_sem.at[1])
     tok_in.start()
@@ -179,13 +193,11 @@
     xb_all[...] = jnp.zeros_like(xb_all)
     barrier = pltpu.get_barrier_semaphore()
 
-    def greet(step, carry):
-        pl.semaphore_signal(
-            barrier, inc=1, device_id=place(lax.rem(mt + step, total)), device_id_type=MESH
-        )
-        return carry
-
-    lax.fori_loop(1, total, greet, 0)
+    shard_peers = [(lax.rem(ms + step, shard_count), mq) for step in range(1, shard_count)]
+    seq_peers = [(ms, lax.rem(mq + step, seq_count)) for step in range(1, seq_count)]
+    peers = shard_peers + seq_peers
+    for peer in peers:
+        pl.semaphore_signal(barrier, inc=1, device_id=peer, device_id_type=MESH)
 
     w_hbm = (wq_hbm, wo_hbm, wu_hbm, wd_hbm)
     w_full = (wq, wo, wu, wd)
@@ -239,10 +251,18 @@
             w_hbm[which], w_full[which].at[rows_of(ms, depth)], w_local.at[which]
         )
 
-    def gather_own(which):
-        for step in range(5):
+    def gather_own_first(which):
+        for step in range(2):
+            w_copies[which][step].start()
+
+    def gather_own_second(which):
+        for step in range(2, 5):
             w_copies[which][step].start()
         own_copy(which).start()
+
+    def gather_own(which):
+        gather_own_first(which)
+        gather_own_second(which)
 
     def gather_forward(which):
         c = w_copies[which]
@@ -273,15 +293,20 @@
 
     tok_in.wait()
 
-    def first_norm(g, carry):
-        at = rows_of(g, SPAN)
+    big = rows // 2
+
+    def first_norm(i, carry):
+        at = rows_of(i, big)
         xhat, inverse = norm_stats(tok[at, :].astype(F32))
         xhat1[at, :] = xhat
         inv1[at, :] = inverse
-        xb_stage[pl.ds(g, 1), :] = jnp.mean(xhat, axis=0, keepdims=True)
+        for u in range(big // SPAN):
+            xb_stage[pl.ds(i * (big // SPAN) + u, 1), :] = jnp.mean(
+                xhat[u * SPAN : (u + 1) * SPAN], axis=0, keepdims=True
+            )
         return carry
 
-    lax.fori_loop(0, groups, first_norm, 0)
+    lax.fori_loop(0, rows // big, first_norm, 0)
     half_width = width // 2
     xb_all[mt] = jnp.concatenate(
         [xb_stage[:, :half_width], xb_stage[:, half_width:]], axis=0
@@ -292,46 +317,66 @@
         vec_own[at : at + 1, 0:shard_rows] = ref[...].astype(F32)
     vec_own[8 : 8 + up_bias_ref.shape[0], :] = up_bias_ref[...].astype(F32)
 
-    pl.semaphore_wait(barrier, total - 1)
-
-    vec_copies = []
-    for step in range(1, shard_count):
-        target = lax.rem(ms + step, shard_count)
-        vec_copies.append(
-            pltpu.make_async_remote_copy(
-                src_ref=vec_own,
-                dst_ref=vec_all.at[ms],
-                send_sem=vec_s.at[step],
-                recv_sem=vec_r.at[step],
-                device_id=(target, mq),
-                device_id_type=MESH,
-            )
+    pl.semaphore_wait(barrier, len(peers))
+
+    def remote(source, target, send, recv, device):
+        return pltpu.make_async_remote_copy(
+            src_ref=source,
+            dst_ref=target,
+            send_sem=send,
+            recv_sem=recv,
+            device_id=device,
+            device_id_type=MESH,
         )
+
+    vec_copies = [
+        remote(vec_own, vec_all.at[ms], vec_s.at[step], vec_r.at[step], peer)
+        for step, peer in enumerate(shard_peers)
+    ]
+    xz_copies = [
+        remote(xb_all.at[mt], xb_all.at[mt], xz_s.at[step], xz_r.at[step], peer)
+        for step, peer in enumerate(seq_peers)
+    ]
+
+    def xb_group(owner):
+        return xb_all.at[rows_of(owner, seq_count)]
+
+    def xs_copy(owner, target):
+        return remote(
+            xb_group(owner), xb_group(owner), xs_s.at[target], xs_r.at[owner], (target, mq)
+        )
+
     gather_own(QKV)
-    for c in vec_copies:
+    for c in xz_copies + vec_copies:
         c.start()
     vec_all[ms] = vec_own[...]
-
-    def xb_copy(source, target, send_at):
-        return pltpu.make_async_remote_copy(
-            src_ref=xb_all.at[source],
-            dst_ref=xb_all.at[source],
-            send_sem=xb_s.at[send_at],
-            recv_sem=xb_r.at[source],
-            device_id=place(target),
-            device_id_type=MESH,
-        )
-
-    def xb_start(target, carry):
-        xb_copy(mt, target, target).start()
-        return carry
-
-    lax.fori_loop(mt + 1, total, xb_start, 0)
+    mean_rows = total * groups
+    new_row = lax.broadcasted_iota(jnp.int32, (mean_rows, mean_rows), 0)
+    old_row = lax.broadcasted_iota(jnp.int32, (mean_rows, mean_rows), 1)
+
+    def scaled(value, down_by, up_by):
+        quotient = lax.shift_right_logical(value, down_by.bit_length() - 1)
+        return lax.shift_left(quotient, up_by.bit_length() - 1)
+
+    wanted = (
+        scaled(new_row & (spans_all - 1), spans_here, groups)
+        + scaled(new_row, spans_all, spans_here)
+        + (new_row & (spans_here - 1))
+    )
+    order[...] = (old_row == wanted).astype(BF)
+    for c in xz_copies:
+        c.wait_recv()
+    for target in range(1, shard_count):
+
+        @pl.when(target > ms)
+        def _(target=target):
+            xs_copy(ms, target).start()
 
     gather_forward(QKV)
     gather_own(OUT)
     gather_own(UP)
     gather_core(QKV)
+    gather_own_first(DOWN)
     for c in vec_copies:
         c.wait_recv()
     low_lane = lax.broadcasted_iota(jnp.int32, (8, lanes), 1) < HD
@@ -342,10 +387,12 @@
             low_lane, even[0:8, :], pltpu.roll(odd[0:8, :], HD, axis=1)
         )
     up_here = ff // shard_count
+    parts = up_here // lanes
+    part_cols = shard_count * lanes
     for owner in range(shard_count):
         piece = vec_all[owner]
         for r in range(up_here // lanes):
-            start = owner * up_here + r * lanes
+            start = r * part_cols + owner * lanes
             up_bias[0:1, start : start + lanes] = piece[8 + r : 9 + r, :]
     gather_last(QKV)
     gather_done(QKV)
@@ -354,42 +401,32 @@
     gain2, bias2 = vfull[3:4, :], vfull[4:5, :]
     down_shift = vfull[5:6, :]
 
-    big = 512
-
-    def project(i, carry):
-        at = rows_of(i, big)
-        tile = (xhat1[at, :] * gain1 + bias1).astype(BF)
-        normed[at, :] = tile
-        for n in range(3):
-            packed[at, n * width : (n + 1) * width] = dot(
-                tile, wq[:, n * width : (n + 1) * width], 1, 0
-            ).astype(BF)
-        return carry
-
-    lax.fori_loop(0, rows // big, project, 0)
+    tile = (xhat1[...] * gain1 + bias1).astype(BF)
+    normed[...] = tile
+
+    def project(n):
+        packed[:, n * width : (n + 1) * width] = dot(
+            tile, wq[:, n * width : (n + 1) * width], 1, 0
+        ).astype(BF)
+
+    project(0)
     gather_forward(OUT)
+    project(1)
     gather_forward(UP)
-    gather_own(DOWN)
+    project(2)
     gather_core(OUT)
-
-    def xb_wait(source, carry):
-        xb_copy(source, flip(mt, 1), 0).wait_recv()
-        return carry
-
-    lax.fori_loop(0, mt, xb_wait, 0)
-    mean_rows = total * groups
+    gather_own_second(DOWN)
+
+    for owner in range(shard_count - 1):
+
+        @pl.when(owner < ms)
+        def _(owner=owner):
+            xs_copy(owner, owner).wait_recv()
+
     arrived = xb_all[...].astype(F32)
     arrived = jnp.concatenate([arrived[:, 0:groups, :], arrived[:, groups:, :]], axis=2)
     arrived = arrived.reshape(mean_rows, width)
-    new_row = lax.broadcasted_iota(jnp.int32, (mean_rows, mean_rows), 0)
-    old_row = lax.broadcasted_iota(jnp.int32, (mean_rows, mean_rows), 1)
-    wanted = (
-        lax.rem(new_row, spans_all) // spans_here * groups
-        + new_row // spans_all * spans_here
-        + lax.rem(new_row, spans_here)
-    )
-    order = (old_row == wanted).astype(BF)
-    nbar[...] = dot(order, (arrived * gain1 + bias1).astype(BF), 1, 0).astype(BF)
+    nbar[...] = dot(order[...], (arrived * gain1 + bias1).astype(BF), 1, 0).astype(BF)
     for n in range(2):
         kv_mean[:, n * width : (n + 1) * width] = dot(
             nbar[...], wq[:, (n + 1) * width : (n + 2) * width], 1, 0
@@ -410,7 +447,7 @@
         i = lax.broadcasted_iota(jnp.int32, (SPAN, SPAN), 1)
         near = jnp.where(j <= i, 0.0, -jnp.inf).astype(F32)
         f = lax.broadcasted_iota(jnp.int32, (spans_all, SPAN), 0)
-        here = mt * spans_here + lax.rem(g, spans_here)
+        here = mt * spans_here + g % spans_here
         far = jnp.where(f < here, math.log(SPAN), -jnp.inf).astype(F32)
         both = jnp.concatenate([near, far], axis=0)
         return jnp.concatenate([both, both], axis=1)
@@ -426,81 +463,114 @@
             axis=0,
         )
 
-    def attend(g, carry):
-        at = rows_of(g, SPAN)
-        mean_at = rows_of(g // spans_here, spans_all)
-        shift = score_shift(g)
+    four = groups // 2
+
+    def attend(i):
+        members = [(i * four + u, p) for u in range(four) for p in range(pairs)]
+        shifts = [score_shift(i * four + u) for u in range(four)]
+        places = {
+            g: (rows_of(g, SPAN), rows_of(g // spans_here, spans_all)) for g, _ in members
+        }
         scores = [
             dot(
-                pair_rows(at, mean_at, 1, p),
-                head_pair(packed[at, p * lanes : (p + 1) * lanes] * factor),
+                pair_rows(*places[g], 1, p),
+                head_pair(packed[places[g][0], p * lanes : (p + 1) * lanes] * factor),
                 1,
                 1,
             )
-            for p in range(pairs)
+            for g, p in members
         ]
         weights = []
-        for p in range(pairs):
-            shifted = scores[p] + shift
+        for n, (g, p) in enumerate(members):
+            shifted = scores[n] + shifts[n // pairs]
             expo = jnp.exp(shifted - jnp.max(shifted, axis=0, keepdims=True))
             total_row = jnp.sum(expo, axis=0, keepdims=True)
             weights.append((expo * (1.0 / total_row)).astype(BF))
-            probs[g * pairs + p] = weights[p]
-        for p in range(pairs):
-            mixed = dot(weights[p], pair_rows(at, mean_at, 2, p), 0, 0)
-            att[at, p * lanes : (p + 1) * lanes] = jnp.where(
+            probs[g * pairs + p] = weights[n]
+        for n, (g, p) in enumerate(members):
+            mixed = dot(weights[n], pair_rows(*places[g], 2, p), 0, 0)
+            att[places[g][0], p * lanes : (p + 1) * lanes] = jnp.where(
                 low_out, mixed[0:SPAN], mixed[SPAN : 2 * SPAN]
             ).astype(BF)
-        return carry
-
-    lax.fori_loop(0, groups // 2, attend, 0)
+
+    attend(0)
+    gather_core(UP)
+    attend(1)
+    gather_forward(DOWN)
     gather_last(OUT)
-    gather_core(UP)
+    gather_done(OUT)
+
+    mid = tok[...].astype(F32) + dot(att[...], wo[...], 1, 0) + out_shift
+    middle[...] = mid
+    xhat, inverse = norm_stats(mid)
+    xhat2[...] = xhat
+    inv2[...] = inverse
+    second[...] = (xhat * gain2 + bias2).astype(BF)
     gather_last(UP)
-    lax.fori_loop(groups // 2, groups, attend, 0)
-    gather_done(OUT)
-
-    def second_norm(i, carry):
-        at = rows_of(i, 256)
-        mid = tok[at, :].astype(F32) + dot(att[at, :], wo[...], 1, 0) + out_shift
-        middle[at, :] = mid
-        xhat, inverse = norm_stats(mid)
-        xhat2[at, :] = xhat
-        inv2[at, :] = inverse
-        second[at, :] = (xhat * gain2 + bias2).astype(BF)
-        return carry
-
-    lax.fori_loop(0, rows // 256, second_norm, 0)
-    gather_forward(DOWN)
+    gather_core(DOWN)
     gather_done(UP)
 
-    def feed_up(i, carry):
-        at = rows_of(i // (ff // 512), big)
-        cols = rows_of(lax.rem(i, ff // 512), 512)
-        before = dot(second[at, :], wu[:, cols], 1, 0) + up_bias[0:1, cols]
+    half_owners = shard_count // 2
+    sub = half_owners * lanes
+
+    def unit_starts(part, side):
+        return [
+            (side * half_owners + n) * up_here + part * lanes for n in range(half_owners)
+        ]
+
+    def up_tile(part, side):
+        return jnp.concatenate(
+            [wu[:, a : a + lanes] for a in unit_starts(part, side)], axis=1
+        )
+
+    def down_tile(part, side):
+        return jnp.concatenate(
+            [wd[a : a + lanes, :] for a in unit_starts(part, side)], axis=0
+        )
+
+    def columns_of(part, side):
+        start = part * part_cols + side * sub
+        return slice(start, start + sub)
+
+    every = [(part, side) for part in range(parts) for side in range(2)]
+
+    def gelu_parts(before):
         cdf = 0.5 + 0.5 * lax.erf(before * math.sqrt(0.5))
         density = jnp.exp(before * before * -0.5) * (1.0 / math.sqrt(2.0 * math.pi))
-        hidden[at, cols] = (before * cdf).astype(BF)
-        gbefore[at, cols] = (cdf + before * density).astype(BF)
-        return carry
-
-    feed_steps = rows // big * (ff // 512)
-    lax.fori_loop(0, feed_steps // 2, feed_up, 0)
-    gather_core(DOWN)
+        return before * cdf, cdf + before * density
+
+    def feed_up(part, side):
+        cols = columns_of(part, side)
+        before = dot(second[...], up_tile(part, side), 1, 0) + up_bias[0:1, cols]
+        value, slope = gelu_parts(before)
+        hidden[:, cols] = value.astype(BF)
+        gbefore[:, cols] = slope.astype(BF)
+
+    def back_down(part, side):
+        cols = columns_of(part, side)
+        grad = dot(cot[...], down_tile(part, side), 1, 1)
+        gbefore[:, cols] = (grad * gbefore[:, cols].astype(F32)).astype(BF)
+
+    feed_up(0, 0)
+    feed_up(0, 1)
+    feed_up(1, 0)
     gather_last(DOWN)
-    lax.fori_loop(feed_steps // 2, feed_steps, feed_up, 0)
+    feed_up(1, 1)
+    cot_in.wait()
     gather_done(DOWN)
-    cot_in.wait()
 
     def chunk(which):
-        if which == GD:
-            return (g_down, r1_down, r2_down, r3_down, r4_down, own_down)
-        if which == GU:
-            return (g_up, r1_up, r2_up, r3_up, r4_up, own_up)
-        if which == GO:
-            return (g_out, r1_out, r2_out, r3_out, r4_out, own_out)
-        n = which - GP
-        return tuple(ref.at[n] for ref in (g_qkv, r1_qkv, r2_qkv, r3_qkv, r4_qkv, own_qkv))
+        if which in (D0, D1):
+            refs, n = (g_down, r1_down, r2_down, r3_down, r4_down, own_down), which - D0
+        elif which in (U0, U1):
+            refs, n = (g_up, r1_up, r2_up, r3_up, r4_up, own_up), which - U0
+        elif which == GO:
+            refs, n = (g_out, r1_out, r2_out, r3_out, r4_out, own_out), 0
+        elif which == QA:
+            refs, n = (g_two, r1_two, r2_two, r3_two, r4_two, own_two), 0
+        else:
+            refs, n = (g_one, r1_one, r2_one, r3_one, r4_one, own_one), which - Q2
+        return tuple(ref.at[n] for ref in refs)
 
     here, x_blk, y_blk, d_blk = yx, flip(yx, 1), flip(yx, 2), flip(flip(yx, 1), 2)
     z_dev = (ms, flip(mq, 1))
@@ -533,7 +603,7 @@
         ]
         return copies
 
-    r_copies = [reduce_copies(which) for which in range(GP + pairs)]
+    r_copies = [reduce_copies(which) for which in range(CHUNKS)]
     edge = jnp.logical_or(mq == 0, mq == seq_count - 1)
     inner = jnp.logical_not(edge)
 
@@ -543,10 +613,10 @@
 
         def one(i, carry):
             at = rows_of(i, step)
-            value = target[at, :].astype(F32)
+            value = target[at, :]
             for source in sources:
-                value = value + source[at, :].astype(F32)
-            target[at, :] = value.astype(BF)
+                value = value + source[at, :]
+            target[at, :] = value
             return carry
 
         lax.fori_loop(0, count // step, one, 0)
@@ -608,13 +678,17 @@
             add_rows(own, r4.at[0])
             c[6].start()
 
-    out_hbm = (gd_hbm, gu_hbm, go_hbm)
-
     def emit(which, source):
-        if which <= GO:
-            target = out_hbm[which]
-        else:
-            target = gq_hbm.at[which - GP]
+        target = {
+            D0: gd_hbm.at[pl.ds(0, lanes)],
+            D1: gd_hbm.at[pl.ds(lanes, lanes)],
+            U0: gu_hbm.at[0],
+            U1: gu_hbm.at[1],
+            GO: go_hbm,
+            QA: gt_hbm,
+            Q2: gs_hbm.at[0],
+            Q3: gs_hbm.at[1],
+        }[which]
         return pltpu.make_async_copy(source, target, out_sem.at[which])
 
     def reduce_f(which):
@@ -647,47 +721,44 @@
             c[step].wait_send()
         emit(which, own).wait()
 
-    down_rows = ff // shard_count
-
-    def down_grad(o, carry):
-        piece = dot(hidden[:, rows_of(o, 2 * down_rows)], cot[...], 0, 0).astype(BF)
-        g_down[0, o] = piece[0:down_rows]
-        g_down[1, o] = piece[down_rows:]
-        return carry
-
-    lax.fori_loop(0, shard_count // 2, down_grad, 0)
-    reduce_a(GD)
-
-    def back_down(i, carry):
-        at = rows_of(i // (ff // 512), big)
-        cols = rows_of(lax.rem(i, ff // 512), 512)
-        grad = dot(cot[at, :], wd[cols, :], 1, 1)
-        grad = (grad * gbefore[at, cols].astype(F32)).astype(BF)
-        gbefore[at, cols] = grad
-        return carry
-
-    lax.fori_loop(0, feed_steps, back_down, 0)
-    reduce_b(GD)
-
-    def up_grad(n, carry):
-        cols = rows_of(n, 512)
-        piece = dot(second[...], gbefore[:, cols], 0, 0).astype(BF)
+    def put_rows(target, piece):
+        count = piece.shape[0] // shard_count
         for owner in range(shard_count):
-            g_up[owner % 2, owner // 2, :, cols] = piece[
-                owner * shard_rows : (owner + 1) * shard_rows
-            ]
+            target[owner % 2, owner // 2] = piece[owner * count : (owner + 1) * count]
+
+    def part_of(part):
+        return slice(part * part_cols, (part + 1) * part_cols)
+
+    def down_grad(part):
+        put_rows(g_down.at[part], dot(hidden[:, part_of(part)], cot[...], 0, 0).astype(BF))
+
+    def up_grad(part):
+        cols = part_of(part)
+        put_rows(g_up.at[part], dot(second[...], gbefore[:, cols], 0, 0).astype(BF))
         upsum[0:1, cols] = jnp.sum(gbefore[:, cols].astype(F32), axis=0, keepdims=True)
-        return carry
-
-    lax.fori_loop(0, ff // 512, up_grad, 0)
-    reduce_a(GU)
-    reduce_c(GD)
+
+    back_down(0, 0)
+    back_down(0, 1)
+    down_grad(0)
+    reduce_a(D0)
+    up_grad(0)
+    reduce_a(U0)
+    back_down(1, 0)
+    back_down(1, 1)
+    reduce_b(D0)
+    down_grad(1)
+    reduce_a(D1)
+    reduce_b(U0)
+    up_grad(1)
+    reduce_a(U1)
+    reduce_c(D0)
 
     vsum[...] = jnp.zeros_like(vsum)
-
-    def back_second(i, carry):
-        at = rows_of(i, 256)
-        grad = dot(gbefore[at, :], wu[...], 1, 1)
+    up_perm = jnp.concatenate([up_tile(*t) for t in every], axis=1)
+
+    def back_second(i):
+        at = rows_of(i, big)
+        grad = dot(gbefore[at, :], up_perm, 1, 1)
         xhat = xhat2[at, :]
         vsum[3:4, :] += jnp.sum(grad * xhat, axis=0, keepdims=True)
         vsum[4:5, :] += jnp.sum(grad, axis=0, keepdims=True)
@@ -699,170 +770,177 @@
         gbranch[at, :] = branch
         vsum[2:3, :] += jnp.sum(branch.astype(F32), axis=0, keepdims=True)
         gatt[at, :] = dot(branch, wo[...], 1, 1).astype(BF)
-        return carry
-
-    lax.fori_loop(0, rows // 256, back_second, 0)
-    reduce_b(GU)
-    reduce_d(GD)
-
-    def put_rows(target, piece):
-        for owner in range(shard_count):
-            target[owner % 2, owner // 2] = piece[
-                owner * shard_rows : (owner + 1) * shard_rows
-            ]
-
-    put_rows(g_out, dot(att[...], gbranch[...], 0, 0).astype(BF))
+
+    back_second(0)
+    reduce_b(D1)
+    reduce_c(U0)
+    reduce_b(U1)
+    back_second(1)
+    reduce_d(D0)
+    reduce_c(D1)
+    put_rows(g_out.at[0], dot(att[...], gbranch[...], 0, 0).astype(BF))
     reduce_a(GO)
-    reduce_c(GU)
 
     low_keys = lax.broadcasted_iota(jnp.int32, (SPAN, lanes), 1) < HD
-    together = 2 * spans_here
-
-    def attend_back(p, i, carry):
+
+    def attend_back(p):
         lo = p * lanes
+        places = [(rows_of(g, SPAN), rows_of(g // spans_here, spans_all)) for g in range(groups)]
         members = []
-        for u in range(together):
-            g = i * together + u
-            at = rows_of(g, SPAN)
-            mean_at = rows_of(g // spans_here, spans_all)
+        for g in range(groups):
+            at, mean_at = places[g]
             go = head_pair(gatt[at, lo : lo + lanes])
             weights = probs[g * pairs + p]
             gw = dot(pair_rows(at, mean_at, 2, p), go, 1, 1)
             gv = dot(weights, go, 1, 0)
-            members.append((at, mean_at, weights, gw, gv))
+            members.append((weights, gw, gv))
         scores = []
-        for at, mean_at, weights, gw, gv in members:
+        for weights, gw, gv in members:
             prob = weights.astype(F32)
             row_inner = jnp.sum(prob * gw, axis=0, keepdims=True)
             scores.append((prob * (gw - row_inner)).astype(BF))
         far_k, far_v = None, None
-        for u in range(together):
-            at, mean_at, weights, gw, gv = members[u]
+        for g in range(groups):
+            at, mean_at = places[g]
+            gv = members[g][2]
             q = head_pair(packed[at, lo : lo + lanes])
-            gq = dot(scores[u], pair_rows(at, mean_at, 1, p), 0, 0)
-            gk = dot(scores[u], q, 1, 0) * factor
-            packed[at, lo : lo + lanes] = (
+            gq = dot(scores[g], pair_rows(at, mean_at, 1, p), 0, 0)
+            gk = dot(scores[g], q, 1, 0) * factor
+            gbefore[at, lo : lo + lanes] = (
                 jnp.where(low_keys, gq[0:SPAN], gq[SPAN : 2 * SPAN]) * factor
             ).astype(BF)
-            packed[at, width + lo : width + lo + lanes] = gk[0:SPAN].astype(BF)
-            packed[at, 2 * width + lo : 2 * width + lo + lanes] = gv[0:SPAN].astype(BF)
-            first = u % spans_here == 0
+            gbefore[at, width + lo : width + lo + lanes] = gk[0:SPAN].astype(BF)
+            gbefore[at, 2 * width + lo : 2 * width + lo + lanes] = gv[0:SPAN].astype(BF)
+            first = g % spans_here == 0
             far_k = gk[SPAN:] if first else far_k + gk[SPAN:]
             far_v = gv[SPAN:] if first else far_v + gv[SPAN:]
-            if u % spans_here == spans_here - 1:
+            if g % spans_here == spans_here - 1:
                 gkv[mean_at, lo : lo + lanes] = far_k.astype(BF)
                 gkv[mean_at, width + lo : width + lo + lanes] = far_v.astype(BF)
-        return carry
-
-    def pair_back(p):
-        lo = p * lanes
-        lax.fori_loop(0, groups // together, functools.partial(attend_back, p), 0)
-        grads = [packed[:, n * width + lo : n * width + lo + lanes] for n in range(3)]
-        means = [gkv[:, n * width + lo : n * width + lo + lanes] for n in range(2)]
+
+    def first_grad(lo, count, target):
+        grads = [gbefore[:, m * width + lo : m * width + lo + count] for m in range(3)]
+        means = [gkv[:, m * width + lo : m * width + lo + count] for m in range(2)]
         local_part = dot(normed[...], jnp.concatenate(grads, axis=1), 0, 0)
         mean_part = dot(nbar[...], jnp.concatenate(means, axis=1), 0, 0)
         piece = jnp.concatenate(
-            [local_part[:, 0:lanes], local_part[:, lanes:] + mean_part], axis=1
+            [local_part[:, 0:count], local_part[:, count:] + mean_part], axis=1
         )
-        put_rows(g_qkv.at[p], piece.astype(BF))
-        reduce_a(GP + p)
-
-    pair_back(0)
+        put_rows(target, piece.astype(BF))
+
+    attend_back(0)
+    attend_back(1)
     reduce_b(GO)
-    reduce_d(GU)
-    reduce_e(GD)
-    pair_back(1)
-    reduce_b(GP)
+    reduce_d(U0)
+    reduce_c(U1)
+    first_grad(0, 2 * lanes, g_two.at[0])
+    reduce_a(QA)
+    reduce_e(D0)
+    attend_back(2)
+    reduce_d(D1)
     reduce_c(GO)
-    reduce_e(GU)
-    reduce_f(GD)
-    pair_back(2)
-    reduce_b(GP + 1)
-    reduce_c(GP)
-    reduce_d(GO)
-    reduce_f(GU)
-    pair_back(3)
-    reduce_b(GP + 2)
-    reduce_c(GP + 1)
-    reduce_d(GP)
-    reduce_e(GO)
+    first_grad(2 * lanes, lanes, g_one.at[0])
+    reduce_a(Q2)
+    reduce_b(QA)
+    reduce_e(U0)
+    attend_back(3)
 
     gmean = dot(gkv[...], wq[:, width : 3 * width], 1, 1).astype(BF)
-    gmean = dot(order, gmean, 0, 0).reshape(total, groups, width)
+    gmean = dot(order[...], gmean, 0, 0).reshape(total, groups, width)
     gn_send[...] = jnp.concatenate(
         [gmean[:, :, :half_width], gmean[:, :, half_width:]], axis=1
     ).astype(BF)
 
-    def gn_copy(source, target, send_at):
-        return pltpu.make_async_remote_copy(
-            src_ref=gn_send.at[target],
-            dst_ref=gn_recv.at[source],
-            send_sem=gn_s.at[send_at],
-            recv_sem=gn_r.at[source],
-            device_id=place(target),
-            device_id_type=MESH,
+    def gs_copy(source, target):
+        return remote(
+            gn_send.at[rows_of(target, seq_count)],
+            gn_recv.at[source],
+            gs_s.at[target],
+            gs_r.at[source],
+            (target, mq),
         )
 
-    def gn_start(target, carry):
-        gn_copy(mt, target, target).start()
-        return carry
-
-    lax.fori_loop(0, mt, gn_start, 0)
-    reduce_b(GP + 3)
-    reduce_c(GP + 2)
-    reduce_d(GP + 1)
-    reduce_e(GP)
-    reduce_f(GO)
-
-    def out_block(i, carry):
-        at = rows_of(i, 256)
+    for target in range(shard_count - 1):
+
+        @pl.when(target < ms)
+        def _(target=target):
+            gs_copy(ms, target).start()
+
+    first_grad(3 * lanes, lanes, g_one.at[1])
+    reduce_a(Q3)
+    reduce_b(Q2)
+    reduce_c(QA)
+    reduce_d(GO)
+    reduce_d(U1)
+    reduce_e(D1)
+    reduce_f(D0)
+    reduce_b(Q3)
+    reduce_f(U0)
+
+    down_perm = jnp.concatenate([down_tile(*t) for t in every], axis=0)
+
+    def out_block(i):
+        at = rows_of(i, big)
         gbranch[at, :] = (
-            middle[at, :] + dot(hidden[at, :], wd[...], 1, 0) + down_shift
+            middle[at, :] + dot(hidden[at, :], down_perm, 1, 0) + down_shift
         ).astype(BF)
-        return carry
-
-    lax.fori_loop(0, rows // 512, out_block, 0)
-    reduce_c(GP + 3)
-    reduce_d(GP + 2)
-    reduce_e(GP + 1)
-    reduce_f(GP)
-    lax.fori_loop(rows // 512, rows // 256, out_block, 0)
+
+    out_block(0)
+    reduce_c(Q2)
+    reduce_e(GO)
+    out_block(1)
     bout_out = pltpu.make_async_copy(gbranch, block_out_hbm, io_sem.at[2])
     bout_out.start()
-
-    def gn_wait(source, carry):
-        gn_copy(source, flip(mt, 1), 0).wait_recv()
-        gnbar[...] += gn_recv[source].astype(F32)
-        return carry
-
-    gnbar[...] = gn_send[mt].astype(F32)
-    lax.fori_loop(mt + 1, total, gn_wait, 0)
-    reduce_d(GP + 3)
-    reduce_e(GP + 2)
-    reduce_f(GP + 1)
-
-    def back_first(i, carry):
-        at = rows_of(i, 2 * SPAN)
+    gz_send[...] = gn_send[rows_of(ms, seq_count)]
+    for source in range(1, shard_count):
+
+        @pl.when(source > ms)
+        def _(source=source):
+            gs_copy(source, source).wait_recv()
+            gz_send[...] += gn_recv[source]
+
+    gz_copies = [
+        remote(gz_send.at[peer[1]], gz_recv.at[mq], gz_s.at[step], gz_r.at[step], peer)
+        for step, peer in enumerate(seq_peers)
+    ]
+    for c in gz_copies:
+        c.start()
+    gz_recv[mq] = gz_send[mq]
+    reduce_d(QA)
+    reduce_f(D1)
+    reduce_c(Q3)
+    reduce_e(U1)
+    reduce_d(Q2)
+    reduce_f(GO)
+    for c in gz_copies:
+        c.wait_recv()
+    gnbar[...] = jnp.sum(gz_recv[...].astype(F32), axis=0)
+
+    def back_first(i):
+        at = rows_of(i, big)
         shares = []
-        for u in range(2):
-            g = 2 * i + u
+        for u in range(big // SPAN):
+            g = i * (big // SPAN) + u
             share = jnp.concatenate(
-                [gnbar[pl.ds(g, 1), :], gnbar[pl.ds(groups + g, 1), :]], axis=1
+                [gnbar[g : g + 1, :], gnbar[groups + g : groups + g + 1, :]], axis=1
             ) * (1.0 / SPAN)
             shares.append(jnp.broadcast_to(share, (SPAN, width)))
-        grad = dot(packed[at, :], wq[...], 1, 1) + jnp.concatenate(shares, axis=0)
+        grad = dot(gbefore[at, 0 : 3 * width], wq[...], 1, 1) + jnp.concatenate(
+            shares, axis=0
+        )
         xhat = xhat1[at, :]
         vsum[0:1, :] += jnp.sum(grad * xhat, axis=0, keepdims=True)
         vsum[1:2, :] += jnp.sum(grad, axis=0, keepdims=True)
         gmid[at, :] = gmid[at, :] + norm_back(grad, xhat, inv1[at, :], gain1)
-        return carry
-
-    lax.fori_loop(0, groups // 4, back_first, 0)
-    reduce_e(GP + 3)
-    reduce_f(GP + 2)
-    lax.fori_loop(groups // 4, groups // 2, back_first, 0)
+
+    back_first(0)
+    reduce_d(Q3)
+    reduce_e(QA)
+    back_first(1)
     tok_out = pltpu.make_async_copy(gmid, grad_tok_hbm, io_sem.at[3])
     tok_out.start()
+    reduce_e(Q2)
+    reduce_f(U1)
 
     for owner in range(shard_count):
         at = owner // 2
@@ -871,63 +949,52 @@
             piece = pltpu.roll(piece, HD, axis=1)
         vec_send[owner, 0:8, :] = piece
         vec_send[owner, 8:16, :] = jnp.zeros((8, lanes), F32)
-        for r in range(up_here // lanes):
-            start = owner * up_here + r * lanes
+        for r in range(parts):
+            start = r * part_cols + owner * lanes
             vec_send[owner, 8 + r : 9 + r, :] = upsum[0:1, start : start + lanes]
-    vo_copies = []
-    for step in range(1, shard_count):
-        target = lax.rem(ms + step, shard_count)
-        vo_copies.append(
-            pltpu.make_async_remote_copy(
-                src_ref=vec_send.at[target],
-                dst_ref=vec_recv.at[ms],
-                send_sem=vo_s.at[step],
-                recv_sem=vo_r.at[step],
-                device_id=(target, mq),
-                device_id_type=MESH,
-            )
-        )
+    vo_copies = [
+        remote(vec_send.at[peer[0]], vec_recv.at[ms], vo_s.at[step], vo_r.at[step], peer)
+        for step, peer in enumerate(shard_peers)
+    ]
     for c in vo_copies:
         c.start()
     vec_recv[ms] = vec_send[ms]
-    reduce_f(GP + 3)
-    for which in range(GP):
+    for which in (D0, U0, D1, GO):
         reduce_g(which)
+    reduce_e(Q3)
+    reduce_f(QA)
+    reduce_f(Q2)
     for c in vo_copies:
         c.wait_recv()
     vec_line[mq] = jnp.sum(vec_recv[...], axis=0)
-    vz_copies = []
-    for step in range(1, seq_count):
-        vz_copies.append(
-            pltpu.make_async_remote_copy(
-                src_ref=vec_line.at[mq],
-                dst_ref=vec_line.at[mq],
-                send_sem=vz_s.at[step],
-                recv_sem=vz_r.at[step],
-                device_id=(ms, lax.rem(mq + step, seq_count)),
-                device_id_type=MESH,
-            )
-        )
+    vz_copies = [
+        remote(vec_line.at[mq], vec_line.at[mq], vz_s.at[step], vz_r.at[step], peer)
+        for step, peer in enumerate(seq_peers)
+    ]
     for c in vz_copies:
         c.start()
-    for which in range(GP, GP + pairs):
-        reduce_g(which)
+    reduce_f(Q3)
+    reduce_g(U1)
+    reduce_g(QA)
     for c in vz_copies:
         c.wait_recv()
     vec_out_ref[...] = jnp.sum(vec_line[...], axis=0)
-
-    def xb_sent(target, carry):
-        xb_copy(mt, target, target).wait_send()
-        return carry
-
-    lax.fori_loop(mt + 1, total, xb_sent, 0)
-
-    def gn_sent(target, carry):
-        gn_copy(mt, target, target).wait_send()
-        return carry
-
-    lax.fori_loop(0, mt, gn_sent, 0)
-    for c in vec_copies + vo_copies + vz_copies:
+    reduce_g(Q2)
+    reduce_g(Q3)
+
+    for target in range(1, shard_count):
+
+        @pl.when(target > ms)
+        def _(target=target):
+            xs_copy(ms, target).wait_send()
+
+    for target in range(shard_count - 1):
+
+        @pl.when(target < ms)
+        def _(target=target):
+            gs_copy(ms, target).wait_send()
+
+    for c in vec_copies + xz_copies + gz_copies + vo_copies + vz_copies:
         c.wait_send()
     for which in range(4):
         for c in w_copies[which]:
@@ -937,34 +1004,55 @@
 
 
 def finish_kernel(*refs):
-    raw, vec, outs, vec_outs = refs[0:6], refs[6], refs[7:13], refs[13:20]
-    low_refs, high_refs, in_sem, out_sem = refs[20:26], refs[26:30], refs[30], refs[31]
-    order = (2, 4, 5, 3, 1, 0)
-    loads = [pltpu.make_async_copy(raw[n], low_refs[n], in_sem.at[n]) for n in range(6)]
+    raw, vec, outs, vec_outs = refs[0:7], refs[7], refs[8:14], refs[14:21]
+    low_refs, high_refs, in_sem, out_sem = refs[21:28], refs[28:32], refs[32], refs[33]
+    order = (5, 6, 4, 0, 1, 2, 3)
+    loads = [pltpu.make_async_copy(raw[n], low_refs[n], in_sem.at[n]) for n in range(7)]
     for n in order:
         loads[n].start()
     for n, ref in enumerate(vec_outs[0:6]):
         ref[...] = vec[n : n + 1, 0 : ref.shape[1]]
     vec_outs[6][...] = vec[8 : 8 + vec_outs[6].shape[0], :]
     stores = []
+    lanes = 2 * HD
+
+    def store(ready, at):
+        stores.append(pltpu.make_async_copy(ready, outs[at], out_sem.at[at]))
+        stores[-1].start()
+
     for n in order:
         loads[n].wait()
-        ready = low_refs[n]
-        if n == 2:
-            ready = high_refs[0]
-            pairs = low_refs[2].shape[0]
-            lanes = low_refs[2].shape[2] // 3
+        low = low_refs[n]
+        if n < 2:
+            store(low, n)
+        elif n == 2:
             for part in range(3):
-                for p in range(pairs):
-                    start = (part * pairs + p) * lanes
-                    ready[:, start : start + lanes] = low_refs[2][
-                        p, :, part * lanes : (part + 1) * lanes
+                start = part * 4 * lanes
+                high_refs[0][:, start : start + 2 * lanes] = low[
+                    :, part * 2 * lanes : (part + 1) * 2 * lanes
+                ].astype(F32)
+        elif n == 3:
+            for part in range(3):
+                for one in range(2):
+                    start = (part * 4 + 2 + one) * lanes
+                    high_refs[0][:, start : start + lanes] = low[
+                        one, :, part * lanes : (part + 1) * lanes
                     ].astype(F32)
-        elif n > 2:
-            ready = high_refs[n - 2]
-            ready[...] = low_refs[n][...].astype(F32)
-        stores.append(pltpu.make_async_copy(ready, outs[n], out_sem.at[n]))
-        stores[-1].start()
+            store(high_refs[0], 2)
+        elif n == 5:
+            high = high_refs[2]
+            part_count, _, columns = low.shape
+            for part in range(part_count):
+                for owner in range(columns // lanes):
+                    start = (owner * part_count + part) * lanes
+                    high[:, start : start + lanes] = low[
+                        part, :, owner * lanes : (owner + 1) * lanes
+                    ].astype(F32)
+            store(high, 4)
+        else:
+            high = high_refs[n - 3]
+            high[...] = low[...].astype(F32)
+            store(high, n - 1)
     for c in stores:
         c.wait()
 
@@ -1012,11 +1100,18 @@
             pltpu.VMEM(lead + (count, columns), BF),
         )
 
-    down_bufs = grads(down_rows, width)
-    up_bufs = grads(shard_rows, ff)
-    out_bufs = grads(shard_rows, width)
-    qkv_bufs = grads(shard_rows, 3 * lanes, (H // 2,))
-    grad_bufs = [buf for four in zip(down_bufs, up_bufs, out_bufs, qkv_bufs) for buf in four]
+    parts = down_rows // lanes
+    part_cols = ff // parts
+    down_bufs = grads(lanes, width, (parts,))
+    up_bufs = grads(shard_rows, part_cols, (parts,))
+    out_bufs = grads(shard_rows, width, (1,))
+    two_bufs = grads(shard_rows, 6 * lanes, (1,))
+    one_bufs = grads(shard_rows, 3 * lanes, (2,))
+    grad_bufs = [
+        buf
+        for five in zip(down_bufs, up_bufs, out_bufs, two_bufs, one_bufs)
+        for buf in five
+    ]
     scratch = [
         pltpu.VMEM((rows, width), BF),
         pltpu.VMEM((rows, width), BF),
@@ -1030,6 +1125,7 @@
         pltpu.VMEM((rows, 1), F32),
         pltpu.VMEM((groups, width), F32),
         pltpu.VMEM((total, 2 * groups, width // 2), BF),
+        pltpu.VMEM((batch * spans_all, batch * spans_all), BF),
         pltpu.VMEM((8, width), F32),
         pltpu.VMEM((8, ff), F32),
         pltpu.VMEM((rows, width), BF),
@@ -1049,7 +1145,9 @@
         pltpu.VMEM((rows, width), BF),
         pltpu.VMEM((batch * spans_all, 2 * width), BF),
         pltpu.VMEM((total, 2 * groups, width // 2), BF),
-        pltpu.VMEM((total, 2 * groups, width // 2), BF),
+        pltpu.VMEM((shard_count, seq_count, 2 * groups, width // 2), BF),
+        pltpu.VMEM((seq_count, 2 * groups, width // 2), BF),
+        pltpu.VMEM((seq_count, 2 * groups, width // 2), BF),
         pltpu.VMEM((2 * groups, width // 2), F32),
         pltpu.VMEM((8, width), F32),
         pltpu.VMEM((8, ff), F32),
@@ -1063,17 +1161,21 @@
         dma((4,)),
         dma((shard_count,)),
         dma((shard_count,)),
-        dma((total,)),
-        dma((total,)),
-        dma((total,)),
-        dma((total,)),
+        dma((seq_count,)),
+        dma((seq_count,)),
+        dma((shard_count,)),
+        dma((shard_count,)),
         dma((shard_count,)),
         dma((shard_count,)),
         dma((seq_count,)),
         dma((seq_count,)),
-        dma(((GP + H // 2) * REDUCE_STEPS,)),
-        dma(((GP + H // 2) * REDUCE_STEPS,)),
-        dma((GP + H // 2,)),
+        dma((shard_count,)),
+        dma((shard_count,)),
+        dma((seq_count,)),
+        dma((seq_count,)),
+        dma((CHUNKS * REDUCE_STEPS,)),
+        dma((CHUNKS * REDUCE_STEPS,)),
+        dma((CHUNKS,)),
     ]
     vectors = [
         v.reshape(1, shard_rows)
@@ -1084,14 +1186,15 @@
         out_shape=(
             jax.ShapeDtypeStruct((rows, width), BF),
             jax.ShapeDtypeStruct((rows, width), F32),
-            jax.ShapeDtypeStruct((H // 2, shard_rows, 3 * lanes), BF),
+            jax.ShapeDtypeStruct((shard_rows, 6 * lanes), BF),
+            jax.ShapeDtypeStruct((2, shard_rows, 3 * lanes), BF),
             jax.ShapeDtypeStruct((shard_rows, width), BF),
-            jax.ShapeDtypeStruct((shard_rows, ff), BF),
+            jax.ShapeDtypeStruct((parts, shard_rows, part_cols), BF),
             jax.ShapeDtypeStruct((down_rows, width), BF),
             jax.ShapeDtypeStruct((16, lanes), F32),
         ),
         in_specs=[hbm, hbm, [vmem] * 6, vmem, hbm, hbm, hbm, hbm],
-        out_specs=(hbm, hbm, hbm, hbm, hbm, hbm, vmem),
+        out_specs=(hbm,) * 7 + (vmem,),
         scratch_shapes=scratch,
         compiler_params=pltpu.CompilerParams(
             collective_id=0, has_side_effects=True, vmem_limit_bytes=63 * 2**20
@@ -1108,12 +1211,18 @@
         down_weight,
     )
     low_shapes = [
-        (H // 2, shard_rows, 3 * lanes),
+        (shard_rows, 6 * lanes),
+        (2, shard_rows, 3 * lanes),
+        (shard_rows, width),
+        (parts, shard_rows, part_cols),
+        (down_rows, width),
+    ]
+    high_shapes = [
+        (shard_rows, 3 * width),
         (shard_rows, width),
         (shard_rows, ff),
         (down_rows, width),
     ]
-    high_shapes = [(shard_rows, 3 * width)] + low_shapes[1:]
     done = pl.pallas_call(
         finish_kernel,
         out_shape=(
@@ -1123,14 +1232,14 @@
             *(jax.ShapeDtypeStruct((1, shard_rows), F32) for _ in range(6)),
             jax.ShapeDtypeStruct((down_rows // lanes, lanes), F32),
         ),
-        in_specs=[hbm] * 6 + [vmem],
+        in_specs=[hbm] * 7 + [vmem],
         out_specs=(hbm,) * 6 + (vmem,) * 7,
         scratch_shapes=[
             pltpu.VMEM((rows, width), BF),
             pltpu.VMEM((rows, width), F32),
             *(pltpu.VMEM(shape, BF) for shape in low_shapes),
             *(pltpu.VMEM(shape, F32) for shape in high_shapes),
-            dma((6,)),
+            dma((7,)),
             dma((6,)),
         ],
         compiler_params=pltpu.CompilerParams(vmem_limit_bytes=62 * 2**20),

time: 114 us -> 98.5 us (0.86)
  Pallas kernels: 113 us -> 97.4 us
    pallas_call x1, Pallas kernels: 108 us -> 92.2 us  [local_block(): pl.pallas_call(functools.partial(block_kernel, batch, shard_count, seq_co...]
where the time goes in v3:
time: 98.5 us; the launch traced here: 98.3 us
  Pallas kernels  97.4 us (99%)
    pallas_call x1, Pallas kernels, local_block(): pl.pallas_call(functools.partial(block_kernel, batch, shard_count, seq_co...  92.2 us
    pallas_call x1, Pallas kernels, local_block(): pl.pallas_call(finish_kernel, out_shape=(jax.ShapeDtypeStruct((rows, widt...  5.23 us

profile of v3, /device:TPU:0, one launch (start us, length us, event | category | flops | bytes accessed | tf_op | source)
XLA Modules:
  0.0 98.3 jit_solution(6471254382867711118)
XLA Ops:
  0.6 92.2 %block.1 = (bf16[1024,512]{1,0:T(8,128)(2,1)}, f32[1024,512]{1,0:T(8,128)}, bf16[64,768]{1,0:T(8,128)(2,1)}, bf16[2,64,384]{2,1,0:T(8,128)(2,1)}, bf16[64,512]{1...) custom-call(bf16[1024,512]{1,0:T(8,128)(2,1)} %bitcast.18, ...), custom_call_target="tpu_custom_call" | custom-call | tf_op jit(solution)/shard_map/block/pallas_call | solution.py:1184
  92.8 5.2 %finish.1 = (bf16[1024,512]{1,0:T(8,128)(2,1)}, f32[1024,512]{1,0:T(8,128)}, f32[64,1536]{1,0:T(8,128)}, f32[64,512]{1,0:T(8,128)}, f32[64,2048]{1,0:T(8,128)}, ...) custom-call(bf16[1024,512]{1,0:T(8,128)(2,1)} %get-tuple-element.34., ...), custom_call_target="tpu_custom_call" | custom-call | tf_op jit(solution)/shard_map/finish/pallas_call | solution.py:1226

commit v4 on v3

--- a/solution.py
+++ b/solution.py
@@ -47,7 +47,8 @@
 QKV, OUT, UP, DOWN = range(4)
 D0, D1, U0, U1, GO, QA, Q2, Q3 = range(8)
 CHUNKS = 8
-GATHER_STEPS = 11
+ALONG_SEQ = ()
+GATHER_STEPS = 12
 REDUCE_STEPS = 8
 
 
@@ -215,22 +216,42 @@
             return full.at[pl.ds(pl.multiple_of(owner * depth + side * half, half), half)]
 
         def own_part(side):
-            return w_hbm[which].at[pl.ds(side * half, half)]
+            return w_hbm[which].at[pl.ds(pl.multiple_of(side * half, half), half)]
 
         x_own, y_own, d_own = flip(ms, 2), flip(ms, 4), flip(flip(ms, 2), 4)
-        plan = (
-            (own_part(0), part(ms, 0), x_dev),
-            (own_part(1), part(ms, 1), y_dev),
-            (own_part(1), part(ms, 1), x_dev),
-            (own_part(0), part(ms, 0), y_dev),
-            (w_hbm[which], block(ms), core_dev),
-            (part(x_own, 0), part(x_own, 0), y_dev),
-            (part(y_own, 1), part(y_own, 1), x_dev),
-            (block(x_own), block(x_own), core_dev),
-            (block(y_own), block(y_own), core_dev),
-            (part(d_own, 0), part(d_own, 0), core_dev),
-            (part(d_own, 1), part(d_own, 1), core_dev),
-        )
+        if which in ALONG_SEQ:
+            h = lax.rem(mq, 2)
+            a_own = x_own + h * (y_own - x_own)
+            b_own = y_own + h * (x_own - y_own)
+            a_dev, b_dev, z_dev = (a_own, mq), (b_own, mq), (ms, flip(mq, 1))
+            plan = (
+                (own_part(h), part(ms, h), a_dev),
+                (own_part(1 - h), part(ms, 1 - h), b_dev),
+                (own_part(1 - h), part(ms, 1 - h), a_dev),
+                (w_hbm[which], block(ms), core_dev),
+                (part(a_own, h), part(a_own, h), b_dev),
+                (part(a_own, 1 - h), part(a_own, 1 - h), z_dev),
+                (block(a_own), block(a_own), core_dev),
+                (part(b_own, 1 - h), part(b_own, 1 - h), core_dev),
+                (part(d_own, h), part(d_own, h), z_dev),
+                (part(d_own, h), part(d_own, h), core_dev),
+                (part(b_own, h), part(b_own, h), core_dev),
+                (part(d_own, 1 - h), part(d_own, 1 - h), core_dev),
+            )
+        else:
+            plan = (
+                (own_part(0), part(ms, 0), x_dev),
+                (own_part(1), part(ms, 1), y_dev),
+                (own_part(1), part(ms, 1), x_dev),
+                (own_part(0), part(ms, 0), y_dev),
+                (w_hbm[which], block(ms), core_dev),
+                (part(x_own, 0), part(x_own, 0), y_dev),
+                (part(y_own, 1), part(y_own, 1), x_dev),
+                (block(x_own), block(x_own), core_dev),
+                (block(y_own), block(y_own), core_dev),
+                (part(d_own, 0), part(d_own, 0), core_dev),
+                (part(d_own, 1), part(d_own, 1), core_dev),
+            )
         return [
             pltpu.make_async_remote_copy(
                 src_ref=src,
@@ -251,44 +272,50 @@
             w_hbm[which], w_full[which].at[rows_of(ms, depth)], w_local.at[which]
         )
 
+    def gather_steps(which, *pairs):
+        c = w_copies[which]
+        for arrived_step, started in pairs:
+            if arrived_step is not None:
+                c[arrived_step].wait_recv()
+            for step in started:
+                c[step].start()
+
     def gather_own_first(which):
-        for step in range(2):
-            w_copies[which][step].start()
+        gather_steps(which, (None, (0, 1)))
 
     def gather_own_second(which):
-        for step in range(2, 5):
-            w_copies[which][step].start()
+        gather_steps(which, (None, (2, 3) if which in ALONG_SEQ else (2, 3, 4)))
         own_copy(which).start()
 
-    def gather_own(which):
-        gather_own_first(which)
-        gather_own_second(which)
-
     def gather_forward(which):
-        c = w_copies[which]
-        c[0].wait_recv()
-        c[5].start()
-        c[1].wait_recv()
-        c[6].start()
+        if which in ALONG_SEQ:
+            gather_steps(which, (0, (4,)))
+        else:
+            gather_steps(which, (0, (5,)), (1, (6,)))
 
     def gather_core(which):
-        c = w_copies[which]
-        c[2].wait_recv()
-        c[7].start()
-        c[3].wait_recv()
-        c[8].start()
+        if which in ALONG_SEQ:
+            gather_steps(which, (2, (5, 6)), (1, (7,)))
+        else:
+            gather_steps(which, (2, (7,)), (3, (8,)))
 
     def gather_last(which):
-        c = w_copies[which]
-        c[5].wait_recv()
-        c[9].start()
-        c[6].wait_recv()
-        c[10].start()
+        if which in ALONG_SEQ:
+            gather_steps(which, (4, (8, 9)))
+        else:
+            gather_steps(which, (5, (9,)), (6, (10,)))
+
+    def gather_z1(which):
+        if which in ALONG_SEQ:
+            gather_steps(which, (5, (10,)))
+
+    def gather_z2(which):
+        if which in ALONG_SEQ:
+            gather_steps(which, (8, (11,)))
 
     def gather_done(which):
-        c = w_copies[which]
-        for step in (4, 7, 8, 9, 10):
-            c[step].wait_recv()
+        for step in (3, 6, 7, 9, 10, 11) if which in ALONG_SEQ else (4, 7, 8, 9, 10):
+            w_copies[which][step].wait_recv()
         own_copy(which).wait()
 
     tok_in.wait()
@@ -346,91 +373,89 @@
             xb_group(owner), xb_group(owner), xs_s.at[target], xs_r.at[owner], (target, mq)
         )
 
-    gather_own(QKV)
-    for c in xz_copies + vec_copies:
-        c.start()
-    vec_all[ms] = vec_own[...]
     mean_rows = total * groups
-    new_row = lax.broadcasted_iota(jnp.int32, (mean_rows, mean_rows), 0)
-    old_row = lax.broadcasted_iota(jnp.int32, (mean_rows, mean_rows), 1)
-
-    def scaled(value, down_by, up_by):
-        quotient = lax.shift_right_logical(value, down_by.bit_length() - 1)
-        return lax.shift_left(quotient, up_by.bit_length() - 1)
-
-    wanted = (
-        scaled(new_row & (spans_all - 1), spans_here, groups)
-        + scaled(new_row, spans_all, spans_here)
-        + (new_row & (spans_here - 1))
-    )
-    order[...] = (old_row == wanted).astype(BF)
-    for c in xz_copies:
-        c.wait_recv()
-    for target in range(1, shard_count):
-
-        @pl.when(target > ms)
-        def _(target=target):
-            xs_copy(ms, target).start()
-
-    gather_forward(QKV)
-    gather_own(OUT)
-    gather_own(UP)
-    gather_core(QKV)
-    gather_own_first(DOWN)
-    for c in vec_copies:
-        c.wait_recv()
-    low_lane = lax.broadcasted_iota(jnp.int32, (8, lanes), 1) < HD
-    for at in range(shard_count // 2):
-        even = vec_all[2 * at]
-        odd = vec_all[2 * at + 1]
-        vfull[:, at * lanes : (at + 1) * lanes] = jnp.where(
-            low_lane, even[0:8, :], pltpu.roll(odd[0:8, :], HD, axis=1)
-        )
     up_here = ff // shard_count
     parts = up_here // lanes
     part_cols = shard_count * lanes
-    for owner in range(shard_count):
-        piece = vec_all[owner]
-        for r in range(up_here // lanes):
-            start = r * part_cols + owner * lanes
-            up_bias[0:1, start : start + lanes] = piece[8 + r : 9 + r, :]
-    gather_last(QKV)
-    gather_done(QKV)
-    gain1, bias1 = vfull[0:1, :], vfull[1:2, :]
-    out_shift = vfull[2:3, :]
-    gain2, bias2 = vfull[3:4, :], vfull[4:5, :]
-    down_shift = vfull[5:6, :]
-
-    tile = (xhat1[...] * gain1 + bias1).astype(BF)
-    normed[...] = tile
+
+    def vec_start():
+        for c in vec_copies:
+            c.start()
+        vec_all[ms] = vec_own[...]
+
+    def xz_start():
+        for c in xz_copies:
+            c.start()
+
+    def xz_wait():
+        for c in xz_copies:
+            c.wait_recv()
+
+    def order_rows():
+        new_row = lax.broadcasted_iota(jnp.int32, (mean_rows, mean_rows), 0)
+        old_row = lax.broadcasted_iota(jnp.int32, (mean_rows, mean_rows), 1)
+
+        def scaled(value, down_by, up_by):
+            quotient = lax.shift_right_logical(value, down_by.bit_length() - 1)
+            return lax.shift_left(quotient, up_by.bit_length() - 1)
+
+        wanted = (
+            scaled(new_row & (spans_all - 1), spans_here, groups)
+            + scaled(new_row, spans_all, spans_here)
+            + (new_row & (spans_here - 1))
+        )
+        order[...] = (old_row == wanted).astype(BF)
+
+    def xs_start():
+        for target in range(1, shard_count):
+
+            @pl.when(target > ms)
+            def _(target=target):
+                xs_copy(ms, target).start()
+
+    def xs_wait():
+        for owner in range(shard_count - 1):
+
+            @pl.when(owner < ms)
+            def _(owner=owner):
+                xs_copy(owner, owner).wait_recv()
+
+    def vec_wait():
+        for c in vec_copies:
+            c.wait_recv()
+        low_lane = lax.broadcasted_iota(jnp.int32, (8, lanes), 1) < HD
+        for at in range(shard_count // 2):
+            even = vec_all[2 * at]
+            odd = vec_all[2 * at + 1]
+            vfull[:, at * lanes : (at + 1) * lanes] = jnp.where(
+                low_lane, even[0:8, :], pltpu.roll(odd[0:8, :], HD, axis=1)
+            )
+        for owner in range(shard_count):
+            piece = vec_all[owner]
+            for r in range(up_here // lanes):
+                start = r * part_cols + owner * lanes
+                up_bias[0:1, start : start + lanes] = piece[8 + r : 9 + r, :]
+
+    def vector(n):
+        return vfull[n : n + 1, :]
 
     def project(n):
+        if n == 0:
+            normed[...] = (xhat1[...] * vector(0) + vector(1)).astype(BF)
         packed[:, n * width : (n + 1) * width] = dot(
-            tile, wq[:, n * width : (n + 1) * width], 1, 0
+            normed[...], wq[:, n * width : (n + 1) * width], 1, 0
         ).astype(BF)
 
-    project(0)
-    gather_forward(OUT)
-    project(1)
-    gather_forward(UP)
-    project(2)
-    gather_core(OUT)
-    gather_own_second(DOWN)
-
-    for owner in range(shard_count - 1):
-
-        @pl.when(owner < ms)
-        def _(owner=owner):
-            xs_copy(owner, owner).wait_recv()
-
-    arrived = xb_all[...].astype(F32)
-    arrived = jnp.concatenate([arrived[:, 0:groups, :], arrived[:, groups:, :]], axis=2)
-    arrived = arrived.reshape(mean_rows, width)
-    nbar[...] = dot(order[...], (arrived * gain1 + bias1).astype(BF), 1, 0).astype(BF)
-    for n in range(2):
-        kv_mean[:, n * width : (n + 1) * width] = dot(
-            nbar[...], wq[:, (n + 1) * width : (n + 2) * width], 1, 0
-        ).astype(BF)
+    def span_means():
+        arrived = xb_all[...].astype(F32)
+        arrived = jnp.concatenate([arrived[:, 0:groups, :], arrived[:, groups:, :]], axis=2)
+        arrived = arrived.reshape(mean_rows, width)
+        arrived = (arrived * vector(0) + vector(1)).astype(BF)
+        nbar[...] = dot(order[...], arrived, 1, 0).astype(BF)
+        for n in range(2):
+            kv_mean[:, n * width : (n + 1) * width] = dot(
+                nbar[...], wq[:, (n + 1) * width : (n + 2) * width], 1, 0
+            ).astype(BF)
 
     factor = HD ** (-0.5)
     keys = SPAN + spans_all
@@ -493,22 +518,13 @@
                 low_out, mixed[0:SPAN], mixed[SPAN : 2 * SPAN]
             ).astype(BF)
 
-    attend(0)
-    gather_core(UP)
-    attend(1)
-    gather_forward(DOWN)
-    gather_last(OUT)
-    gather_done(OUT)
-
-    mid = tok[...].astype(F32) + dot(att[...], wo[...], 1, 0) + out_shift
-    middle[...] = mid
-    xhat, inverse = norm_stats(mid)
-    xhat2[...] = xhat
-    inv2[...] = inverse
-    second[...] = (xhat * gain2 + bias2).astype(BF)
-    gather_last(UP)
-    gather_core(DOWN)
-    gather_done(UP)
+    def second_norm():
+        mid = tok[...].astype(F32) + dot(att[...], wo[...], 1, 0) + vector(2)
+        middle[...] = mid
+        xhat, inverse = norm_stats(mid)
+        xhat2[...] = xhat
+        inv2[...] = inverse
+        second[...] = (xhat * vector(3) + vector(4)).astype(BF)
 
     half_owners = shard_count // 2
     sub = half_owners * lanes
@@ -550,14 +566,6 @@
         cols = columns_of(part, side)
         grad = dot(cot[...], down_tile(part, side), 1, 1)
         gbefore[:, cols] = (grad * gbefore[:, cols].astype(F32)).astype(BF)
-
-    feed_up(0, 0)
-    feed_up(0, 1)
-    feed_up(1, 0)
-    gather_last(DOWN)
-    feed_up(1, 1)
-    cot_in.wait()
-    gather_done(DOWN)
 
     def chunk(which):
         if which in (D0, D1):
@@ -719,7 +727,6 @@
 
         for step in range(5):
             c[step].wait_send()
-        emit(which, own).wait()
 
     def put_rows(target, piece):
         count = piece.shape[0] // shard_count
@@ -737,49 +744,24 @@
         put_rows(g_up.at[part], dot(second[...], gbefore[:, cols], 0, 0).astype(BF))
         upsum[0:1, cols] = jnp.sum(gbefore[:, cols].astype(F32), axis=0, keepdims=True)
 
-    back_down(0, 0)
-    back_down(0, 1)
-    down_grad(0)
-    reduce_a(D0)
-    up_grad(0)
-    reduce_a(U0)
-    back_down(1, 0)
-    back_down(1, 1)
-    reduce_b(D0)
-    down_grad(1)
-    reduce_a(D1)
-    reduce_b(U0)
-    up_grad(1)
-    reduce_a(U1)
-    reduce_c(D0)
-
-    vsum[...] = jnp.zeros_like(vsum)
-    up_perm = jnp.concatenate([up_tile(*t) for t in every], axis=1)
-
     def back_second(i):
         at = rows_of(i, big)
+        up_perm = jnp.concatenate([up_tile(*t) for t in every], axis=1)
         grad = dot(gbefore[at, :], up_perm, 1, 1)
         xhat = xhat2[at, :]
         vsum[3:4, :] += jnp.sum(grad * xhat, axis=0, keepdims=True)
         vsum[4:5, :] += jnp.sum(grad, axis=0, keepdims=True)
         incoming = cot[at, :].astype(F32)
         vsum[5:6, :] += jnp.sum(incoming, axis=0, keepdims=True)
-        grad_mid = incoming + norm_back(grad, xhat, inv2[at, :], gain2)
+        grad_mid = incoming + norm_back(grad, xhat, inv2[at, :], vector(3))
         gmid[at, :] = grad_mid
         branch = grad_mid.astype(BF)
         gbranch[at, :] = branch
         vsum[2:3, :] += jnp.sum(branch.astype(F32), axis=0, keepdims=True)
         gatt[at, :] = dot(branch, wo[...], 1, 1).astype(BF)
 
-    back_second(0)
-    reduce_b(D1)
-    reduce_c(U0)
-    reduce_b(U1)
-    back_second(1)
-    reduce_d(D0)
-    reduce_c(D1)
-    put_rows(g_out.at[0], dot(att[...], gbranch[...], 0, 0).astype(BF))
-    reduce_a(GO)
+    def out_grad():
+        put_rows(g_out.at[0], dot(att[...], gbranch[...], 0, 0).astype(BF))
 
     low_keys = lax.broadcasted_iota(jnp.int32, (SPAN, lanes), 1) < HD
 
@@ -828,28 +810,12 @@
         )
         put_rows(target, piece.astype(BF))
 
-    attend_back(0)
-    attend_back(1)
-    reduce_b(GO)
-    reduce_d(U0)
-    reduce_c(U1)
-    first_grad(0, 2 * lanes, g_two.at[0])
-    reduce_a(QA)
-    reduce_e(D0)
-    attend_back(2)
-    reduce_d(D1)
-    reduce_c(GO)
-    first_grad(2 * lanes, lanes, g_one.at[0])
-    reduce_a(Q2)
-    reduce_b(QA)
-    reduce_e(U0)
-    attend_back(3)
-
-    gmean = dot(gkv[...], wq[:, width : 3 * width], 1, 1).astype(BF)
-    gmean = dot(order[...], gmean, 0, 0).reshape(total, groups, width)
-    gn_send[...] = jnp.concatenate(
-        [gmean[:, :, :half_width], gmean[:, :, half_width:]], axis=1
-    ).astype(BF)
+    def mean_grad():
+        gmean = dot(gkv[...], wq[:, width : 3 * width], 1, 1).astype(BF)
+        gmean = dot(order[...], gmean, 0, 0).reshape(total, groups, width)
+        gn_send[...] = jnp.concatenate(
+            [gmean[:, :, :half_width], gmean[:, :, half_width:]], axis=1
+        ).astype(BF)
 
     def gs_copy(source, target):
         return remote(
@@ -860,61 +826,49 @@
             (target, mq),
         )
 
-    for target in range(shard_count - 1):
-
-        @pl.when(target < ms)
-        def _(target=target):
-            gs_copy(ms, target).start()
-
-    first_grad(3 * lanes, lanes, g_one.at[1])
-    reduce_a(Q3)
-    reduce_b(Q2)
-    reduce_c(QA)
-    reduce_d(GO)
-    reduce_d(U1)
-    reduce_e(D1)
-    reduce_f(D0)
-    reduce_b(Q3)
-    reduce_f(U0)
-
-    down_perm = jnp.concatenate([down_tile(*t) for t in every], axis=0)
-
-    def out_block(i):
-        at = rows_of(i, big)
-        gbranch[at, :] = (
-            middle[at, :] + dot(hidden[at, :], down_perm, 1, 0) + down_shift
-        ).astype(BF)
-
-    out_block(0)
-    reduce_c(Q2)
-    reduce_e(GO)
-    out_block(1)
-    bout_out = pltpu.make_async_copy(gbranch, block_out_hbm, io_sem.at[2])
-    bout_out.start()
-    gz_send[...] = gn_send[rows_of(ms, seq_count)]
-    for source in range(1, shard_count):
-
-        @pl.when(source > ms)
-        def _(source=source):
-            gs_copy(source, source).wait_recv()
-            gz_send[...] += gn_recv[source]
+    def gs_start():
+        for target in range(shard_count - 1):
+
+            @pl.when(target < ms)
+            def _(target=target):
+                gs_copy(ms, target).start()
+
+    def gs_wait():
+        gz_send[...] = gn_send[rows_of(ms, seq_count)]
+        for source in range(1, shard_count):
+
+            @pl.when(source > ms)
+            def _(source=source):
+                gs_copy(source, source).wait_recv()
+                gz_send[...] += gn_recv[source]
 
     gz_copies = [
         remote(gz_send.at[peer[1]], gz_recv.at[mq], gz_s.at[step], gz_r.at[step], peer)
         for step, peer in enumerate(seq_peers)
     ]
-    for c in gz_copies:
-        c.start()
-    gz_recv[mq] = gz_send[mq]
-    reduce_d(QA)
-    reduce_f(D1)
-    reduce_c(Q3)
-    reduce_e(U1)
-    reduce_d(Q2)
-    reduce_f(GO)
-    for c in gz_copies:
-        c.wait_recv()
-    gnbar[...] = jnp.sum(gz_recv[...].astype(F32), axis=0)
+
+    def gz_start():
+        for c in gz_copies:
+            c.start()
+        gz_recv[mq] = gz_send[mq]
+
+    def gz_wait():
+        for c in gz_copies:
+            c.wait_recv()
+        gnbar[...] = jnp.sum(gz_recv[...].astype(F32), axis=0)
+
+    bout_out = pltpu.make_async_copy(gbranch, block_out_hbm, io_sem.at[2])
+
+    def out_block(i):
+        at = rows_of(i, big)
+        down_perm = jnp.concatenate([down_tile(*t) for t in every], axis=0)
+        gbranch[at, :] = (
+            middle[at, :] + dot(hidden[at, :], down_perm, 1, 0) + vector(5)
+        ).astype(BF)
+        if i == 1:
+            bout_out.start()
+
+    tok_out = pltpu.make_async_copy(gmid, grad_tok_hbm, io_sem.at[3])
 
     def back_first(i):
         at = rows_of(i, big)
@@ -931,55 +885,181 @@
         xhat = xhat1[at, :]
         vsum[0:1, :] += jnp.sum(grad * xhat, axis=0, keepdims=True)
         vsum[1:2, :] += jnp.sum(grad, axis=0, keepdims=True)
-        gmid[at, :] = gmid[at, :] + norm_back(grad, xhat, inv1[at, :], gain1)
-
-    back_first(0)
-    reduce_d(Q3)
-    reduce_e(QA)
-    back_first(1)
-    tok_out = pltpu.make_async_copy(gmid, grad_tok_hbm, io_sem.at[3])
-    tok_out.start()
-    reduce_e(Q2)
-    reduce_f(U1)
-
-    for owner in range(shard_count):
-        at = owner // 2
-        piece = vsum[:, at * lanes : (at + 1) * lanes]
-        if owner % 2 == 1:
-            piece = pltpu.roll(piece, HD, axis=1)
-        vec_send[owner, 0:8, :] = piece
-        vec_send[owner, 8:16, :] = jnp.zeros((8, lanes), F32)
-        for r in range(parts):
-            start = r * part_cols + owner * lanes
-            vec_send[owner, 8 + r : 9 + r, :] = upsum[0:1, start : start + lanes]
+        gmid[at, :] = gmid[at, :] + norm_back(grad, xhat, inv1[at, :], vector(0))
+        if i == 1:
+            tok_out.start()
+
+    def vec_build():
+        for owner in range(shard_count):
+            at = owner // 2
+            piece = vsum[:, at * lanes : (at + 1) * lanes]
+            if owner % 2 == 1:
+                piece = pltpu.roll(piece, HD, axis=1)
+            vec_send[owner, 0:8, :] = piece
+            vec_send[owner, 8:16, :] = jnp.zeros((8, lanes), F32)
+            for r in range(parts):
+                start = r * part_cols + owner * lanes
+                vec_send[owner, 8 + r : 9 + r, :] = upsum[0:1, start : start + lanes]
+
     vo_copies = [
         remote(vec_send.at[peer[0]], vec_recv.at[ms], vo_s.at[step], vo_r.at[step], peer)
         for step, peer in enumerate(shard_peers)
     ]
-    for c in vo_copies:
-        c.start()
-    vec_recv[ms] = vec_send[ms]
-    for which in (D0, U0, D1, GO):
-        reduce_g(which)
-    reduce_e(Q3)
-    reduce_f(QA)
-    reduce_f(Q2)
-    for c in vo_copies:
-        c.wait_recv()
-    vec_line[mq] = jnp.sum(vec_recv[...], axis=0)
     vz_copies = [
         remote(vec_line.at[mq], vec_line.at[mq], vz_s.at[step], vz_r.at[step], peer)
         for step, peer in enumerate(seq_peers)
     ]
-    for c in vz_copies:
-        c.start()
+
+    def vo_start():
+        for c in vo_copies:
+            c.start()
+        vec_recv[ms] = vec_send[ms]
+
+    def vo_wait():
+        for c in vo_copies:
+            c.wait_recv()
+        vec_line[mq] = jnp.sum(vec_recv[...], axis=0)
+
+    def vz_start():
+        for c in vz_copies:
+            c.start()
+
+    def vz_wait():
+        for c in vz_copies:
+            c.wait_recv()
+        vec_out_ref[...] = jnp.sum(vec_line[...], axis=0)
+
+    vsum[...] = jnp.zeros_like(vsum)
+    cot_in.wait()
+    gather_own_first(QKV)
+    order_rows()
+    gather_own_second(QKV)
+    gather_own_first(OUT)
+    gather_forward(QKV)
+    vec_start()
+    gather_own_second(OUT)
+    gather_core(QKV)
+    gather_forward(OUT)
+    gather_own_first(UP)
+    xz_start()
+    gather_last(QKV)
+    xz_wait()
+    xs_start()
+    gather_last(OUT)
+    gather_done(QKV)
+    vec_wait()
+    gather_core(OUT)
+    project(0)
+    gather_own_second(UP)
+    gather_forward(UP)
+    gather_done(OUT)
+    gather_own_first(DOWN)
+    project(1)
+    gather_own_second(DOWN)
+    project(2)
+    xs_wait()
+    span_means()
+    attend(0)
+    gather_core(UP)
+    attend(1)
+    gather_last(UP)
+    second_norm()
+    gather_done(UP)
+    feed_up(0, 0)
+    gather_forward(DOWN)
+    feed_up(0, 1)
+    down_grad(0)
+    reduce_a(D0)
+    gather_core(DOWN)
+    feed_up(1, 0)
+    feed_up(1, 1)
+    gather_last(DOWN)
+    reduce_b(D0)
+    down_grad(1)
+    gather_done(DOWN)
+    reduce_a(D1)
+    back_down(0, 0)
+    back_down(0, 1)
+    up_grad(0)
+    reduce_c(D0)
+    back_down(1, 0)
+    back_down(1, 1)
+    up_grad(1)
+    reduce_a(U1)
+    reduce_a(U0)
+    reduce_b(D1)
+    back_second(0)
+    reduce_d(D0)
+    reduce_b(U1)
+    reduce_c(D1)
+    reduce_b(U0)
+    back_second(1)
+    out_grad()
+    reduce_c(U1)
+    reduce_a(GO)
+    attend_back(0)
+    reduce_e(D0)
+    attend_back(1)
+    reduce_d(D1)
+    reduce_b(GO)
+    first_grad(0, 2 * lanes, g_two.at[0])
+    reduce_a(QA)
+    reduce_c(U0)
+    attend_back(2)
+    reduce_d(U1)
+    reduce_b(QA)
+    reduce_c(GO)
+    attend_back(3)
+    reduce_e(D1)
+    mean_grad()
+    gs_start()
+    reduce_d(U0)
+    reduce_f(D0)
+    first_grad(2 * lanes, lanes, g_one.at[0])
+    reduce_a(Q2)
+    reduce_e(U1)
+    reduce_c(QA)
+    first_grad(3 * lanes, lanes, g_one.at[1])
+    reduce_d(GO)
+    reduce_a(Q3)
+    reduce_b(Q2)
+    gs_wait()
+    reduce_f(D1)
+    gz_start()
+    reduce_b(Q3)
+    reduce_e(U0)
+    reduce_d(QA)
+    reduce_f(U1)
+    reduce_c(Q2)
+    reduce_e(GO)
+    reduce_c(Q3)
+    gz_wait()
+    back_first(0)
+    reduce_e(QA)
+    reduce_f(U0)
+    reduce_g(D1)
+    reduce_d(Q2)
+    reduce_d(Q3)
+    back_first(1)
+    reduce_g(D0)
+    reduce_g(U1)
+    reduce_f(GO)
+    reduce_e(Q2)
+    vec_build()
+    vo_start()
+    reduce_e(Q3)
+    reduce_f(QA)
+    vo_wait()
+    reduce_f(Q2)
+    reduce_g(GO)
+    vz_start()
     reduce_f(Q3)
-    reduce_g(U1)
+    out_block(0)
     reduce_g(QA)
-    for c in vz_copies:
-        c.wait_recv()
-    vec_out_ref[...] = jnp.sum(vec_line[...], axis=0)
+    reduce_g(U0)
+    out_block(1)
     reduce_g(Q2)
+    vz_wait()
     reduce_g(Q3)
 
     for target in range(1, shard_count):
@@ -999,6 +1079,8 @@
     for which in range(4):
         for c in w_copies[which]:
             c.wait_send()
+    for which in range(CHUNKS):
+        emit(which, chunk(which)[5]).wait()
     bout_out.wait()
     tok_out.wait()
 

time: 98.5 us -> 94 us (0.954)
  Pallas kernels: 97.4 us -> 92.9 us
    pallas_call x1, Pallas kernels: 92.2 us -> 87.7 us  [local_block(): pl.pallas_call(functools.partial(block_kernel, batch, shard_count, seq_co...]
where the time goes in v4:
time: 94 us; the launch traced here: 93.7 us
  Pallas kernels  92.9 us (99%)
    pallas_call x1, Pallas kernels, local_block(): pl.pallas_call(functools.partial(block_kernel, batch, shard_count, seq_co...  87.7 us
    pallas_call x1, Pallas kernels, local_block(): pl.pallas_call(finish_kernel, out_shape=(jax.ShapeDtypeStruct((rows, widt...  5.23 us

profile of v4, /device:TPU:0, one launch (start us, length us, event | category | flops | bytes accessed | tf_op | source)
XLA Modules:
  0.0 93.7 jit_solution(7980454512507910595)
XLA Ops:
  0.6 87.7 %block.1 = (bf16[1024,512]{1,0:T(8,128)(2,1)}, f32[1024,512]{1,0:T(8,128)}, bf16[64,768]{1,0:T(8,128)(2,1)}, bf16[2,64,384]{2,1,0:T(8,128)(2,1)}, bf16[64,512]{1...) custom-call(bf16[1024,512]{1,0:T(8,128)(2,1)} %bitcast.18, ...), custom_call_target="tpu_custom_call" | custom-call | tf_op jit(solution)/shard_map/block/pallas_call | solution.py:1266
  88.3 5.2 %finish.1 = (bf16[1024,512]{1,0:T(8,128)(2,1)}, f32[1024,512]{1,0:T(8,128)}, f32[64,1536]{1,0:T(8,128)}, f32[64,512]{1,0:T(8,128)}, f32[64,2048]{1,0:T(8,128)}, ...) custom-call(bf16[1024,512]{1,0:T(8,128)(2,1)} %get-tuple-element.34., ...), custom_call_target="tpu_custom_call" | custom-call | tf_op jit(solution)/shard_map/finish/pallas_call | solution.py:1308

commit v5 on v4

--- a/solution.py
+++ b/solution.py
@@ -58,8 +58,8 @@
     seq_count,
     tok_hbm,
     cot_hbm,
-    vec_refs,
-    up_bias_ref,
+    vec_hbm,
+    up_bias_hbm,
     wq_hbm,
     wo_hbm,
     wu_hbm,
@@ -71,7 +71,10 @@
     go_hbm,
     gu_hbm,
     gd_hbm,
-    vec_out_ref,
+    vec_out_hbm,
+    vec_refs,
+    up_bias_ref,
+    vec_total,
     tok,
     cot,
     wq,
@@ -147,6 +150,7 @@
     w_recv,
     w_local,
     io_sem,
+    small_sem,
     vec_s,
     vec_r,
     xz_s,
@@ -188,7 +192,15 @@
 
     tok_in = pltpu.make_async_copy(tok_hbm, tok, io_sem.at[0])
     cot_in = pltpu.make_async_copy(cot_hbm, cot, io_sem.at[1])
+    vec_in = [
+        pltpu.make_async_copy(source, target, small_sem.at[n])
+        for n, (source, target) in enumerate(
+            zip([*vec_hbm, up_bias_hbm], [*vec_refs, up_bias_ref])
+        )
+    ]
     tok_in.start()
+    for c in vec_in:
+        c.start()
     cot_in.start()
 
     xb_all[...] = jnp.zeros_like(xb_all)
@@ -340,10 +352,31 @@
     ).astype(BF)
 
     shard_rows = width // shard_count
+    for c in vec_in:
+        c.wait()
     for at, ref in enumerate(vec_refs):
         vec_own[at : at + 1, 0:shard_rows] = ref[...].astype(F32)
     vec_own[8 : 8 + up_bias_ref.shape[0], :] = up_bias_ref[...].astype(F32)
 
+    mean_rows = total * groups
+
+    def order_rows():
+        new_row = lax.broadcasted_iota(jnp.int32, (mean_rows, mean_rows), 0)
+        old_row = lax.broadcasted_iota(jnp.int32, (mean_rows, mean_rows), 1)
+
+        def scaled(value, down_by, up_by):
+            quotient = lax.shift_right_logical(value, down_by.bit_length() - 1)
+            return lax.shift_left(quotient, up_by.bit_length() - 1)
+
+        wanted = (
+            scaled(new_row & (spans_all - 1), spans_here, groups)
+            + scaled(new_row, spans_all, spans_here)
+            + (new_row & (spans_here - 1))
+        )
+        order[...] = (old_row == wanted).astype(BF)
+
+    order_rows()
+    vsum[...] = jnp.zeros_like(vsum)
     pl.semaphore_wait(barrier, len(peers))
 
     def remote(source, target, send, recv, device):
@@ -373,7 +406,6 @@
             xb_group(owner), xb_group(owner), xs_s.at[target], xs_r.at[owner], (target, mq)
         )
 
-    mean_rows = total * groups
     up_here = ff // shard_count
     parts = up_here // lanes
     part_cols = shard_count * lanes
@@ -390,21 +422,6 @@
     def xz_wait():
         for c in xz_copies:
             c.wait_recv()
-
-    def order_rows():
-        new_row = lax.broadcasted_iota(jnp.int32, (mean_rows, mean_rows), 0)
-        old_row = lax.broadcasted_iota(jnp.int32, (mean_rows, mean_rows), 1)
-
-        def scaled(value, down_by, up_by):
-            quotient = lax.shift_right_logical(value, down_by.bit_length() - 1)
-            return lax.shift_left(quotient, up_by.bit_length() - 1)
-
-        wanted = (
-            scaled(new_row & (spans_all - 1), spans_here, groups)
-            + scaled(new_row, spans_all, spans_here)
-            + (new_row & (spans_here - 1))
-        )
-        order[...] = (old_row == wanted).astype(BF)
 
     def xs_start():
         for target in range(1, shard_count):
@@ -567,6 +584,14 @@
         grad = dot(cot[...], down_tile(part, side), 1, 1)
         gbefore[:, cols] = (grad * gbefore[:, cols].astype(F32)).astype(BF)
 
+    def feed_both(part, side):
+        cols = columns_of(part, side)
+        before = dot(second[...], up_tile(part, side), 1, 0) + up_bias[0:1, cols]
+        grad = dot(cot[...], down_tile(part, side), 1, 1)
+        value, slope = gelu_parts(before)
+        hidden[:, cols] = value.astype(BF)
+        gbefore[:, cols] = (grad * slope).astype(BF)
+
     def chunk(which):
         if which in (D0, D1):
             refs, n = (g_down, r1_down, r2_down, r3_down, r4_down, own_down), which - D0
@@ -615,19 +640,8 @@
     edge = jnp.logical_or(mq == 0, mq == seq_count - 1)
     inner = jnp.logical_not(edge)
 
-    def add_rows(target, *sources):
-        count = target.shape[0]
-        step = min(count, 32)
-
-        def one(i, carry):
-            at = rows_of(i, step)
-            value = target[at, :]
-            for source in sources:
-                value = value + source[at, :]
-            target[at, :] = value
-            return carry
-
-        lax.fori_loop(0, count // step, one, 0)
+    def add_rows(target, source):
+        target[...] += source[...]
 
     def reduce_a(which):
         r_copies[which][0].start()
@@ -658,19 +672,8 @@
         c = r_copies[which]
         c[3].wait_recv()
         c[4].wait_recv()
-        count = own.shape[0]
-
-        def one(i, carry):
-            at = rows_of(i, 32)
-            value = (
-                g[core, here, at, :].astype(F32)
-                + r3[0, at, :].astype(F32)
-                + r3[1, at, :].astype(F32)
-            )
-            own[at, :] = value.astype(BF)
-            return carry
-
-        lax.fori_loop(0, count // 32, one, 0)
+        value = g[core, here].astype(F32) + r3[0].astype(F32) + r3[1].astype(F32)
+        own[...] = value.astype(BF)
 
         @pl.when(edge)
         def _():
@@ -924,141 +927,142 @@
         for c in vz_copies:
             c.start()
 
+    vec_out = pltpu.make_async_copy(vec_total, vec_out_hbm, io_sem.at[4])
+
     def vz_wait():
         for c in vz_copies:
             c.wait_recv()
-        vec_out_ref[...] = jnp.sum(vec_line[...], axis=0)
-
-    vsum[...] = jnp.zeros_like(vsum)
+        vec_total[...] = jnp.sum(vec_line[...], axis=0)
+        vec_out.start()
+
     cot_in.wait()
     gather_own_first(QKV)
-    order_rows()
+    xz_start()
+    gather_own_first(OUT)
     gather_own_second(QKV)
-    gather_own_first(OUT)
     gather_forward(QKV)
-    vec_start()
-    gather_own_second(OUT)
-    gather_core(QKV)
-    gather_forward(OUT)
-    gather_own_first(UP)
-    xz_start()
-    gather_last(QKV)
     xz_wait()
     xs_start()
+    vec_start()
+    gather_core(QKV)
+    gather_own_second(OUT)
+    gather_own_first(UP)
+    gather_last(QKV)
+    gather_own_second(UP)
+    vec_wait()
+    gather_done(QKV)
+    gather_forward(OUT)
+    xs_wait()
+    project(0)
+    project(1)
+    gather_core(OUT)
+    project(2)
+    span_means()
+    gather_forward(UP)
+    gather_own_first(DOWN)
+    attend(0)
+    gather_own_second(DOWN)
     gather_last(OUT)
-    gather_done(QKV)
-    vec_wait()
-    gather_core(OUT)
-    project(0)
-    gather_own_second(UP)
-    gather_forward(UP)
-    gather_done(OUT)
-    gather_own_first(DOWN)
-    project(1)
-    gather_own_second(DOWN)
-    project(2)
-    xs_wait()
-    span_means()
-    attend(0)
     gather_core(UP)
     attend(1)
+    gather_done(OUT)
     gather_last(UP)
     second_norm()
     gather_done(UP)
     feed_up(0, 0)
     gather_forward(DOWN)
+    feed_up(1, 1)
     feed_up(0, 1)
+    gather_core(DOWN)
     down_grad(0)
     reduce_a(D0)
-    gather_core(DOWN)
     feed_up(1, 0)
-    feed_up(1, 1)
     gather_last(DOWN)
+    down_grad(1)
     reduce_b(D0)
-    down_grad(1)
     gather_done(DOWN)
     reduce_a(D1)
-    back_down(0, 0)
-    back_down(0, 1)
-    up_grad(0)
-    reduce_c(D0)
     back_down(1, 0)
     back_down(1, 1)
     up_grad(1)
+    reduce_b(D1)
+    reduce_c(D0)
+    back_down(0, 1)
     reduce_a(U1)
+    back_down(0, 0)
+    up_grad(0)
     reduce_a(U0)
-    reduce_b(D1)
+    reduce_c(D1)
     back_second(0)
+    reduce_b(U1)
     reduce_d(D0)
-    reduce_b(U1)
-    reduce_c(D1)
     reduce_b(U0)
     back_second(1)
     out_grad()
+    reduce_a(GO)
     reduce_c(U1)
-    reduce_a(GO)
     attend_back(0)
-    reduce_e(D0)
-    attend_back(1)
     reduce_d(D1)
     reduce_b(GO)
+    reduce_c(U0)
+    attend_back(1)
     first_grad(0, 2 * lanes, g_two.at[0])
     reduce_a(QA)
-    reduce_c(U0)
     attend_back(2)
+    reduce_e(D0)
+    reduce_c(GO)
     reduce_d(U1)
+    attend_back(3)
     reduce_b(QA)
-    reduce_c(GO)
-    attend_back(3)
     reduce_e(D1)
     mean_grad()
     gs_start()
+    reduce_d(GO)
     reduce_d(U0)
-    reduce_f(D0)
     first_grad(2 * lanes, lanes, g_one.at[0])
+    reduce_c(QA)
     reduce_a(Q2)
     reduce_e(U1)
-    reduce_c(QA)
+    reduce_f(D0)
     first_grad(3 * lanes, lanes, g_one.at[1])
-    reduce_d(GO)
     reduce_a(Q3)
     reduce_b(Q2)
+    reduce_f(D1)
     gs_wait()
-    reduce_f(D1)
     gz_start()
+    reduce_e(GO)
     reduce_b(Q3)
     reduce_e(U0)
     reduce_d(QA)
+    reduce_c(Q2)
     reduce_f(U1)
-    reduce_c(Q2)
-    reduce_e(GO)
     reduce_c(Q3)
     gz_wait()
     back_first(0)
+    reduce_f(GO)
     reduce_e(QA)
-    reduce_f(U0)
-    reduce_g(D1)
     reduce_d(Q2)
     reduce_d(Q3)
+    reduce_f(U0)
     back_first(1)
-    reduce_g(D0)
-    reduce_g(U1)
-    reduce_f(GO)
     reduce_e(Q2)
     vec_build()
+    reduce_g(U1)
     vo_start()
     reduce_e(Q3)
     reduce_f(QA)
+    out_block(0)
+    reduce_f(Q2)
+    reduce_g(D1)
     vo_wait()
-    reduce_f(Q2)
     reduce_g(GO)
+    reduce_g(D0)
+    reduce_g(U0)
     vz_start()
     reduce_f(Q3)
-    out_block(0)
-    reduce_g(QA)
-    reduce_g(U0)
     out_block(1)
     reduce_g(Q2)
+    reduce_g(QA)
     vz_wait()
     reduce_g(Q3)
 
@@ -1083,19 +1087,28 @@
         emit(which, chunk(which)[5]).wait()
     bout_out.wait()
     tok_out.wait()
+    vec_out.wait()
 
 
 def finish_kernel(*refs):
-    raw, vec, outs, vec_outs = refs[0:7], refs[7], refs[8:14], refs[14:21]
-    low_refs, high_refs, in_sem, out_sem = refs[21:28], refs[28:32], refs[32], refs[33]
+    raw, outs, vec_outs = refs[0:8], refs[8:14], refs[14:21]
+    low_refs, high_refs, vec, small = refs[21:28], refs[28:32], refs[32], refs[33:40]
+    in_sem, out_sem = refs[40:42]
     order = (5, 6, 4, 0, 1, 2, 3)
     loads = [pltpu.make_async_copy(raw[n], low_refs[n], in_sem.at[n]) for n in range(7)]
+    vec_load = pltpu.make_async_copy(raw[7], vec, in_sem.at[7])
+    vec_load.start()
     for n in order:
         loads[n].start()
-    for n, ref in enumerate(vec_outs[0:6]):
-        ref[...] = vec[n : n + 1, 0 : ref.shape[1]]
-    vec_outs[6][...] = vec[8 : 8 + vec_outs[6].shape[0], :]
+    vec_load.wait()
     stores = []
+    for n in range(7):
+        if n < 6:
+            small[n][...] = vec[n : n + 1, 0 : small[n].shape[1]]
+        else:
+            small[n][...] = vec[8 : 8 + small[n].shape[0], :]
+        stores.append(pltpu.make_async_copy(small[n], vec_outs[n], out_sem.at[6 + n]))
+        stores[n].start()
     lanes = 2 * HD
 
     def store(ready, at):
@@ -1166,7 +1179,6 @@
     lanes = 2 * HD
     shard_rows = width // shard_count
     down_rows = ff // shard_count
-    vmem = pl.BlockSpec(memory_space=pltpu.VMEM)
     hbm = pl.BlockSpec(memory_space=pl.ANY)
     dma = pltpu.SemaphoreType.DMA
     half_yx = shard_count // 2
@@ -1195,6 +1207,9 @@
         for buf in five
     ]
     scratch = [
+        [pltpu.VMEM((1, shard_rows), BF)] * 6,
+        pltpu.VMEM((down_rows // lanes, lanes), BF),
+        pltpu.VMEM((16, lanes), F32),
         pltpu.VMEM((rows, width), BF),
         pltpu.VMEM((rows, width), BF),
         pltpu.VMEM((width, 3 * width), BF),
@@ -1240,7 +1255,8 @@
         dma((4 * GATHER_STEPS,)),
         dma((4 * GATHER_STEPS,)),
         dma((4,)),
-        dma((4,)),
+        dma((5,)),
+        dma((7,)),
         dma((shard_count,)),
         dma((shard_count,)),
         dma((seq_count,)),
@@ -1275,8 +1291,8 @@
             jax.ShapeDtypeStruct((down_rows, width), BF),
             jax.ShapeDtypeStruct((16, lanes), F32),
         ),
-        in_specs=[hbm, hbm, [vmem] * 6, vmem, hbm, hbm, hbm, hbm],
-        out_specs=(hbm,) * 7 + (vmem,),
+        in_specs=[hbm, hbm, [hbm] * 6, hbm, hbm, hbm, hbm, hbm],
+        out_specs=(hbm,) * 8,
         scratch_shapes=scratch,
         compiler_params=pltpu.CompilerParams(
             collective_id=0, has_side_effects=True, vmem_limit_bytes=63 * 2**20
@@ -1314,15 +1330,18 @@
             *(jax.ShapeDtypeStruct((1, shard_rows), F32) for _ in range(6)),
             jax.ShapeDtypeStruct((down_rows // lanes, lanes), F32),
         ),
-        in_specs=[hbm] * 7 + [vmem],
-        out_specs=(hbm,) * 6 + (vmem,) * 7,
+        in_specs=[hbm] * 8,
+        out_specs=(hbm,) * 13,
         scratch_shapes=[
             pltpu.VMEM((rows, width), BF),
             pltpu.VMEM((rows, width), F32),
             *(pltpu.VMEM(shape, BF) for shape in low_shapes),
             *(pltpu.VMEM(shape, F32) for shape in high_shapes),
-            dma((7,)),
-            dma((6,)),
+            pltpu.VMEM((16, lanes), F32),
+            *(pltpu.VMEM((1, shard_rows), F32) for _ in range(6)),
+            pltpu.VMEM((down_rows // lanes, lanes), F32),
+            dma((8,)),
+            dma((13,)),
         ],
         compiler_params=pltpu.CompilerParams(vmem_limit_bytes=62 * 2**20),
         name="finish",

time: 94 us -> 91.3 us (0.971)
  Pallas kernels: 92.9 us -> 90.2 us
    pallas_call x1, Pallas kernels: 87.7 us -> 86.2 us  [local_block(): pl.pallas_call(functools.partial(block_kernel, batch, shard_count, seq_co...]
    pallas_call x1, Pallas kernels: 5.23 us -> 4.04 us  [local_block(): pl.pallas_call(finish_kernel, out_shape=(jax.ShapeDtypeStruct((rows, widt...]
where the time goes in v5:
time: 91.3 us; the launch traced here: 91.1 us
  Pallas kernels  90.2 us (99%)
    pallas_call x1, Pallas kernels, local_block(): pl.pallas_call(functools.partial(block_kernel, batch, shard_count, seq_co...  86.2 us
    pallas_call x1, Pallas kernels, local_block(): pl.pallas_call(finish_kernel, out_shape=(jax.ShapeDtypeStruct((rows, widt...  4.04 us

profile of v5, /device:TPU:0, one launch (start us, length us, event | category | flops | bytes accessed | tf_op | source)
XLA Modules:
  0.0 91.1 jit_solution(14874632115054920727)
XLA Ops:
  0.6 86.2 %block.1 = (bf16[1024,512]{1,0:T(8,128)(2,1)}, f32[1024,512]{1,0:T(8,128)}, bf16[64,768]{1,0:T(8,128)(2,1)}, bf16[2,64,384]{2,1,0:T(8,128)(2,1)}, bf16[64,512]{1...) custom-call(bf16[1024,512]{1,0:T(8,128)(2,1)} %bitcast.18, ...), custom_call_target="tpu_custom_call" | custom-call | tf_op jit(solution)/shard_map/block/pallas_call | solution.py:1282
  86.8 4.0 %finish.1 = (bf16[1024,512]{1,0:T(8,128)(2,1)}, f32[1024,512]{1,0:T(8,128)}, f32[64,1536]{1,0:T(8,128)}, f32[64,512]{1,0:T(8,128)}, f32[64,2048]{1,0:T(8,128)}, ...) custom-call(bf16[1024,512]{1,0:T(8,128)(2,1)} %get-tuple-element.34., ...), custom_call_target="tpu_custom_call" | custom-call | tf_op jit(solution)/shard_map/finish/pallas_call | solution.py:1324

commit v6 on v5

--- a/solution.py
+++ b/solution.py
@@ -860,7 +860,15 @@
             c.wait_recv()
         gnbar[...] = jnp.sum(gz_recv[...].astype(F32), axis=0)
 
-    bout_out = pltpu.make_async_copy(gbranch, block_out_hbm, io_sem.at[2])
+    def halves(source, target, first_sem):
+        return [
+            pltpu.make_async_copy(
+                source.at[rows_of(i, big)], target.at[rows_of(i, big)], io_sem.at[first_sem + i]
+            )
+            for i in range(2)
+        ]
+
+    bout_out = halves(gbranch, block_out_hbm, 5)
 
     def out_block(i):
         at = rows_of(i, big)
@@ -868,10 +876,9 @@
         gbranch[at, :] = (
             middle[at, :] + dot(hidden[at, :], down_perm, 1, 0) + vector(5)
         ).astype(BF)
-        if i == 1:
-            bout_out.start()
-
-    tok_out = pltpu.make_async_copy(gmid, grad_tok_hbm, io_sem.at[3])
+        bout_out[i].start()
+
+    tok_out = halves(gmid, grad_tok_hbm, 7)
 
     def back_first(i):
         at = rows_of(i, big)
@@ -889,8 +896,7 @@
         vsum[0:1, :] += jnp.sum(grad * xhat, axis=0, keepdims=True)
         vsum[1:2, :] += jnp.sum(grad, axis=0, keepdims=True)
         gmid[at, :] = gmid[at, :] + norm_back(grad, xhat, inv1[at, :], vector(0))
-        if i == 1:
-            tok_out.start()
+        tok_out[i].start()
 
     def vec_build():
         for owner in range(shard_count):
@@ -1085,8 +1091,8 @@
             c.wait_send()
     for which in range(CHUNKS):
         emit(which, chunk(which)[5]).wait()
-    bout_out.wait()
-    tok_out.wait()
+    for c in bout_out + tok_out:
+        c.wait()
     vec_out.wait()
 
 
@@ -1094,12 +1100,33 @@
     raw, outs, vec_outs = refs[0:8], refs[8:14], refs[14:21]
     low_refs, high_refs, vec, small = refs[21:28], refs[28:32], refs[32], refs[33:40]
     in_sem, out_sem = refs[40:42]
-    order = (5, 6, 4, 0, 1, 2, 3)
-    loads = [pltpu.make_async_copy(raw[n], low_refs[n], in_sem.at[n]) for n in range(7)]
+    order = (1, 0, 5, 6, 4, 2, 3)
+    loads = {
+        n: pltpu.make_async_copy(raw[n], low_refs[n], in_sem.at[n]) for n in range(2, 7)
+    }
+    pieces = 4
+
+    def piece_copies(n):
+        count = low_refs[n].shape[0] // pieces
+        spans = [pl.ds(k * count, count) for k in range(pieces)]
+        return [
+            (
+                pltpu.make_async_copy(
+                    raw[n].at[at], low_refs[n].at[at], in_sem.at[8 + n * pieces + k]
+                ),
+                pltpu.make_async_copy(
+                    low_refs[n].at[at], outs[n].at[at], out_sem.at[13 + n * pieces + k]
+                ),
+            )
+            for k, at in enumerate(spans)
+        ]
+
+    large = [piece_copies(n) for n in range(2)]
     vec_load = pltpu.make_async_copy(raw[7], vec, in_sem.at[7])
     vec_load.start()
     for n in order:
-        loads[n].start()
+        for c in [load for load, _ in large[n]] if n < 2 else [loads[n]]:
+            c.start()
     vec_load.wait()
     stores = []
     for n in range(7):
@@ -1116,11 +1143,15 @@
         stores[-1].start()
 
     for n in order:
+        if n < 2:
+            for load, piece_store in large[n]:
+                load.wait()
+                piece_store.start()
+                stores.append(piece_store)
+            continue
         loads[n].wait()
         low = low_refs[n]
-        if n < 2:
-            store(low, n)
-        elif n == 2:
+        if n == 2:
             for part in range(3):
                 start = part * 4 * lanes
                 high_refs[0][:, start : start + 2 * lanes] = low[
@@ -1255,7 +1286,7 @@
         dma((4 * GATHER_STEPS,)),
         dma((4 * GATHER_STEPS,)),
         dma((4,)),
-        dma((5,)),
+        dma((9,)),
         dma((7,)),
         dma((shard_count,)),
         dma((shard_count,)),
@@ -1340,8 +1371,8 @@
             pltpu.VMEM((16, lanes), F32),
             *(pltpu.VMEM((1, shard_rows), F32) for _ in range(6)),
             pltpu.VMEM((down_rows // lanes, lanes), F32),
-            dma((8,)),
-            dma((13,)),
+            dma((16,)),
+            dma((21,)),
         ],
         compiler_params=pltpu.CompilerParams(vmem_limit_bytes=62 * 2**20),
         name="finish",

time: 91.3 us -> 90.8 us (level)
  no operation moved by 1% of the time
where the time goes in v6:
time: 90.8 us; the launch traced here: 90.6 us
  Pallas kernels  89.8 us (99%)
    pallas_call x1, Pallas kernels, local_block(): pl.pallas_call(functools.partial(block_kernel, batch, shard_count, seq_co...  86.2 us
    pallas_call x1, Pallas kernels, local_block(): pl.pallas_call(finish_kernel, out_shape=(jax.ShapeDtypeStruct((rows, widt...  3.56 us

profile of v6, /device:TPU:0, one launch (start us, length us, event | category | flops | bytes accessed | tf_op | source)
XLA Modules:
  0.0 90.6 jit_solution(17588669315156684934)
XLA Ops:
  0.6 86.2 %block.1 = (bf16[1024,512]{1,0:T(8,128)(2,1)}, f32[1024,512]{1,0:T(8,128)}, bf16[64,768]{1,0:T(8,128)(2,1)}, bf16[2,64,384]{2,1,0:T(8,128)(2,1)}, bf16[64,512]{1...) custom-call(bf16[1024,512]{1,0:T(8,128)(2,1)} %bitcast.18, ...), custom_call_target="tpu_custom_call" | custom-call | tf_op jit(solution)/shard_map/block/pallas_call | solution.py:1313
  86.9 3.6 %finish.1 = (bf16[1024,512]{1,0:T(8,128)(2,1)}, f32[1024,512]{1,0:T(8,128)}, f32[64,1536]{1,0:T(8,128)}, f32[64,512]{1,0:T(8,128)}, f32[64,2048]{1,0:T(8,128)}, ...) custom-call(bf16[1024,512]{1,0:T(8,128)(2,1)} %get-tuple-element.34., ...), custom_call_target="tpu_custom_call" | custom-call | tf_op jit(solution)/shard_map/finish/pallas_call | solution.py:1355
